TPU v7x, 32 devices: a whole 2x2x4 slice. The times are simulated.
32 devices in a mesh: dp: 2 (over y), seq: 16 (over z, x, core).
Axes of the slice: x: 2, y: 2, z: 4, core: 2. Of those that a mesh axis runs over, the one named last changes fastest.
Arguments:
- mel_frames: bfloat16 [2, 4096, 128], P('dp', 'seq'), may hold values from -6 to 6
- positions: int32 [2, 2048], P('dp', 'seq'), may hold values from 0 to 4095, as said below
- conv_weight: bfloat16 [128, 3, 1280], replicated, may hold values from -0.3125 to 0.3125
- conv_bias: float32 [1280], replicated, may hold values from -3 to 3
- proj_weight: bfloat16 [1280, 2048], P('dp'), may hold values from -0.15625 to 0.15625
- proj_bias: float32 [2048], replicated, may hold values from -3 to 3
- cotangent: bfloat16 [2, 4096, 2048], P('dp', 'seq'), may hold values from -0.13183594 to 0.13183594
Outputs:
- merged: bfloat16 [2, 4096, 2048], P('dp', 'seq')
- grad_weight: float32 [128, 3, 1280], P('seq', None, 'dp')
Inputs may be any that keep to these rules, and one draw needn't show every extreme that they name: Within a recording the 2048 entries are distinct. Block b of the sequence is positions b * 256 to b * 256 + 255; the 128 tokens of one window put at most 16 entries into any one block, and in each recording one block receives exactly 16 from every window.
All inputs are finite; a program needn't handle non-finite values.
Results may differ from a plain program's by a relative error of at most 0.012.
Values may be sent and summed in bfloat16 or wider, within the bound.
No kernel may reach another device: no remote copies, remote signals or barrier semaphores. Data moves between devices by JAX's collectives and lax.ppermute only.
A program may use at most 64 MiB of HBM per device.

v0:
```python
import jax
import jax.numpy as jnp
from jax import lax
from jax.sharding import PartitionSpec as P

SQRT_HALF = 0.7071067811865476
INV_SQRT_TWO_PI = 0.3989422804014327


def gelu_value(x):
    return x * 0.5 * (1.0 + lax.erf(x * SQRT_HALF))


def gelu_slope(x):
    return 0.5 * (1.0 + lax.erf(x * SQRT_HALF)) + x * INV_SQRT_TWO_PI * jnp.exp(-0.5 * x * x)


def body(mel_frames, positions, conv_weight, conv_bias, proj_weight, proj_bias, cotangent):
    frames = mel_frames[0]
    local_spots = positions[0]
    grads_in = cotangent[0]
    owner_count = lax.axis_size("seq")
    frame_count = frames.shape[0]
    tok_count = frame_count // 2
    rows_own = grads_in.shape[0]
    capacity = rows_own // owner_count
    tap_count = conv_weight.shape[1]
    channels = conv_weight.shape[2]
    padded = jnp.pad(frames, ((1, 1), (0, 0)))
    stacked = jnp.concatenate([padded[k : k + frame_count] for k in range(tap_count)], axis=1)
    kernel = jnp.transpose(conv_weight, (1, 0, 2)).reshape(-1, channels)
    pre_act = jnp.dot(stacked, kernel, preferred_element_type=jnp.float32) + conv_bias
    act_pairs = gelu_value(pre_act).reshape(tok_count, 2, channels)
    pooled = (0.5 * (act_pairs[:, 0, :] + act_pairs[:, 1, :])).astype(jnp.bfloat16)
    full_weight = lax.all_gather(proj_weight, "dp", axis=0, tiled=True)
    owner_index = local_spots // rows_own
    owner_row = local_spots % rows_own
    onehot = (owner_index[:, None] == jnp.arange(owner_count, dtype=jnp.int32)[None, :]).astype(
        jnp.int32
    )
    rank_before = jnp.cumsum(onehot, axis=0) - onehot
    slot_rank = jnp.sum(rank_before * onehot, axis=1)
    slot_index = owner_index * capacity + slot_rank
    dest_rows = (
        jnp.full((owner_count * capacity,), rows_own, jnp.int32).at[slot_index].set(owner_row)
    )
    dest_rows = dest_rows.reshape(owner_count, capacity)
    contract_last = (((1,), (1,)), ((), ()))
    projected = (
        jnp.dot(pooled, full_weight, preferred_element_type=jnp.float32) + proj_bias
    ).astype(jnp.bfloat16)
    outgoing = (
        jnp.zeros((owner_count * capacity, projected.shape[1]), jnp.bfloat16)
        .at[slot_index]
        .set(projected)
    )
    outgoing = outgoing.reshape(owner_count, capacity, -1)
    arrived, arrived_rows = (
        lax.all_to_all(outgoing, "seq", split_axis=0, concat_axis=0, tiled=True),
        lax.all_to_all(dest_rows, "seq", split_axis=0, concat_axis=0, tiled=True),
    )
    flat_rows = arrived_rows.reshape(-1)
    merged = (
        jnp.zeros_like(grads_in)
        .at[flat_rows]
        .set(arrived.reshape(flat_rows.shape[0], -1), mode="drop")
    )
    picked = jnp.take(grads_in, flat_rows, axis=0, mode="clip").reshape(owner_count, capacity, -1)
    returned = lax.all_to_all(picked, "seq", split_axis=0, concat_axis=0, tiled=True)
    grad_tokens = returned.reshape(owner_count * capacity, -1)[slot_index]
    grad_pooled = lax.dot_general(
        grad_tokens, full_weight, contract_last, preferred_element_type=jnp.float32
    ).astype(jnp.bfloat16)
    slopes = gelu_slope(pre_act).reshape(tok_count, 2, channels)
    grad_pre = (0.5 * grad_pooled.astype(jnp.float32)[:, None, :] * slopes).astype(jnp.bfloat16)
    grad_pre = grad_pre.reshape(frame_count, channels)
    contract_first = (((0,), (0,)), ((), ()))
    tap_terms = [
        lax.dot_general(
            padded[k : k + frame_count],
            grad_pre,
            contract_first,
            preferred_element_type=jnp.float32,
        )
        for k in range(tap_count)
    ]
    seq_share = lax.psum_scatter(
        jnp.stack(tap_terms, axis=1), "seq", scatter_dimension=0, tiled=True
    )
    grad_weight = lax.psum_scatter(seq_share, "dp", scatter_dimension=2, tiled=True)
    return (merged[None], grad_weight)


def solution(mesh):
    in_specs = (
        P("dp", "seq", None),
        P("dp", "seq"),
        P(),
        P(),
        P("dp", None),
        P(),
        P("dp", "seq", None),
    )
    out_specs = (P("dp", "seq", None), P("seq", None, "dp"))
    return jax.shard_map(body, mesh=mesh, in_specs=in_specs, out_specs=out_specs, check_vma=False)
```

profile of v0, /device:TPU:0, one launch (start us, length us, event | category | flops | bytes accessed | tf_op | source)
XLA Modules:
  0.0 175.8 jit_solution(8942438320500561267)
XLA Ops:
  7.2 0.7 all-gather.2.cloned.1.call-update
  8.4 1.0 scatter_custom_fusion
  9.5 13.6 %all_to_all.19 = s32[16,1,16]{2,1,0:T(1,128)S(1)} all-to-all(s32[16,1,16]{2,1,0:T(1,128)S(1)} %all_to_all.12), channel_id=1, replica_groups=mesh['dp'=2,'seq'=16] {'seq'}, dimensions={0} | all-to-all | bytes 2048 | tf_op jit(solution)/shard_map/all_to_all | solution.py:60
  23.1 2.3 %gather_fusion = bf16[256,2048]{1,0:T(8,128)(2,1)} fusion(bf16[256,2048]{1,0:T(8,128)(2,1)S(1)} %bitcast.66, s32[1024]{0:T(1024)S(1)} %pad_clamp_fusion.1), kind=kCustom, calls=%fused_computation | custom fusion | bytes 2098176 | tf_op jit(solution)/shard_map/jit(_take)/gather | solution.py:68
  25.5 3.8 %all-to-all-start.2 = ((bf16[16,16,2048]{2,1,0:T(8,128)(2,1)}), bf16[16,16,2048]{2,1,0:T(8,128)(2,1)S(1)}, u32[]{:S(2)}, u32[]{:S(2)}) async-start(bf16[16,16,2048]{2,1,0:T(8,128)(2,1)} %bitcast.13), calls=%async_computation.2 | async-start | bytes 2097152 | tf_op jit(solution)/shard_map/all_to_all | solution.py:69
  29.4 22.8 %all-to-all-done.2 = bf16[16,16,2048]{2,1,0:T(8,128)(2,1)S(1)} async-done(((bf16[16,16,2048]{2,1,0:T(8,128)(2,1)}), bf16[16,16,2048]{2,1,0:T(8,128)(2,1)S(1)}, u32[]{:S(2)}, u32[]{:S(2)}) %all-to-all-start.2) | async-done | bytes 1048608 | tf_op jit(solution)/shard_map/all_to_all | solution.py:69
  52.2 0.9 gather_fusion.1
  53.1 27.8 %all-gather.2.cloned.1.call-done = bf16[1280,2048]{1,0:T(8,128)(2,1)} async-done(((bf16[640,2048]{1,0:T(8,128)(2,1)}), bf16[1280,2048]{1,0:T(8,128)(2,1)}) %all-gather.2.cloned.1.call-update) | async-done | bytes 5242896 | tf_op jit(solution)/shard_map/all_gather | solution.py:35
  80.9 4.3 %fusion.2 = f32[128,1280]{1,0:T(8,128)S(1)} fusion(bf16[128,2048]{1,0:T(8,128)(2,1)S(1)} %gather_fusion.1, bf16[1280,2048]{1,0:T(8,128)(2,1)} %all-gather.2.cloned.1.call-done), kind=kOutput, calls=%fused_computation.13 | convolution fusion | flops 671580160 | bytes 6422528 | tf_op jit(solution)/shard_map/dot_general | solution.py:71
  85.2 0.5 mul.82
  85.7 2.0 %mul.83 = f32[256,1280]{1,0:T(8,128)} reshape(f32[128,2,1280]{2,1,0:T(2,128)S(1)} %mul.82) | data formatting | bytes 2621440 | tf_op jit(solution)/shard_map/mul | solution.py:75
  87.7 3.3 %fusion.7 = (bf16[256,1280]{1,0:T(8,128)(2,1)S(1)}, f32[256,1280]{1,0:T(8,128)}) fusion(f32[256,1280]{1,0:T(8,128)} %mul.83, f32[1280]{0:T(1024)} %param.10, bf16[384,1280]{1,0:T(8,128)(2,1)S(1)} %bitcast.76, bf16[256,128]{1,0:T(8,128)(2,1)S(1)} %get-tuple-element.7, bf16[256,128]{1,0:T(8,128)(2,1)S(1)} %bitcast.71, bf16[256,128]{1,0:T(8,128)(2,1)S(1)} %get-tuple-element.6), kind=kOutput, calls=%fused_computation.20 | convolution fusion | flops 256507904 | bytes 4461568 | tf_op jit(solution)/shard_map/dot_general | solution.py:32
  91.2 0.3 convolution_bitcast_fusion.1
  91.8 1.5 pad_maximum_fusion
  93.3 2.1 %reshape.171 = f32[128,2,1280]{2,1,0:T(2,128)S(1)} reshape(f32[256,1280]{1,0:T(8,128)} %get-tuple-element.3) | data formatting | bytes 2621440 | tf_op jit(solution)/shard_map/reshape | solution.py:33
  95.4 1.0 fusion.29
  96.4 3.4 %fusion = bf16[128,2048]{1,0:T(8,128)(2,1)S(1)} fusion(bf16[1280,2048]{1,0:T(8,128)(2,1)} %all-gather.2.cloned.1.call-done, f32[2048]{0:T(1024)S(1)} %copy-done.2, f32[128,1,1280]{2,1,0:T(1,128)S(1)} %get-tuple-element.5, f32[128,1,1280]{2,1,0:T(1,128)S(1)} %get-tuple-element.4), kind=kOutput, calls=%fused_computation.10 | convolution fusion | flops 672104448 | bytes 7086080 | tf_op jit(solution)/shard_map/dot_general | solution.py:50
  99.8 2.4 %scatter_custom_fusion.1 = bf16[256,2048]{1,0:T(8,128)(2,1)} fusion(s32[128]{0:T(128)S(1)} %fusion.23, bf16[128,2048]{1,0:T(8,128)(2,1)S(1)} %fusion, bf16[]{:T(256)} %constant.25.clone.1), kind=kCustom, calls=%fused_computation.28 | custom fusion | bytes 1048578 | tf_op jit(solution)/shard_map/scatter | solution.py:55
  102.3 5.6 %all-to-all-start.1 = ((bf16[16,16,2048]{2,1,0:T(8,128)(2,1)}), bf16[16,16,2048]{2,1,0:T(8,128)(2,1)S(1)}, u32[]{:S(2)}, u32[]{:S(2)}) async-start(bf16[16,16,2048]{2,1,0:T(8,128)(2,1)} %bitcast.9), calls=%async_computation.1 | async-start | bytes 2097152 | tf_op jit(solution)/shard_map/all_to_all | solution.py:59
  107.9 49.3 %reduce-scatter.3.cloned.1.call-done = f32[8,3,1280]{2,0,1:T(8,128)} async-done(((f32[128,3,1280]{2,0,1:T(8,128)}), f32[8,3,1280]{2,0,1:T(8,128)}) %reduce-scatter.3.cloned.1.call-update) | async-done | bytes 122896 | tf_op jit(solution)/shard_map/reduce_scatter | solution.py:87
  157.3 0.5 broadcast.196
  157.8 0.7 reduce.5
  158.6 3.1 %scatter_custom_fusion.2 = bf16[256,2048]{1,0:T(8,128)(2,1)} fusion(s32[256]{0:T(256)S(1)} %bitcast.75, bf16[256,2048]{1,0:T(8,128)(2,1)S(1)} %bitcast.68, bf16[]{:T(256)} %constant.25.clone.1), kind=kCustom, calls=%fused_computation.26 | custom fusion | bytes 1048578 | tf_op jit(solution)/shard_map/scatter | solution.py:66
  161.7 7.5 %reduce-scatter.5.cloned.1.call-done = f32[8,3,640]{2,0,1:T(8,128)} async-done(((f32[8,3,1280]{2,0,1:T(8,128)}), f32[8,3,640]{2,0,1:T(8,128)}) %reduce-scatter.5.cloned.1.call-update) | async-done | bytes 61456 | tf_op jit(solution)/shard_map/reduce_scatter | solution.py:90
  (30 shorter events, 1.5 us)
Async XLA Ops:
  7.2 16.0 %copy-start = (bf16[1,256,2048]{2,1,0:T(8,128)(2,1)S(1)}, bf16[1,256,2048]{2,1,0:T(8,128)(2,1)}, u32[]{:S(2)}) copy-start(bf16[1,256,2048]{2,1,0:T(8,128)(2,1)} %param.13) | copy-start | bytes 3145732
  7.2 0.7 copy-start.4
  7.2 73.7 %all-gather.2.cloned.1.call-start = ((), (), s32[]{:S(2)}) async-start(), calls=%async_computation.5 | async-start | bytes 7864320 | tf_op jit(solution)/shard_map/all_gather | solution.py:35
  25.5 3.9 %copy-start.1 = (bf16[1,256,128]{2,1,0:T(8,128)(2,1)S(1)}, bf16[1,256,128]{2,1,0:T(8,128)(2,1)}, u32[]{:S(2)}) copy-start(bf16[1,256,128]{2,1,0:T(8,128)(2,1)} %param.7) | copy-start | bytes 196612
  25.5 26.7 %all-to-all-start.2 = ((bf16[16,16,2048]{2,1,0:T(8,128)(2,1)}), bf16[16,16,2048]{2,1,0:T(8,128)(2,1)S(1)}, u32[]{:S(2)}, u32[]{:S(2)}) async-start(bf16[16,16,2048]{2,1,0:T(8,128)(2,1)} %bitcast.13), calls=%async_computation.2 | async-start | bytes 2097152 | tf_op jit(solution)/shard_map/all_to_all | solution.py:69
  29.3 128.0 %reduce-scatter.3.cloned.1.call-start = ((), (), s32[]{:S(2)}) async-start(), calls=%async_computation.6 | async-start | bytes 2088960 | tf_op jit(solution)/shard_map/reduce_scatter | solution.py:87
  85.7 2.0 %copy-start.3 = (bf16[128,3,1280]{2,0,1:T(8,128)(2,1)S(1)}, bf16[128,3,1280]{2,0,1:T(8,128)(2,1)}, u32[]{:S(2)}) copy-start(bf16[128,3,1280]{2,0,1:T(8,128)(2,1)} %param.9) | copy-start | bytes 2949124
  95.4 1.0 copy-start.2
  102.3 56.3 %all-to-all-start.1 = ((bf16[16,16,2048]{2,1,0:T(8,128)(2,1)}), bf16[16,16,2048]{2,1,0:T(8,128)(2,1)S(1)}, u32[]{:S(2)}, u32[]{:S(2)}) async-start(bf16[16,16,2048]{2,1,0:T(8,128)(2,1)} %bitcast.9), calls=%async_computation.1 | async-start | bytes 2097152 | tf_op jit(solution)/shard_map/all_to_all | solution.py:59
  107.9 61.3 %reduce-scatter.5.cloned.1.call-start = ((), (), s32[]{:S(2)}) async-start(), calls=%async_computation.7 | async-start | bytes 184320 | tf_op jit(solution)/shard_map/reduce_scatter | solution.py:90
Sparse Core Ops, SparseCore 0:
  9.6 71.2 all-gather.1
  93.4 63.7 reduce-scatter.2
  160.0 9.1 reduce-scatter.4
where the time goes:
time: 176 us
  waiting for transfers between devices  108 us (61%)
  local copies, waits for them, and re-layouts  16.2 us (9%)
  between operations  14 us (8%)
  blocking collectives  13.6 us (8%)
  matrix products  11.9 us (7%)
  starting transfers between devices  9.5 us (5%)
  other arithmetic  2.59 us (1%)
    reduce_scatter x1, waiting for transfers between devices, body(): lax.psum_scatter(jnp.stack(tap_terms, axis=1), 'seq', scatter_dimension=0...  49.3 us
    all_gather x1, waiting for transfers between devices, body(): full_weight = lax.all_gather(proj_weight, 'dp', axis=0, tiled=True)  27.8 us
    all_to_all x1, waiting for transfers between devices, body(): lax.all_to_all(picked, 'seq', split_axis=0, concat_axis=0, tiled=True)  22.8 us
    all_to_all x1, blocking collectives, body(): lax.all_to_all(dest_rows, 'seq', split_axis=0, concat_axis=0, tiled=True)  13.6 us
    reduce_scatter x1, waiting for transfers between devices, body(): lax.psum_scatter(seq_share, 'dp', scatter_dimension=2, tiled=True)  7.53 us
    all_to_all x1, starting transfers between devices, body(): lax.all_to_all(outgoing, 'seq', split_axis=0, concat_axis=0, tiled=True)  5.6 us
    dot_general x1, matrix products, body(): lax.dot_general(grad_tokens, full_weight, contract_last, preferred_elemen...  4.34 us
    all_to_all x1, starting transfers between devices, body(): lax.all_to_all(picked, 'seq', split_axis=0, concat_axis=0, tiled=True)  3.79 us
  transfers between devices with their start and end apart: 5, of which 4 were waited for; matrix products, arithmetic and copies ran while one was open for 10% of the time, Pallas kernels for 0%

commit v1 on v0

v1 whole, which is shorter than its diff:
```python
import functools

import jax
import jax.numpy as jnp
from jax import lax
from jax.experimental import pallas as pl
from jax.experimental.pallas import tpu as pltpu
from jax.sharding import PartitionSpec as P

SQRT_HALF = 0.7071067811865476
INV_SQRT_TWO_PI = 0.3989422804014327
META_ROWS = 16
LANES = 128
VMEM_LIMIT = 48 * 1024 * 1024
F32, BF16, I32 = jnp.float32, jnp.bfloat16, jnp.int32


def iota(shape, dim):
    return lax.broadcasted_iota(I32, shape, dim)


def mm(a, b):
    return jnp.dot(a, b, preferred_element_type=F32)


def pack_kernel(owners, capacity, rows_own, *refs):
    bufs, out = refs[:-1], refs[-1]
    slots = owners * capacity
    frames = bufs[0].shape[0] - META_ROWS
    mel = bufs[0].shape[1]
    toks = frames // 2
    before = (iota((toks, toks), 0) < iota((toks, toks), 1)).astype(F32).astype(BF16)
    lane = iota((slots, LANES), 1)
    meta_out = jnp.zeros((slots, LANES), F32)
    for j, buf in enumerate(bufs):
        meta = buf[frames : frames + META_ROWS, :].astype(F32)
        owner, row = meta[0:1, :].astype(I32), meta[1:2, :]
        mine = (iota((owners, toks), 0) == owner).astype(F32)
        ahead = mm(mine.astype(BF16), before)
        rank = jnp.sum(mine * ahead, axis=0, keepdims=True).astype(I32)
        onehot = (iota((slots, toks), 0) == owner * capacity + rank).astype(F32)
        spot = jnp.sum(onehot * (row - rows_own), axis=1, keepdims=True) + rows_own
        meta_out = jnp.where(lane == j, spot, meta_out)
        onehot = onehot.astype(BF16)
        window = buf[0:frames, :]
        for k in range(4):
            pick = (iota((toks, frames), 1) == 2 * iota((toks, frames), 0) - 1 + k).astype(F32)
            part = mm(pick.astype(BF16), window).astype(BF16)
            left = (j * 4 + k) * mel
            out[:, left : left + mel] = mm(onehot, part).astype(BF16)
    out[:, len(bufs) * 4 * mel :] = meta_out.astype(BF16)


def rows_from_slots(arrived, meta, j, rows):
    spots = jnp.transpose(meta.astype(F32)).astype(I32)
    spots = jnp.sum(jnp.where(iota(spots.shape, 0) == j, spots, 0), axis=0, keepdims=True)
    onehot = (iota((rows, spots.shape[1]), 0) == spots).astype(F32)
    return mm(onehot.astype(BF16), arrived).astype(BF16), onehot


def halves(patch, kernel, bias):
    depth = kernel.shape[0]
    mel = patch.shape[1] // 4
    return mm(patch[:, :depth], kernel) + bias, mm(patch[:, mel:], kernel) + bias


def cdf_of(x):
    return 0.5 * (1.0 + lax.erf(x * SQRT_HALF))


def slope_of(x, cdf):
    return cdf + x * INV_SQRT_TWO_PI * jnp.exp(-0.5 * x * x)


def forward_kernel(arrived, meta, kernel, bias, weight, out):
    rows = out.shape[1]
    patch, _ = rows_from_slots(arrived[...], meta[...], pl.program_id(0) + 1, rows)
    even, odd = halves(patch, kernel[...], bias[...])
    pooled = (0.5 * (even * cdf_of(even) + odd * cdf_of(odd))).astype(BF16)
    out[0] = mm(pooled, weight[...]).astype(BF16)


def backward_kernel(arrived, meta, kernel, bias, weight, grads, grad_out, own_out, valid_out):
    j = pl.program_id(0)
    rows = grads.shape[1]
    patch, onehot = rows_from_slots(arrived[...], meta[...], j, rows)
    even, odd = halves(patch, kernel[...], bias[...])
    even_cdf, odd_cdf = cdf_of(even), cdf_of(odd)

    @pl.when(j == 0)
    def _():
        pooled = (0.5 * (even * even_cdf + odd * odd_cdf)).astype(BF16)
        own_out[...] = mm(pooled, weight[...])
        valid_out[...] = jnp.broadcast_to(jnp.sum(onehot, axis=1, keepdims=True), valid_out.shape)
        grad_out[...] = jnp.zeros_like(grad_out)

    half = 0.5 * grads[0].astype(F32)
    even_grad = (half * slope_of(even, even_cdf)).astype(BF16)
    odd_grad = (half * slope_of(odd, odd_cdf)).astype(BF16)
    depth = kernel.shape[0]
    mel = patch.shape[1] // 4
    first = (((0,), (0,)), ((), ()))
    grad_out[...] += lax.dot_general(
        patch[:, :depth], even_grad, first, preferred_element_type=F32
    ) + lax.dot_general(patch[:, mel:], odd_grad, first, preferred_element_type=F32)


def body(mel_frames, positions, conv_weight, conv_bias, proj_weight, proj_bias, cotangent):
    recs, owners = lax.axis_size("dp"), lax.axis_size("seq")
    dp_index, seq_index = lax.axis_index("dp"), lax.axis_index("seq")
    frames, mel = mel_frames.shape[1:]
    toks = positions.shape[1]
    rows, feats = cotangent.shape[1:]
    capacity = rows // owners
    slots = owners * capacity
    taps = conv_weight.shape[1]
    chans = proj_weight.shape[0]
    assert taps == 3 and toks == LANES == mel and frames == 2 * toks and rows <= 256

    def shift(x, by):
        return lax.ppermute(x, "dp", [(i, (i + by) % recs) for i in range(recs)])

    spots = positions[0][None, :]
    meta = jnp.concatenate(
        [spots // rows, spots % rows, jnp.zeros((META_ROWS - 2, toks), I32)], axis=0
    ).astype(BF16)
    buf = jnp.concatenate([mel_frames[0], meta], axis=0)
    bufs = [buf] + [shift(buf, j) for j in range(1, recs)]
    cots = [cotangent[0]] + [shift(cotangent[0], j) for j in range(1, recs)]

    width = recs * 4 * mel + LANES
    packed = pl.pallas_call(
        functools.partial(pack_kernel, owners, capacity, rows),
        out_shape=jax.ShapeDtypeStruct((slots, width), BF16),
        compiler_params=pltpu.CompilerParams(vmem_limit_bytes=VMEM_LIMIT),
        name="pack_patches",
    )(*bufs)
    arrived = lax.all_to_all(
        packed.reshape(owners, capacity, width), "seq", split_axis=0, concat_axis=0, tiled=True
    ).reshape(slots, width)

    kernel = lax.dynamic_slice_in_dim(conv_weight, dp_index * chans, chans, 2)
    kernel = jnp.transpose(kernel, (1, 0, 2)).reshape(taps * mel, chans)
    bias = lax.dynamic_slice_in_dim(conv_bias, dp_index * chans, chans, 0)[None, :]

    whole = lambda *shape: pl.BlockSpec(shape, lambda j: (0,) * len(shape))
    partial = pl.pallas_call(
        forward_kernel,
        grid=(recs - 1,),
        in_specs=[
            pl.BlockSpec((slots, 4 * mel), lambda j: (0, j + 1)),
            pl.BlockSpec((slots, LANES), lambda j: (0, recs * 4 * mel // LANES)),
            whole(taps * mel, chans),
            whole(1, chans),
            whole(chans, feats),
        ],
        out_specs=pl.BlockSpec((1, rows, feats), lambda j: (j, 0, 0)),
        out_shape=jax.ShapeDtypeStruct((recs - 1, rows, feats), BF16),
        compiler_params=pltpu.CompilerParams(vmem_limit_bytes=VMEM_LIMIT),
        name="forward_partial",
    )(arrived, arrived, kernel, bias, proj_weight)
    returned = [shift(partial[j - 1], -j) for j in range(1, recs)]

    contract_last = (((1,), (1,)), ((), ()))
    grads = jnp.stack(
        [
            lax.dot_general(c, proj_weight, contract_last, preferred_element_type=F32).astype(BF16)
            for c in cots
        ]
    )
    grad_part, own, valid = pl.pallas_call(
        backward_kernel,
        grid=(recs,),
        in_specs=[
            pl.BlockSpec((slots, 4 * mel), lambda j: (0, j)),
            pl.BlockSpec((slots, LANES), lambda j: (0, recs * 4 * mel // LANES)),
            whole(taps * mel, chans),
            whole(1, chans),
            whole(chans, feats),
            pl.BlockSpec((1, rows, chans), lambda j: (j, 0, 0)),
        ],
        out_specs=[whole(taps * mel, chans), whole(rows, feats), whole(rows, LANES)],
        out_shape=[
            jax.ShapeDtypeStruct((taps * mel, chans), F32),
            jax.ShapeDtypeStruct((rows, feats), F32),
            jax.ShapeDtypeStruct((rows, LANES), F32),
        ],
        compiler_params=pltpu.CompilerParams(vmem_limit_bytes=VMEM_LIMIT),
        name="backward",
    )(arrived, arrived, kernel, bias, proj_weight, grads)

    total = own
    for part in returned:
        total = total + part.astype(F32)
    merged = jnp.where(valid[:, :1] > 0.0, total + proj_bias, 0.0).astype(BF16)

    share = mel // owners
    split = grad_part.reshape(taps, owners // 2, 2, share, chans)
    core = seq_index % 2
    keep = lax.dynamic_index_in_dim(split, core, 2, keepdims=False)
    send = lax.dynamic_index_in_dim(split, 1 - core, 2, keepdims=False).astype(BF16)
    got = lax.ppermute(send, "seq", [(i, i ^ 1) for i in range(owners)])
    pair = (keep + got.astype(F32)).astype(BF16)
    pair = jnp.transpose(pair, (1, 0, 2, 3)).reshape(owners // 2, taps * share, chans)
    groups = [list(range(c, owners, 2)) for c in range(2)]
    pieces = lax.all_to_all(
        pair, "seq", split_axis=0, concat_axis=0, axis_index_groups=groups, tiled=True
    )
    grad_weight = jnp.sum(pieces.astype(F32), axis=0).reshape(taps, share, chans)
    return merged[None], jnp.transpose(grad_weight, (1, 0, 2))


def solution(mesh):
    in_specs = (
        P("dp", "seq", None),
        P("dp", "seq"),
        P(),
        P(),
        P("dp", None),
        P(),
        P("dp", "seq", None),
    )
    out_specs = (P("dp", "seq", None), P("seq", None, "dp"))
    return jax.shard_map(body, mesh=mesh, in_specs=in_specs, out_specs=out_specs, check_vma=False)
```

time: 176 us -> 91.7 us (0.52)
  waiting for transfers between devices: 108 us -> 49.7 us
  blocking collectives: 13.6 us -> 0 us
  between operations: 14 us -> 0.81 us
  local copies, waits for them, and re-layouts: 16.2 us -> 3.33 us
  Pallas kernels: 0 us -> 9.95 us
  matrix products: 11.9 us -> 5.26 us
  starting transfers between devices: 9.5 us -> 15.3 us
  other arithmetic: 2.59 us -> 6.87 us
    reduce_scatter x2 -> x0, waiting for transfers between devices: 56.8 us -> none  [the longest x1 49.3 us: body(): lax.psum_scatter(jnp.stack(tap_terms, axis=1), 'seq', scatter_dimension=0...]
    ppermute x0 -> x4, waiting for transfers between devices: none -> 30.9 us  [the longest x3 29.2 us: shift(): return lax.ppermute(x, 'dp', [(i, (i + by) % recs) for i in range(recs)])]
    all_gather x1 -> x0, waiting for transfers between devices: 27.8 us -> none  [body(): full_weight = lax.all_gather(proj_weight, 'dp', axis=0, tiled=True)]
    all_to_all x1 -> x0, blocking collectives: 13.6 us -> none  [body(): lax.all_to_all(dest_rows, 'seq', split_axis=0, concat_axis=0, tiled=True)]
    pallas_call x0 -> x3, Pallas kernels: none -> 9.95 us  [the longest x1 5.77 us: body(): pl.pallas_call(backward_kernel, grid=(recs,), in_specs=[pl.BlockSpec((slo...]
    dot_general x6 -> x2, matrix products: 11.9 us -> 5.26 us  [body(): lax.dot_general(c, proj_weight, contract_last, preferred_element_type=F32)]
    scatter x3 -> x0, local copies, waits for them, and re-layouts: 6.54 us -> none  [the longest x1 3.13 us: body(): merged = jnp.zeros_like(grads_in).at[flat_rows].set(arrived.reshape(flat_...]
    ppermute x0 -> x4, starting transfers between devices: none -> 4.84 us  [the longest x3 4.76 us: shift(): return lax.ppermute(x, 'dp', [(i, (i + by) % recs) for i in range(recs)])]
  transfers between devices with their start and end apart: 5 -> 6, of which waited for: 4 -> 5; matrix products, arithmetic and copies ran while one was open for 10% -> 11% of each run, Pallas kernels for 0% -> 2%
where the time goes in v1:
time: 91.7 us; the launch traced here: 91.2 us
  waiting for transfers between devices  49.7 us (54%)
  starting transfers between devices  15.3 us (17%)
  Pallas kernels  9.95 us (11%)
  other arithmetic  6.87 us (7%)
  matrix products  5.26 us (6%)
  local copies, waits for them, and re-layouts  3.33 us (4%)
    ppermute x3, waiting for transfers between devices, shift(): return lax.ppermute(x, 'dp', [(i, (i + by) % recs) for i in range(recs)])  29.2 us
    all_to_all x1, waiting for transfers between devices, body(): lax.all_to_all(packed.reshape(owners, capacity, width), 'seq', split_axis...  9.98 us
    all_to_all x1, waiting for transfers between devices, body(): lax.all_to_all(pair, 'seq', split_axis=0, concat_axis=0, axis_index_group...  8.87 us
    all_to_all x1, starting transfers between devices, body(): lax.all_to_all(packed.reshape(owners, capacity, width), 'seq', split_axis...  6.13 us
    pallas_call x1, Pallas kernels, body(): pl.pallas_call(backward_kernel, grid=(recs,), in_specs=[pl.BlockSpec((slo...  5.77 us
    dot_general x2, matrix products, body(): lax.dot_general(c, proj_weight, contract_last, preferred_element_type=F32)  5.26 us
    ppermute x3, starting transfers between devices, shift(): return lax.ppermute(x, 'dp', [(i, (i + by) % recs) for i in range(recs)])  4.76 us
    all_to_all x1, starting transfers between devices, body(): lax.all_to_all(pair, 'seq', split_axis=0, concat_axis=0, axis_index_group...  4.3 us
  transfers between devices with their start and end apart: 6, of which 5 were waited for; matrix products, arithmetic and copies ran while one was open for 11% of the time, Pallas kernels for 2%

profile of v1, /device:TPU:0, one launch (start us, length us, event | category | flops | bytes accessed | tf_op | source)
XLA Modules:
  0.0 91.2 jit_solution(5072535641531028210)
XLA Ops:
  0.7 3.0 %collective-permute-start.1 = (bf16[256,2048]{1,0:T(8,128)(2,1)}, bf16[256,2048]{1,0:T(8,128)(2,1)}, u32[]{:S(2)}, u32[]{:S(2)}) collective-permute-start(bf16[256,2048]{1,0:T(8,128)(2,1)} %bitcast.45), channel_id=1, source_target_pairs={{0,16},{16,0},{1,17},{17,1},{2,18},{18,2},{3,19},{19,3},{4,20},{20... | collective-permute-start | bytes 3145736 | tf_op jit(solution)/shard_map/ppermute | solution.py:121
  3.7 0.7 fusion.8
  4.4 0.9 %maximum_maximum_fusion.refs_0_ = bf16[272,128]{1,0:T(8,128)(2,1)S(1)} fusion(bf16[1,128]{1,0:T(2,128)(2,1)S(1)} %get-tuple-element.9, bf16[1,128]{1,0:T(2,128)(2,1)S(1)} %get-tuple-element.8, bf16[256,128]{1,0:T(8,128)(2,1)} %bitcast.43, bf16[272]{0:T(512)(128)(2,1)S(1)} %pad.5.clone), kind=kLoop, calls=%fused_computation.15 | loop fusion | flops 278528 | bytes 136224 | tf_op jit(solution)/shard_map/concatenate | solution.py:127
  5.4 0.2 collective-permute-start
  5.6 23.0 %collective-permute-done.refs_1_ = bf16[272,128]{1,0:T(8,128)(2,1)S(1)} collective-permute-done((bf16[272,128]{1,0:T(8,128)(2,1)S(1)}, bf16[272,128]{1,0:T(8,128)(2,1)S(1)}, u32[]{:S(2)}, u32[]{:S(2)}) %collective-permute-start) | collective-permute-done | bytes 69664 | tf_op jit(solution)/shard_map/ppermute | solution.py:121
  28.6 1.5 %pack_patches.1 = bf16[256,1152]{1,0:T(8,128)(2,1)} custom-call(bf16[272,128]{1,0:T(8,128)(2,1)S(1)} %maximum_maximum_fusion.refs_0_, bf16[272,128]{1,0:T(8,128)(2,1)S(1)} %collective-permute-done.refs_1_), custom_call_target="tpu_custom_call" | custom-call | tf_op jit(solution)/shard_map/pack_patches/pallas_call | solution.py:132
  30.1 6.1 %all-to-all-start = ((bf16[16,16,1152]{2,1,0:T(8,128)(2,1)}), bf16[16,16,1152]{2,1,0:T(8,128)(2,1)S(1)}, u32[]{:S(2)}, u32[]{:S(2)}) async-start(bf16[16,16,1152]{2,1,0:T(8,128)(2,1)} %bitcast.1), calls=%async_computation | async-start | bytes 1179648 | tf_op jit(solution)/shard_map/all_to_all | solution.py:138
  36.3 0.1 dynamic_slice.14
  36.4 3.0 %fusion = bf16[1,256,640]{2,1,0:T(8,128)(2,1)S(1)} fusion(bf16[640,2048]{1,0:T(8,128)(2,1)} %weight.3, bf16[1,256,2048]{2,1,0:T(8,128)(2,1)S(1)} %copy-done.8), kind=kOutput, calls=%fused_computation.3 | convolution fusion | flops 671252480 | bytes 3997696 | tf_op jit(solution)/shard_map/dot_general | solution.py:167
  39.4 2.3 %fusion.1 = bf16[1,256,640]{2,1,0:T(8,128)(2,1)S(1)} fusion(bf16[256,2048]{1,0:T(8,128)(2,1)} %collective-permute-done.1, bf16[640,2048]{1,0:T(8,128)(2,1)S(1)} %copy-done.1), kind=kOutput, calls=%fused_computation.4 | convolution fusion | flops 671252480 | bytes 3997696 | tf_op jit(solution)/shard_map/dot_general | solution.py:167
  41.8 10.0 %all-to-all-done = bf16[16,16,1152]{2,1,0:T(8,128)(2,1)S(1)} async-done(((bf16[16,16,1152]{2,1,0:T(8,128)(2,1)}), bf16[16,16,1152]{2,1,0:T(8,128)(2,1)S(1)}, u32[]{:S(2)}, u32[]{:S(2)}) %all-to-all-start) | async-done | bytes 589856 | tf_op jit(solution)/shard_map/all_to_all | solution.py:138
  51.8 1.7 %copy-done.2 = bf16[640,2048]{1,0:T(8,128)(2,1)S(1)} copy-done((bf16[640,2048]{1,0:T(8,128)(2,1)S(1)}, bf16[640,2048]{1,0:T(8,128)(2,1)}, u32[]{:S(2)}) %copy-start.2) | copy-done | bytes 2621464
  53.5 2.6 %forward_partial.1 = bf16[1,256,2048]{2,1,0:T(8,128)(2,1)} custom-call(bf16[256,1152]{1,0:T(8,128)(2,1)S(1)} %bitcast.35, bf16[256,1152]{1,0:T(8,128)(2,1)S(1)} %bitcast.36, bf16[384,640]{1,0:T(8,128)(2,1)S(1)} %bitcast.39, f32[1,640]{1,0:T(1,128)S(1)} %broadcast_in_dim.25.bias, bf16[640,2048]{1,0:T(8,128)(2,1)S(1)} %copy-done.2), custom_call_target="tpu_custom_call" | custom-call | tf_op jit(solution)/shard_map/forward_partial/pallas_call | solution.py:147
  56.2 5.8 %backward.1 = (f32[384,640]{1,0:T(8,128)S(1)}, f32[256,2048]{1,0:T(8,128)S(1)}, f32[256,128]{1,0:T(8,128)S(1)}) custom-call(bf16[256,1152]{1,0:T(8,128)(2,1)S(1)} %bitcast.37, bf16[256,1152]{1,0:T(8,128)(2,1)S(1)} %bitcast.38, bf16[384,640]{1,0:T(8,128)(2,1)S(1)} %bitcast.40, f32[1,640]{1,0:T(1,128)S(1)} %broadcast_in_dim.25.bias, bf16[640,2048]{1,0:T(8,128)(2,1)} %weight.3, ...), custom_call_target="tpu_custom_call" | custom-call | tf_op jit(solution)/shard_map/backward/pallas_call | solution.py:171
  62.0 1.3 %copy-done.3 = f32[256,2048]{1,0:T(8,128)} copy-done((f32[256,2048]{1,0:T(8,128)}, f32[256,2048]{1,0:T(8,128)S(1)}, u32[]{:S(2)}) %copy-start.3) | copy-done | bytes 2097176
  63.3 1.5 %collective-permute-start.2 = (bf16[256,2048]{1,0:T(8,128)(2,1)}, bf16[256,2048]{1,0:T(8,128)(2,1)}, u32[]{:S(2)}, u32[]{:S(2)}) collective-permute-start(bf16[256,2048]{1,0:T(8,128)(2,1)} %bitcast.9), channel_id=1, source_target_pairs={{0,16},{16,0},{1,17},{17,1},{2,18},{18,2},{3,19},{19,3},{4,20},{20... | collective-permute-start | bytes 3145736 | tf_op jit(solution)/shard_map/ppermute | solution.py:121
  64.9 1.6 %collective-permute-done.3 = bf16[3,8,8,640]{3,2,0,1:T(8,128)(2,1)} collective-permute-done((bf16[3,8,8,640]{3,2,0,1:T(8,128)(2,1)S(1)}, bf16[3,8,8,640]{3,2,0,1:T(8,128)(2,1)}, u32[]{:S(2)}, u32[]{:S(2)}) %collective-permute-start.3) | collective-permute-done | bytes 245792 | tf_op jit(solution)/shard_map/ppermute | solution.py:202
  66.6 1.9 %fusion.4 = bf16[8,24,640]{2,1,0:T(8,128)(2,1)} fusion(bf16[3,8,8,640]{3,2,0,1:T(8,128)(2,1)} %collective-permute-done.3, f32[3,8,2,8,640]{4,3,2,1,0:T(8,128)} %bitcast.42, s32[]{:T(128)S(6)} %select_n.38), kind=kLoop, calls=%fused_computation.11 | loop fusion | flops 368640 | bytes 983044 | tf_op jit(solution)/shard_map/reshape | solution.py:204
  68.5 4.3 %all-to-all-start.1 = ((bf16[8,24,640]{2,1,0:T(8,128)(2,1)}), bf16[8,24,640]{2,1,0:T(8,128)(2,1)S(1)}, u32[]{:S(2)}, u32[]{:S(2)}) async-start(bf16[8,24,640]{2,1,0:T(8,128)(2,1)} %fusion.4), calls=%async_computation.1 | async-start | bytes 491520 | tf_op jit(solution)/shard_map/all_to_all | solution.py:206
  72.8 0.1 fusion.6
  72.9 8.9 %all-to-all-done.1 = bf16[8,24,640]{2,1,0:T(8,128)(2,1)S(1)} async-done(((bf16[8,24,640]{2,1,0:T(8,128)(2,1)}), bf16[8,24,640]{2,1,0:T(8,128)(2,1)S(1)}, u32[]{:S(2)}, u32[]{:S(2)}) %all-to-all-start.1) | async-done | bytes 245792 | tf_op jit(solution)/shard_map/all_to_all | solution.py:206
  81.7 0.7 convert_reduce_fusion
  82.4 6.3 %collective-permute-done.2 = bf16[256,2048]{1,0:T(8,128)(2,1)} collective-permute-done((bf16[256,2048]{1,0:T(8,128)(2,1)}, bf16[256,2048]{1,0:T(8,128)(2,1)}, u32[]{:S(2)}, u32[]{:S(2)}) %collective-permute-start.2) | collective-permute-done | bytes 1048608 | tf_op jit(solution)/shard_map/ppermute | solution.py:121
  88.7 2.5 %fusion.2 = bf16[1,256,2048]{2,1,0:T(8,128)(2,1)} fusion(f32[256,2048]{1,0:T(8,128)S(1)} %copy-done.4, bf16[256,2048]{1,0:T(8,128)(2,1)} %collective-permute-done.2, f32[2048]{0:T(1024)S(1)} %copy-done.6, pred[256]{0:T(512)(128)(4,1)S(1)} %fusion.6), kind=kLoop, calls=%fused_computation.5 | loop fusion | flops 2621440 | bytes 4202752 | tf_op jit(solution)/shard_map/broadcast_in_dim | solution.py:210
  (24 shorter events, 0.3 us)
Async XLA Ops:
  0.6 35.7 %copy-start = (bf16[128,3,1280]{2,0,1:T(8,128)(2,1)S(1)}, bf16[128,3,1280]{2,0,1:T(8,128)(2,1)}, u32[]{:S(2)}) copy-start(bf16[128,3,1280]{2,0,1:T(8,128)(2,1)} %param.9) | copy-start | bytes 2949124
  0.6 35.7 %copy-start.8 = (bf16[1,256,2048]{2,1,0:T(8,128)(2,1)S(1)}, bf16[1,256,2048]{2,1,0:T(8,128)(2,1)}, u32[]{:S(2)}) copy-start(bf16[1,256,2048]{2,1,0:T(8,128)(2,1)} %param.13) | copy-start | bytes 3145732
  0.7 35.6 %copy-start.7 = (f32[1280]{0:T(1024)S(1)}, f32[1280]{0:T(1024)}, u32[]{:S(2)}) copy-start(f32[1280]{0:T(1024)} %param.10) | copy-start | bytes 15364
  0.7 38.8 %collective-permute-start.1 = (bf16[256,2048]{1,0:T(8,128)(2,1)}, bf16[256,2048]{1,0:T(8,128)(2,1)}, u32[]{:S(2)}, u32[]{:S(2)}) collective-permute-start(bf16[256,2048]{1,0:T(8,128)(2,1)} %bitcast.45), channel_id=1, source_target_pairs={{0,16},{16,0},{1,17},{17,1},{2,18},{18,2},{3,19},{19,3},{4,20},{20... | collective-permute-start | bytes 3145736 | tf_op jit(solution)/shard_map/ppermute | solution.py:121
  5.4 23.2 %collective-permute-start = (bf16[272,128]{1,0:T(8,128)(2,1)S(1)}, bf16[272,128]{1,0:T(8,128)(2,1)S(1)}, u32[]{:S(2)}, u32[]{:S(2)}) collective-permute-start(bf16[272,128]{1,0:T(8,128)(2,1)S(1)} %maximum_maximum_fusion.refs_0_), channel_id=1, source_target_pairs={{0,16},{16,0},{1,17},{17,1},{2,18},{18,2},{3,19},{19,3},{4,20},{20... | collective-permute-start | bytes 208904 | tf_op jit(solution)/shard_map/ppermute | solution.py:121
  30.1 21.7 %all-to-all-start = ((bf16[16,16,1152]{2,1,0:T(8,128)(2,1)}), bf16[16,16,1152]{2,1,0:T(8,128)(2,1)S(1)}, u32[]{:S(2)}, u32[]{:S(2)}) async-start(bf16[16,16,1152]{2,1,0:T(8,128)(2,1)} %bitcast.1), calls=%async_computation | async-start | bytes 1179648 | tf_op jit(solution)/shard_map/all_to_all | solution.py:138
  36.4 3.0 %copy-start.1 = (bf16[640,2048]{1,0:T(8,128)(2,1)S(1)}, bf16[640,2048]{1,0:T(8,128)(2,1)}, u32[]{:S(2)}) copy-start(bf16[640,2048]{1,0:T(8,128)(2,1)} %weight.3) | copy-start | bytes 7864324
  51.8 1.7 %copy-start.2 = (bf16[640,2048]{1,0:T(8,128)(2,1)S(1)}, bf16[640,2048]{1,0:T(8,128)(2,1)}, u32[]{:S(2)}) copy-start(bf16[640,2048]{1,0:T(8,128)(2,1)} %weight.3) | copy-start | bytes 7864324
  61.9 1.3 %copy-start.3 = (f32[256,2048]{1,0:T(8,128)}, f32[256,2048]{1,0:T(8,128)S(1)}, u32[]{:S(2)}) copy-start(f32[256,2048]{1,0:T(8,128)S(1)} %get-tuple-element.6) | copy-start | bytes 6291460
  63.3 1.5 %copy-start.5 = (f32[384,640]{1,0:T(8,128)}, f32[384,640]{1,0:T(8,128)S(1)}, u32[]{:S(2)}) copy-start(f32[384,640]{1,0:T(8,128)S(1)} %get-tuple-element.7) | copy-start | bytes 2949124
  63.3 25.4 %copy-start.6 = (f32[2048]{0:T(1024)S(1)}, f32[2048]{0:T(1024)}, u32[]{:S(2)}) copy-start(f32[2048]{0:T(1024)} %param.12) | copy-start | bytes 24580
  63.3 25.4 %copy-start.4 = (f32[256,2048]{1,0:T(8,128)S(1)}, f32[256,2048]{1,0:T(8,128)}, u32[]{:S(2)}) copy-start(f32[256,2048]{1,0:T(8,128)} %copy-done.3) | copy-start | bytes 6291460
  63.3 25.4 %collective-permute-start.2 = (bf16[256,2048]{1,0:T(8,128)(2,1)}, bf16[256,2048]{1,0:T(8,128)(2,1)}, u32[]{:S(2)}, u32[]{:S(2)}) collective-permute-start(bf16[256,2048]{1,0:T(8,128)(2,1)} %bitcast.9), channel_id=1, source_target_pairs={{0,16},{16,0},{1,17},{17,1},{2,18},{18,2},{3,19},{19,3},{4,20},{20... | collective-permute-start | bytes 3145736 | tf_op jit(solution)/shard_map/ppermute | solution.py:121
  64.8 1.7 %collective-permute-start.3 = (bf16[3,8,8,640]{3,2,0,1:T(8,128)(2,1)S(1)}, bf16[3,8,8,640]{3,2,0,1:T(8,128)(2,1)}, u32[]{:S(2)}, u32[]{:S(2)}) collective-permute-start(bf16[3,8,8,640]{3,2,0,1:T(8,128)(2,1)S(1)} %fusion.5), channel_id=1, source_target_pairs={{0,1},{1,0},{2,3},{3,2},{4,5},{5,4},{6,7},{7,6},{8,9},{9,8},{10,11... | collective-permute-start | bytes 737288 | tf_op jit(solution)/shard_map/ppermute | solution.py:202
  68.5 13.3 %all-to-all-start.1 = ((bf16[8,24,640]{2,1,0:T(8,128)(2,1)}), bf16[8,24,640]{2,1,0:T(8,128)(2,1)S(1)}, u32[]{:S(2)}, u32[]{:S(2)}) async-start(bf16[8,24,640]{2,1,0:T(8,128)(2,1)} %fusion.4), calls=%async_computation.1 | async-start | bytes 491520 | tf_op jit(solution)/shard_map/all_to_all | solution.py:206

commit v2 on v0

v2 whole, which is shorter than its diff:
```python
import functools

import jax
import jax.numpy as jnp
from jax import lax
from jax.experimental import pallas as pl
from jax.experimental.pallas import tpu as pltpu
from jax.sharding import PartitionSpec as P

SQRT_HALF = 0.7071067811865476
INV_SQRT_TWO_PI = 0.3989422804014327
LANES = 128
VMEM_LIMIT = 48 * 1024 * 1024
F32, BF16, I32 = jnp.float32, jnp.bfloat16, jnp.int32


def iota(shape, dim):
    return lax.broadcasted_iota(I32, shape, dim)


def mm(a, b):
    return jnp.dot(a, b, preferred_element_type=F32)


def call(kernel, out_shape, name, **kwargs):
    return pl.pallas_call(
        kernel,
        out_shape=out_shape,
        compiler_params=pltpu.CompilerParams(vmem_limit_bytes=VMEM_LIMIT),
        name=name,
        **kwargs,
    )


def pack_kernel(owners, capacity, rows_own, mel_ref, spots_ref, out):
    slots = owners * capacity
    frames, mel = mel_ref.shape
    toks = frames // 2
    spots = spots_ref[...]
    owner = spots // rows_own
    row = spots - owner * rows_own
    before = (iota((toks, toks), 0) < iota((toks, toks), 1)).astype(F32).astype(BF16)
    mine = (iota((owners, toks), 0) == owner).astype(F32)
    ahead = mm(mine.astype(BF16), before)
    rank = jnp.sum(mine * ahead, axis=0, keepdims=True).astype(I32)
    onehot = (iota((slots, toks), 0) == owner * capacity + rank).astype(F32)
    spot = jnp.sum(onehot * (row - rows_own).astype(F32), axis=1, keepdims=True) + rows_own
    onehot = onehot.astype(BF16)
    window = mel_ref[...]
    for k in range(4):
        pick = (iota((toks, frames), 1) == 2 * iota((toks, frames), 0) - 1 + k).astype(F32)
        part = mm(pick.astype(BF16), window).astype(BF16)
        out[:, k * mel : (k + 1) * mel] = mm(onehot, part).astype(BF16)
    out[:, 4 * mel :] = jnp.broadcast_to(spot, (slots, LANES)).astype(BF16)


def rows_from_slots(arrived, rows):
    width = arrived.shape[1] - LANES
    spots = jnp.transpose(arrived[:, width:].astype(F32))[0:1, :].astype(I32)
    onehot = (iota((rows, spots.shape[1]), 0) == spots).astype(F32)
    return mm(onehot.astype(BF16), arrived[:, :width]).astype(BF16), onehot


def activation_kernel(own, other, kernel, bias, order, pooled_out, slope_out, left_out, valid_out):
    rows = pooled_out.shape[1]
    depth = kernel.shape[0]
    for n, ref in enumerate((own, other)):
        patch, onehot = rows_from_slots(ref, rows)
        if n == 0:
            valid_out[...] = jnp.broadcast_to(
                jnp.sum(onehot, axis=1, keepdims=True), valid_out.shape
            )
        mel = patch.shape[1] // 4
        acts = []
        for p in range(2):
            frames = patch[:, p * mel : p * mel + depth]
            left_out[n, p] = mm(frames, order[...]).astype(BF16)
            x = mm(frames, kernel[...]) + bias[...]
            cdf = 0.5 * (1.0 + lax.erf(x * SQRT_HALF))
            acts.append(x * cdf)
            slope_out[n, p] = 0.5 * (cdf + x * INV_SQRT_TWO_PI * jnp.exp(-0.5 * x * x))
        pooled_out[n] = (0.5 * (acts[0] + acts[1])).astype(BF16)


def assemble(offsets, weights, whole):
    for n, ref in enumerate(weights):
        start = pl.multiple_of(offsets[n], 16)
        whole[pl.ds(start, ref.shape[0]), :] = ref[...]


def backward_kernel(offsets, halves, cot_own, cot_other, slope, left, *refs):
    weights, out, whole = refs[:-2], refs[-2], refs[-1]
    assemble(offsets, weights, whole)
    first = (((0,), (0,)), ((), ()))
    last = (((1,), (1,)), ((), ()))
    total = None
    for n, cot in enumerate((cot_own, cot_other)):
        grads = lax.dot_general(cot[...], whole[...], last, preferred_element_type=F32)
        grads = grads.astype(BF16).astype(F32)
        for p in range(2):
            pre = (grads * slope[n, p]).astype(BF16)
            term = lax.dot_general(left[n, p], pre, first, preferred_element_type=F32)
            total = term if total is None else total + term
    share = out.shape[2]
    for j in range(out.shape[0]):
        out[halves[j]] = total[:, j * share : (j + 1) * share].astype(BF16)


def forward_kernel(offsets, pooled, *refs):
    weights, other_out, own_out, whole = refs[:-3], refs[-3], refs[-2], refs[-1]
    assemble(offsets, weights, whole)
    other_out[...] = mm(pooled[1], whole[...]).astype(BF16)
    own_out[...] = mm(pooled[0], whole[...])


def body(mel_frames, positions, conv_weight, conv_bias, proj_weight, proj_bias, cotangent):
    recs, owners = lax.axis_size("dp"), lax.axis_size("seq")
    dp_index, seq_index = lax.axis_index("dp"), lax.axis_index("seq")
    core, side = seq_index % 2, (seq_index // 2) % 2
    frames, mel = mel_frames.shape[1:]
    toks = positions.shape[1]
    rows, feats = cotangent.shape[1:]
    capacity = rows // owners
    slots = owners * capacity
    taps = conv_weight.shape[1]
    depth = taps * mel
    chans = proj_weight.shape[0]
    quarter = chans // 2
    width = recs * quarter
    assert taps == 3 and toks == LANES == mel and frames == 2 * toks and rows <= 256

    def shift(x, by):
        return lax.ppermute(x, "dp", [(i, (i + by) % recs) for i in range(recs)])

    def swap(x, bit):
        return lax.ppermute(x, "seq", [(i, i ^ bit) for i in range(owners)])

    end = quarter * 7 // 20 // 16 * 16
    middle = quarter - 2 * end
    base = core * quarter
    head = lax.dynamic_slice_in_dim(proj_weight, base + side * (end + middle), end, 0)
    mid = lax.dynamic_slice_in_dim(proj_weight, base + end, middle, 0)
    own_rows = lax.dynamic_slice_in_dim(proj_weight, base, quarter, 0)
    weights, offsets = [own_rows], [0]
    heads = [shift(head, j) for j in range(1, recs)]
    mids = [shift(mid, j) for j in range(1, recs)]
    tails = [swap(h, 2) for h in heads]
    for j in range(1, recs):
        weights += [heads[j - 1], mids[j - 1], tails[j - 1]]
        at = j * quarter
        offsets += [at + side * (end + middle), at + end, at + (1 - side) * (end + middle)]
    offsets = jnp.stack([jnp.asarray(o, I32) for o in offsets])
    halves = jnp.stack([(dp_index - j) % recs for j in range(recs)]).astype(I32)
    smem = pl.BlockSpec(memory_space=pltpu.SMEM)
    vmem = pl.BlockSpec(memory_space=pltpu.VMEM)

    cot_own = cotangent[0]
    cot_other = swap(cot_own, 1)

    packed = call(
        functools.partial(pack_kernel, owners, capacity, rows),
        jax.ShapeDtypeStruct((slots, 4 * mel + LANES), BF16),
        "pack_patches",
    )(mel_frames[0], positions)
    arrived = lax.all_to_all(
        packed.reshape(owners, capacity, -1), "seq", split_axis=0, concat_axis=0, tiled=True
    ).reshape(slots, -1)
    arrived_other = swap(arrived, 1)

    def mine(x):
        x = x.reshape(x.shape[0], recs, 2, quarter)
        x = lax.dynamic_index_in_dim(x, core, 2, keepdims=False)
        return jnp.concatenate(
            [lax.dynamic_index_in_dim(x, halves[j], 1, keepdims=False) for j in range(recs)], axis=1
        )

    kernel = mine(jnp.transpose(conv_weight, (1, 0, 2)).reshape(depth, -1))
    bias = mine(conv_bias[None, :])
    share = mel // owners
    target = jnp.arange(depth)
    target = (target // share % taps) * mel + target // (taps * share) * share + target % share
    order = (jnp.arange(depth)[:, None] == target[None, :]).astype(BF16)

    pooled, slope, left, valid = call(
        activation_kernel,
        [
            jax.ShapeDtypeStruct((2, rows, width), BF16),
            jax.ShapeDtypeStruct((2, 2, rows, width), F32),
            jax.ShapeDtypeStruct((2, 2, rows, depth), BF16),
            jax.ShapeDtypeStruct((rows, LANES), F32),
        ],
        "activations",
    )(arrived, arrived_other, kernel, bias, order)

    whole = pltpu.VMEM((width, feats), BF16)
    sums = call(
        backward_kernel,
        jax.ShapeDtypeStruct((recs, depth, quarter), BF16),
        "backward",
        in_specs=[smem, smem] + [vmem] * (4 + len(weights)),
        scratch_shapes=[whole],
    )(offsets, halves, cot_own, cot_other, slope, left, *weights)
    pieces = lax.all_to_all(
        sums.reshape(recs * owners, taps * share, quarter),
        ("dp", "seq"),
        split_axis=0,
        concat_axis=0,
        tiled=True,
    )
    pieces = pieces.reshape(recs * owners // 2, 2, taps * share, quarter)
    grad_weight = jnp.sum(pieces.astype(F32), axis=0)
    grad_weight = jnp.transpose(grad_weight, (1, 0, 2)).reshape(taps, share, chans)

    partial, own = call(
        forward_kernel,
        [
            jax.ShapeDtypeStruct((rows, feats), BF16),
            jax.ShapeDtypeStruct((rows, feats), F32),
        ],
        "forward",
        in_specs=[smem] + [vmem] * (1 + len(weights)),
        scratch_shapes=[whole],
    )(offsets, pooled, *weights)
    total = own + swap(partial, 1).astype(F32) + proj_bias
    merged = jnp.where(valid[:, :1] > 0.0, total, 0.0).astype(BF16)
    return merged[None], jnp.transpose(grad_weight, (1, 0, 2))


def solution(mesh):
    in_specs = (
        P("dp", "seq", None),
        P("dp", "seq"),
        P(),
        P(),
        P("dp", None),
        P(),
        P("dp", "seq", None),
    )
    out_specs = (P("dp", "seq", None), P("seq", None, "dp"))
    return jax.shard_map(body, mesh=mesh, in_specs=in_specs, out_specs=out_specs, check_vma=False)
```

time: 176 us -> 73.7 us (0.42)
  waiting for transfers between devices: 108 us -> 22.8 us
  Pallas kernels: 0 us -> 15.6 us
  blocking collectives: 13.6 us -> 0 us
  between operations: 14 us -> 0.85 us
  matrix products: 11.9 us -> 0 us
  starting transfers between devices: 9.5 us -> 17.1 us
  local copies, waits for them, and re-layouts: 16.2 us -> 11.2 us
  other arithmetic: 2.59 us -> 5.61 us
    reduce_scatter x2 -> x0, waiting for transfers between devices: 56.8 us -> none  [the longest x1 49.3 us: body(): lax.psum_scatter(jnp.stack(tap_terms, axis=1), 'seq', scatter_dimension=0...]
    all_gather x1 -> x0, waiting for transfers between devices: 27.8 us -> none  [body(): full_weight = lax.all_gather(proj_weight, 'dp', axis=0, tiled=True)]
    pallas_call x0 -> x4, Pallas kernels: none -> 15.6 us  [the longest x1 6.52 us: body(): call(backward_kernel, jax.ShapeDtypeStruct((recs, depth, quarter), BF16),...]
    all_to_all x1 -> x0, blocking collectives: 13.6 us -> none  [body(): lax.all_to_all(dest_rows, 'seq', split_axis=0, concat_axis=0, tiled=True)]
    dot_general x6 -> x0, matrix products: 11.9 us -> none  [the longest x1 4.34 us: body(): lax.dot_general(grad_tokens, full_weight, contract_last, preferred_elemen...]
    ppermute x0 -> x6, waiting for transfers between devices: none -> 8.82 us  [the longest x4 4.5 us: swap(): return lax.ppermute(x, 'seq', [(i, i ^ bit) for i in range(owners)])]
    all_to_all x2, waiting for transfers between devices: 22.8 us -> 14 us  [the longest x1 14 us: body(): lax.all_to_all(sums.reshape(recs * owners, taps * share, quarter), ('dp',...]
    scatter x3 -> x0, local copies, waits for them, and re-layouts: 6.54 us -> none  [the longest x1 3.13 us: body(): merged = jnp.zeros_like(grads_in).at[flat_rows].set(arrived.reshape(flat_...]
  transfers between devices with their start and end apart: 5 -> 8, of which waited for: 4 -> 4; matrix products, arithmetic and copies ran while one was open for 10% -> 16% of each run, Pallas kernels for 0% -> 20%
where the time goes in v2:
time: 73.7 us; the launch traced here: 73.2 us
  waiting for transfers between devices  22.8 us (31%)
  starting transfers between devices  17.1 us (23%)
  Pallas kernels  15.6 us (21%)
  local copies, waits for them, and re-layouts  11.2 us (15%)
  other arithmetic  5.61 us (8%)
  between operations  0.85 us (1%)
    all_to_all x1, waiting for transfers between devices, body(): lax.all_to_all(sums.reshape(recs * owners, taps * share, quarter), ('dp',...  14 us
    all_to_all x1, starting transfers between devices, body(): lax.all_to_all(packed.reshape(owners, capacity, -1), 'seq', split_axis=0,...  7.4 us
    pallas_call x1, Pallas kernels, body(): call(backward_kernel, jax.ShapeDtypeStruct((recs, depth, quarter), BF16),...  6.52 us
    all_to_all x1, starting transfers between devices, body(): lax.all_to_all(sums.reshape(recs * owners, taps * share, quarter), ('dp',...  5.69 us
    pallas_call x1, Pallas kernels, body(): call(forward_kernel, [jax.ShapeDtypeStruct((rows, feats), BF16), jax.Shap...  4.51 us
    ppermute x4, waiting for transfers between devices, swap(): return lax.ppermute(x, 'seq', [(i, i ^ bit) for i in range(owners)])  4.5 us
    ppermute x2, waiting for transfers between devices, shift(): return lax.ppermute(x, 'dp', [(i, (i + by) % recs) for i in range(recs)])  4.32 us
    pallas_call x1, Pallas kernels, body(): call(activation_kernel, [jax.ShapeDtypeStruct((2, rows, width), BF16), ja...  3.45 us
  transfers between devices with their start and end apart: 8, of which 4 were waited for; matrix products, arithmetic and copies ran while one was open for 16% of the time, Pallas kernels for 20%

profile of v2, /device:TPU:0, one launch (start us, length us, event | category | flops | bytes accessed | tf_op | source)
XLA Modules:
  0.0 73.2 jit_solution(4298139529483872912)
XLA Ops:
  0.7 1.0 %copy-done.6 = bf16[1,256,128]{2,1,0:T(8,128)(2,1)S(1)} copy-done((bf16[1,256,128]{2,1,0:T(8,128)(2,1)S(1)}, bf16[1,256,128]{2,1,0:T(8,128)(2,1)}, u32[]{:S(2)}) %copy-start.6) | copy-done | bytes 65560
  1.6 0.7 copy-done.7
  2.3 1.2 %pack_patches.1 = bf16[256,640]{1,0:T(8,128)(2,1)} custom-call(bf16[256,128]{1,0:T(8,128)(2,1)S(1)} %bitcast.28, s32[1,128]{1,0:T(1,128)S(1)} %copy-done.7), custom_call_target="tpu_custom_call" | custom-call | tf_op jit(solution)/shard_map/pack_patches/pallas_call | solution.py:160
  3.4 7.4 %all-to-all-start = ((bf16[16,16,640]{2,1,0:T(8,128)(2,1)}), bf16[16,16,640]{2,1,0:T(8,128)(2,1)}, u32[]{:S(2)}, u32[]{:S(2)}) async-start(bf16[16,16,640]{2,1,0:T(8,128)(2,1)} %bitcast.1), calls=%async_computation | async-start | bytes 655360 | tf_op jit(solution)/shard_map/all_to_all | solution.py:165
  10.9 0.8 %constant_dynamic-slice_fusion.1 = bf16[112,2048]{1,0:T(8,128)(2,1)} fusion(bf16[640,2048]{1,0:T(8,128)(2,1)S(1)} %copy-done, s32[]{:T(128)S(6)} %select_n.108), kind=kLoop, calls=%fused_computation.33 | loop fusion | bytes 917508 | tf_op jit(solution)/shard_map/dynamic_slice | solution.py:141
  11.7 1.5 %collective-permute-start.1 = (bf16[112,2048]{1,0:T(8,128)(2,1)}, bf16[112,2048]{1,0:T(8,128)(2,1)}, u32[]{:S(2)}, u32[]{:S(2)}) collective-permute-start(bf16[112,2048]{1,0:T(8,128)(2,1)} %constant_dynamic-slice_fusion.1), channel_id=1, source_target_pairs={{0,16},{16,0},{1,17},{17,1},{2,18},{18,2},{3,19},{19,3},{4,20},{20... | collective-permute-start | bytes 1376264 | tf_op jit(solution)/shard_map/ppermute | solution.py:133
  13.3 0.8 %constant_dynamic-slice_fusion = bf16[96,2048]{1,0:T(8,128)(2,1)} fusion(bf16[640,2048]{1,0:T(8,128)(2,1)S(1)} %copy-done, s32[]{:T(128)S(6)} %select_n.109), kind=kLoop, calls=%fused_computation.32 | loop fusion | bytes 786436 | tf_op jit(solution)/shard_map/dynamic_slice | solution.py:142
  14.0 0.5 collective-permute-start.2
  14.5 2.9 %reshape_reshape.3 = bf16[384,2,2,320]{3,2,1,0:T(2,128)(2,1)} reshape(bf16[3,128,1280]{2,1,0:T(8,128)(2,1)} %bitcast.29) | data formatting | bytes 1966080 | tf_op jit(solution)/shard_map/reshape;reshape | solution.py:171
  17.5 2.5 %constant_dynamic-slice_fusion.6 = (bf16[384,1,1,320]{3,2,1,0:T(2,128)(2,1)S(1)}, bf16[384,1,1,320]{3,2,1,0:T(2,128)(2,1)S(1)}) fusion(bf16[384,2,2,320]{3,2,1,0:T(2,128)(2,1)} %reshape_reshape.3, s32[]{:T(128)S(6)} %select_n.94, s32[]{:T(128)S(6)} %select_n.97, s32[]{:T(128)S(6)} %select_n.100), kind=kLoop, calls=%fused_computation.38 | loop fusion | bytes 983052 | tf_op jit(solution)/shard_map/jit(dynamic_index_in_dim)/dynamic_slice | solution.py:174
  20.3 0.8 %fusion.1.order = bf16[384,384]{1,0:T(8,128)(2,1)} fusion(s32[384]{0:T(512)S(1)} %fusion.9), kind=kLoop, calls=%fused_computation.4 | loop fusion | flops 294912 | bytes 296448 | tf_op jit(solution)/shard_map/convert_element_type | solution.py:182
  21.1 4.3 %collective-permute-done.1.refs_1_ = bf16[112,2048]{1,0:T(8,128)(2,1)} collective-permute-done((bf16[112,2048]{1,0:T(8,128)(2,1)}, bf16[112,2048]{1,0:T(8,128)(2,1)}, u32[]{:S(2)}, u32[]{:S(2)}) %collective-permute-start.1) | collective-permute-done | bytes 458784 | tf_op jit(solution)/shard_map/ppermute | solution.py:133
  25.4 1.9 %collective-permute-start.3 = (bf16[112,2048]{1,0:T(8,128)(2,1)}, bf16[112,2048]{1,0:T(8,128)(2,1)}, u32[]{:S(2)}, u32[]{:S(2)}) collective-permute-start(bf16[112,2048]{1,0:T(8,128)(2,1)} %collective-permute-done.1.refs_1_), channel_id=1, source_target_pairs={{0,2},{1,3},{2,0},{3,1},{4,6},{5,7},{6,4},{7,5},{8,10},{9,11},{10,... | collective-permute-start | bytes 1376264 | tf_op jit(solution)/shard_map/ppermute | solution.py:136
  27.7 1.6 %collective-permute-done.other = bf16[256,640]{1,0:T(8,128)(2,1)S(1)} collective-permute-done((bf16[256,640]{1,0:T(8,128)(2,1)}, bf16[256,640]{1,0:T(8,128)(2,1)S(1)}, u32[]{:S(2)}, u32[]{:S(2)}) %collective-permute-start) | collective-permute-done | bytes 327712 | tf_op jit(solution)/shard_map/ppermute | solution.py:136
  29.3 3.5 %activations.1 = (bf16[2,256,640]{2,1,0:T(8,128)(2,1)S(1)}, f32[2,2,256,640]{3,2,1,0:T(8,128)S(1)}, bf16[2,2,256,384]{3,2,1,0:T(8,128)(2,1)S(1)}, f32[256,128]{1,0:T(8,128)S(1)}) custom-call(bf16[256,640]{1,0:T(8,128)(2,1)} %bitcast.2.own, bf16[256,640]{1,0:T(8,128)(2,1)S(1)} %collective-permute-done.other, bf16[384,640]{1,0:T(8,128)(2,1)S(1)} %pad_maximum_fusion.kernel, ...), custom_call_target="tpu_custom_call" | custom-call | tf_op jit(solution)/shard_map/activations/pallas_call | solution.py:184
  32.7 1.5 %copy-done.1 = f32[2,2,256,640]{3,2,1,0:T(8,128)} copy-done((f32[2,2,256,640]{3,2,1,0:T(8,128)}, f32[2,2,256,640]{3,2,1,0:T(8,128)S(1)}, u32[]{:S(2)}) %copy-start.1) | copy-done | bytes 2621464
  34.2 2.9 %collective-permute-done.3.refs_3_ = bf16[112,2048]{1,0:T(8,128)(2,1)} collective-permute-done((bf16[112,2048]{1,0:T(8,128)(2,1)}, bf16[112,2048]{1,0:T(8,128)(2,1)}, u32[]{:S(2)}, u32[]{:S(2)}) %collective-permute-start.3) | collective-permute-done | bytes 458784 | tf_op jit(solution)/shard_map/ppermute | solution.py:136
  37.1 4.5 %forward.1 = (bf16[256,2048]{1,0:T(8,128)(2,1)}, f32[256,2048]{1,0:T(8,128)}) custom-call(s32[4]{0:T(128)S(1)} %pad_add_fusion.offsets, bf16[2,256,640]{2,1,0:T(8,128)(2,1)S(1)} %get-tuple-element.9.pooled, bf16[320,2048]{1,0:T(8,128)(2,1)S(1)} %constant_dynamic-slice_fusion.2.refs_0_, bf16[112,2048]{1,0:T(8,128)(2,1)} %collective-permute-done.1.refs_1_, ...), custom_call_target="tpu_custom_call" | custom-call | tf_op jit(solution)/shard_map/forward/pallas_call | solution.py:214
  41.7 6.5 %backward.1 = bf16[2,384,320]{2,1,0:T(8,128)(2,1)} custom-call(s32[4]{0:T(128)S(1)} %pad_add_fusion.offsets, s32[2]{0:T(128)S(1)} %pad_add_fusion.1.halves, bf16[256,2048]{1,0:T(8,128)(2,1)S(1)} %bitcast.27, bf16[256,2048]{1,0:T(8,128)(2,1)} %collective-permute-done.5.cot_other, f32[2,2,256,640]{3,2,1,0:T(8,128)} %copy-done.1, ...), custom_call_target="tpu_custom_call" | custom-call | tf_op jit(solution)/shard_map/backward/pallas_call | solution.py:196
  48.2 5.7 %all-to-all-start.1 = ((bf16[32,24,320]{2,1,0:T(8,128)(2,1)}), bf16[32,24,320]{2,1,0:T(8,128)(2,1)}, u32[]{:S(2)}, u32[]{:S(2)}) async-start(bf16[32,24,320]{2,1,0:T(8,128)(2,1)} %bitcast.16), calls=%async_computation.1 | async-start | bytes 1179648 | tf_op jit(solution)/shard_map/all_to_all | solution.py:203
  54.1 3.1 %fusion = bf16[1,256,2048]{2,1,0:T(8,128)(2,1)} fusion(f32[256,2048]{1,0:T(8,128)} %get-tuple-element.10, bf16[256,2048]{1,0:T(8,128)(2,1)} %collective-permute-done.4, f32[2048]{0:T(1024)S(1)} %copy-done.8, pred[256]{0:T(512)(128)(4,1)S(1)} %fusion.2), kind=kLoop, calls=%fused_computation.2 | loop fusion | flops 2621440 | bytes 4202752 | tf_op jit(solution)/shard_map/broadcast_in_dim | solution.py:226
  57.2 14.0 %all-to-all-done.1 = bf16[32,24,320]{2,1,0:T(8,128)(2,1)} async-done(((bf16[32,24,320]{2,1,0:T(8,128)(2,1)}), bf16[32,24,320]{2,1,0:T(8,128)(2,1)}, u32[]{:S(2)}, u32[]{:S(2)}) %all-to-all-start.1) | async-done | bytes 491552 | tf_op jit(solution)/shard_map/all_to_all | solution.py:203
  71.3 1.2 %convert_reduce_fusion = f32[2,24,320]{2,1,0:T(8,128)S(1)} fusion(bf16[16,2,24,320]{3,2,1,0:T(8,128)(2,1)} %bitcast.20), kind=kLoop, calls=%fused_computation.1 | loop fusion | flops 476160 | bytes 552960 | tf_op jit(solution)/shard_map/reduce_sum | solution.py:211
  72.5 0.7 %reshape.69 = f32[3,8,640]{2,1,0:T(8,128)} reshape(f32[24,2,320]{2,1,0:T(2,128)S(1)} %copy.23) | data formatting | bytes 122880 | tf_op jit(solution)/shard_map/reshape | solution.py:212
  (35 shorter events, 1.0 us)
Async XLA Ops:
  0.6 10.3 %copy-start = (bf16[640,2048]{1,0:T(8,128)(2,1)S(1)}, bf16[640,2048]{1,0:T(8,128)(2,1)}, u32[]{:S(2)}) copy-start(bf16[640,2048]{1,0:T(8,128)(2,1)} %param.11) | copy-start | bytes 7864324
  0.6 1.0 %copy-start.6 = (bf16[1,256,128]{2,1,0:T(8,128)(2,1)S(1)}, bf16[1,256,128]{2,1,0:T(8,128)(2,1)}, u32[]{:S(2)}) copy-start(bf16[1,256,128]{2,1,0:T(8,128)(2,1)} %param.7) | copy-start | bytes 196612
  1.6 0.7 copy-start.7
  3.4 23.9 %all-to-all-start = ((bf16[16,16,640]{2,1,0:T(8,128)(2,1)}), bf16[16,16,640]{2,1,0:T(8,128)(2,1)}, u32[]{:S(2)}, u32[]{:S(2)}) async-start(bf16[16,16,640]{2,1,0:T(8,128)(2,1)} %bitcast.1), calls=%async_computation | async-start | bytes 655360 | tf_op jit(solution)/shard_map/all_to_all | solution.py:165
  10.9 6.6 %copy-start.9 = (f32[1280]{0:T(1024)S(1)}, f32[1280]{0:T(1024)}, u32[]{:S(2)}) copy-start(f32[1280]{0:T(1024)} %param.10) | copy-start | bytes 15364
  11.7 13.7 %collective-permute-start.1 = (bf16[112,2048]{1,0:T(8,128)(2,1)}, bf16[112,2048]{1,0:T(8,128)(2,1)}, u32[]{:S(2)}, u32[]{:S(2)}) collective-permute-start(bf16[112,2048]{1,0:T(8,128)(2,1)} %constant_dynamic-slice_fusion.1), channel_id=1, source_target_pairs={{0,16},{16,0},{1,17},{17,1},{2,18},{18,2},{3,19},{19,3},{4,20},{20... | collective-permute-start | bytes 1376264 | tf_op jit(solution)/shard_map/ppermute | solution.py:133
  14.0 20.2 %collective-permute-start.2 = (bf16[96,2048]{1,0:T(8,128)(2,1)}, bf16[96,2048]{1,0:T(8,128)(2,1)S(1)}, u32[]{:S(2)}, u32[]{:S(2)}) collective-permute-start(bf16[96,2048]{1,0:T(8,128)(2,1)} %constant_dynamic-slice_fusion), channel_id=1, source_target_pairs={{0,16},{16,0},{1,17},{17,1},{2,18},{18,2},{3,19},{19,3},{4,20},{20... | collective-permute-start | bytes 1179656 | tf_op jit(solution)/shard_map/ppermute | solution.py:133
  14.5 27.2 %collective-permute-start.5 = (bf16[256,2048]{1,0:T(8,128)(2,1)}, bf16[256,2048]{1,0:T(8,128)(2,1)}, u32[]{:S(2)}, u32[]{:S(2)}) collective-permute-start(bf16[256,2048]{1,0:T(8,128)(2,1)} %bitcast.26), channel_id=1, source_target_pairs={{0,1},{1,0},{2,3},{3,2},{4,5},{5,4},{6,7},{7,6},{8,9},{9,8},{10,11... | collective-permute-start | bytes 3145736 | tf_op jit(solution)/shard_map/ppermute | solution.py:136
  25.4 11.7 %collective-permute-start.3 = (bf16[112,2048]{1,0:T(8,128)(2,1)}, bf16[112,2048]{1,0:T(8,128)(2,1)}, u32[]{:S(2)}, u32[]{:S(2)}) collective-permute-start(bf16[112,2048]{1,0:T(8,128)(2,1)} %collective-permute-done.1.refs_1_), channel_id=1, source_target_pairs={{0,2},{1,3},{2,0},{3,1},{4,6},{5,7},{6,4},{7,5},{8,10},{9,11},{10,... | collective-permute-start | bytes 1376264 | tf_op jit(solution)/shard_map/ppermute | solution.py:136
  27.4 1.9 %copy-start.2 = (bf16[384,384]{1,0:T(8,128)(2,1)S(1)}, bf16[384,384]{1,0:T(8,128)(2,1)}, u32[]{:S(2)}) copy-start(bf16[384,384]{1,0:T(8,128)(2,1)} %fusion.1.order) | copy-start | bytes 884740
  27.4 1.9 %collective-permute-start = (bf16[256,640]{1,0:T(8,128)(2,1)}, bf16[256,640]{1,0:T(8,128)(2,1)S(1)}, u32[]{:S(2)}, u32[]{:S(2)}) collective-permute-start(bf16[256,640]{1,0:T(8,128)(2,1)} %bitcast.2.own), channel_id=1, source_target_pairs={{0,1},{1,0},{2,3},{3,2},{4,5},{5,4},{6,7},{7,6},{8,9},{9,8},{10,11... | collective-permute-start | bytes 983048 | tf_op jit(solution)/shard_map/ppermute | solution.py:136
  27.6 14.1 %copy-start.3 = (bf16[1,256,2048]{2,1,0:T(8,128)(2,1)S(1)}, bf16[1,256,2048]{2,1,0:T(8,128)(2,1)}, u32[]{:S(2)}) copy-start(bf16[1,256,2048]{2,1,0:T(8,128)(2,1)} %param.13) | copy-start | bytes 3145732
  32.7 1.5 %copy-start.1 = (f32[2,2,256,640]{3,2,1,0:T(8,128)}, f32[2,2,256,640]{3,2,1,0:T(8,128)S(1)}, u32[]{:S(2)}) copy-start(f32[2,2,256,640]{3,2,1,0:T(8,128)S(1)} %get-tuple-element.12.slope) | copy-start | bytes 7864324
  34.2 7.4 %copy-start.4 = (f32[256,128]{1,0:T(8,128)}, f32[256,128]{1,0:T(8,128)S(1)}, u32[]{:S(2)}) copy-start(f32[256,128]{1,0:T(8,128)S(1)} %get-tuple-element.8) | copy-start | bytes 393220
  41.6 12.4 %collective-permute-start.4 = (bf16[256,2048]{1,0:T(8,128)(2,1)}, bf16[256,2048]{1,0:T(8,128)(2,1)}, u32[]{:S(2)}, u32[]{:S(2)}) collective-permute-start(bf16[256,2048]{1,0:T(8,128)(2,1)} %get-tuple-element.11), channel_id=1, source_target_pairs={{0,1},{1,0},{2,3},{3,2},{4,5},{5,4},{6,7},{7,6},{8,9},{9,8},{10,11... | collective-permute-start | bytes 3145736 | tf_op jit(solution)/shard_map/ppermute | solution.py:136
  41.7 12.2 %copy-start.5 = (f32[256,128]{1,0:T(8,128)S(1)}, f32[256,128]{1,0:T(8,128)}, u32[]{:S(2)}) copy-start(f32[256,128]{1,0:T(8,128)} %copy-done.4) | copy-start | bytes 393220
  41.7 12.4 %copy-start.8 = (f32[2048]{0:T(1024)S(1)}, f32[2048]{0:T(1024)}, u32[]{:S(2)}) copy-start(f32[2048]{0:T(1024)} %param.12) | copy-start | bytes 24580
  48.2 23.0 %all-to-all-start.1 = ((bf16[32,24,320]{2,1,0:T(8,128)(2,1)}), bf16[32,24,320]{2,1,0:T(8,128)(2,1)}, u32[]{:S(2)}, u32[]{:S(2)}) async-start(bf16[32,24,320]{2,1,0:T(8,128)(2,1)} %bitcast.16), calls=%async_computation.1 | async-start | bytes 1179648 | tf_op jit(solution)/shard_map/all_to_all | solution.py:203

commit v3 on v2

v3 whole, which is shorter than its diff:
```python
import functools

import jax
import jax.numpy as jnp
from jax import lax
from jax.experimental import pallas as pl
from jax.experimental.pallas import tpu as pltpu
from jax.sharding import PartitionSpec as P

SQRT_HALF = 0.7071067811865476
INV_SQRT_TWO_PI = 0.3989422804014327
LANES = 128
VMEM_LIMIT = 16 * 1024 * 1024
HBM = pltpu.MemorySpace.HBM
F32, BF16, I32 = jnp.float32, jnp.bfloat16, jnp.int32


def iota(shape, dim):
    return lax.broadcasted_iota(I32, shape, dim)


def mm(a, b):
    return jnp.dot(a, b, preferred_element_type=F32)


def call(kernel, out_shape, name, micros=1, **kwargs):
    cost = pl.CostEstimate(flops=micros * 10**9, bytes_accessed=0, transcendentals=0)
    return pl.pallas_call(
        kernel,
        out_shape=out_shape,
        compiler_params=pltpu.CompilerParams(vmem_limit_bytes=VMEM_LIMIT),
        cost_estimate=cost,
        name=name,
        **kwargs,
    )


def in_hbm(x):
    return pltpu.with_memory_space_constraint(x, HBM)


def fetch(copies):
    for copy in copies:
        copy.start()


def settle(copies):
    for copy in copies:
        copy.wait()


def pack_kernel(owners, capacity, rows_own, mel_hbm, spots_hbm, out, mel_ref, spots_ref, sems):
    loads = [
        pltpu.make_async_copy(spots_hbm, spots_ref, sems.at[0]),
        pltpu.make_async_copy(mel_hbm, mel_ref, sems.at[1]),
    ]
    fetch(loads)
    slots = owners * capacity
    frames, mel = mel_ref.shape
    toks = frames // 2
    settle(loads)
    spots = spots_ref[...]
    owner = spots // rows_own
    row = spots - owner * rows_own
    before = (iota((toks, toks), 0) < iota((toks, toks), 1)).astype(F32).astype(BF16)
    mine = (iota((owners, toks), 0) == owner).astype(F32)
    ahead = mm(mine.astype(BF16), before)
    rank = jnp.sum(mine * ahead, axis=0, keepdims=True).astype(I32)
    onehot = (iota((slots, toks), 0) == owner * capacity + rank).astype(F32)
    spot = jnp.sum(onehot * (row - rows_own).astype(F32), axis=1, keepdims=True) + rows_own
    onehot = onehot.astype(BF16)
    window = mel_ref[...]
    for k in range(4):
        pick = (iota((toks, frames), 1) == 2 * iota((toks, frames), 0) - 1 + k).astype(F32)
        part = mm(pick.astype(BF16), window).astype(BF16)
        out[:, k * mel : (k + 1) * mel] = mm(onehot, part).astype(BF16)
    out[:, 4 * mel :] = jnp.broadcast_to(spot, (slots, LANES)).astype(BF16)


def rows_from_slots(arrived, rows):
    width = arrived.shape[1] - LANES
    spots = jnp.transpose(arrived[:, width:].astype(F32))[0:1, :].astype(I32)
    onehot = (iota((rows, spots.shape[1]), 0) == spots).astype(F32)
    return mm(onehot.astype(BF16), arrived[:, :width]).astype(BF16), onehot


LAST = (((1,), (1,)), ((), ()))


def ordered(frames, taps, share):
    depth = frames.shape[1]
    mel = depth // taps
    row = iota((depth, 1), 0).astype(F32)
    block = jnp.floor((row + 0.5) / (taps * share))
    within = row - block * (taps * share)
    tap = jnp.floor((within + 0.5) / share)
    source = (tap * mel + block * share + within - tap * share).astype(I32)
    order = (iota((depth, depth), 1) == source).astype(F32).astype(BF16)
    return lax.dot_general(order, frames, LAST, preferred_element_type=F32).astype(BF16)


def activations(frames, kernel, bias, rows):
    acts = mm(frames, kernel) + bias
    pool, slopes = None, []
    for p in range(2):
        x = acts[p * rows : (p + 1) * rows]
        cdf = 0.5 * (1.0 + lax.erf(x * SQRT_HALF))
        act = x * cdf
        pool = act if pool is None else pool + act
        slopes.append(0.5 * (cdf + x * INV_SQRT_TWO_PI * jnp.exp(-0.5 * x * x)))
    return (0.5 * pool).astype(BF16), slopes


def both_frames(patch, depth):
    mel = patch.shape[1] // 4
    return jnp.concatenate([patch[:, p * mel : p * mel + depth] for p in range(2)], axis=0)


def prepare_kernel(share, base, offsets, arrived, kernel, bias, own_in, other_in, weight_in, *refs):
    heads, (cots, whole, left, slopes, pooled, valid, sems) = refs[:-7], refs[-7:]
    rows = pooled.shape[0]
    depth = kernel.shape[0]
    quarter = whole.shape[0] // (len(heads) + 1)
    start = pl.multiple_of(base[0], 16)
    loads = [
        pltpu.make_async_copy(own_in, cots.at[pl.ds(0, rows)], sems.at[0]),
        pltpu.make_async_copy(other_in, cots.at[pl.ds(rows, rows)], sems.at[1]),
        pltpu.make_async_copy(
            weight_in.at[pl.ds(start, quarter)], whole.at[pl.ds(0, quarter)], sems.at[2]
        ),
    ]
    fetch(loads)
    place(offsets, heads, whole)
    patch, onehot = rows_from_slots(arrived[...], rows)
    valid[...] = jnp.broadcast_to(jnp.sum(onehot, axis=1, keepdims=True), valid.shape)
    frames = both_frames(patch, depth)
    left[...] = ordered(frames, depth // (patch.shape[1] // 4), share)
    pooled[...], halves = activations(frames, kernel[...], bias[...], rows)
    for p in range(2):
        slopes[p] = halves[p]
    settle(loads)


def place(offsets, weights, whole):
    for n, ref in enumerate(weights):
        start = pl.multiple_of(offsets[n], 16)
        whole[pl.ds(start, ref.shape[0]), :] = ref[...]


def backward_kernel(share, offsets, halves, cots, whole_in, left, slopes, kernel, bias, arrived, *refs):
    weights, (sums_out, pooled_out, whole, sums, pooled, sems) = refs[:-6], refs[-6:]
    rows = pooled.shape[0]
    depth = kernel.shape[0]
    place(offsets, weights, whole)
    patch, _ = rows_from_slots(arrived[...], rows)
    frames = both_frames(patch, depth)
    other_left = ordered(frames, depth // (patch.shape[1] // 4), share)
    pooled[...], other_slopes = activations(frames, kernel[...], bias[...], rows)
    stores = [pltpu.make_async_copy(pooled, pooled_out, sems.at[0])]
    stores[0].start()
    grads = lax.dot_general(cots[...], whole[...], LAST, preferred_element_type=F32)
    grads = grads.astype(BF16).astype(F32)
    pres = [grads[:rows] * slopes[p] for p in range(2)]
    pres += [grads[rows:] * other_slopes[p] for p in range(2)]
    pres = jnp.concatenate([pre.astype(BF16) for pre in pres], axis=0)
    total = mm(jnp.concatenate([left[...], other_left], axis=1), pres)
    quarter = sums.shape[2]
    for j in range(sums.shape[0]):
        sums[j] = total[:, j * quarter : (j + 1) * quarter].astype(BF16)
        stores.append(pltpu.make_async_copy(sums.at[j], sums_out.at[halves[j]], sems.at[1 + j]))
        stores[-1].start()
    settle(stores)


def merge_kernel(bases, offsets, pooled, other, valid, bias, *refs):
    weights, out, whole, sems = refs[:-3], refs[-3], refs[-2], refs[-1]
    count = (len(weights) - 1) // 2
    quarter = whole.shape[1] // (count // 3 + 1)
    loads = []
    for n in range(2):
        start = pl.multiple_of(bases[n], 16)
        loads.append((weights[0].at[pl.ds(start, quarter)], whole.at[n, pl.ds(0, quarter)]))
        for i in range(count):
            ref = weights[1 + n * count + i]
            start = pl.multiple_of(offsets[i], 16)
            loads.append((ref, whole.at[n, pl.ds(start, ref.shape[0])]))
    loads = [
        pltpu.make_async_copy(source, target, sems.at[i]) for i, (source, target) in enumerate(loads)
    ]
    fetch(loads)
    settle(loads)
    total = mm(pooled[...], whole[0]) + mm(other[...], whole[1]) + bias[...]
    out[...] = jnp.where(valid[:, 0:1] > 0.0, total, 0.0).astype(BF16)


def sum_kernel(pieces, out):
    share = pieces.shape[2]
    for core in range(2):
        total = pieces[core].astype(F32)
        for n in range(core + 2, pieces.shape[0], 2):
            total = total + pieces[n].astype(F32)
        out[:, core * share : (core + 1) * share] = total


def body(mel_frames, positions, conv_weight, conv_bias, proj_weight, proj_bias, cotangent):
    recs, owners = lax.axis_size("dp"), lax.axis_size("seq")
    dp_index, seq_index = lax.axis_index("dp"), lax.axis_index("seq")
    core, side = seq_index % 2, (seq_index // 2) % 2
    frames, mel = mel_frames.shape[1:]
    toks = positions.shape[1]
    rows, feats = cotangent.shape[1:]
    capacity = rows // owners
    slots = owners * capacity
    taps = conv_weight.shape[1]
    depth = taps * mel
    chans = proj_weight.shape[0]
    quarter = chans // 2
    width = recs * quarter
    assert taps == 3 and toks == LANES == mel and frames == 2 * toks and rows <= 256

    def shift(x, by):
        return lax.ppermute(x, "dp", [(i, (i + by) % recs) for i in range(recs)])

    def swap(x, bit):
        return lax.ppermute(x, "seq", [(i, i ^ bit) for i in range(owners)])

    end = quarter * 3 // 10 // 16 * 16
    middle = quarter - 2 * end
    base = core * quarter
    head = lax.dynamic_slice_in_dim(proj_weight, base + side * (end + middle), end, 0)
    heads = [shift(head, j) for j in range(1, recs)]
    tails = [swap(h, 2) for h in heads]
    weight_in, _ = lax.optimization_barrier((proj_weight, head))
    mid = lax.dynamic_slice_in_dim(weight_in, base + end, middle, 0)
    mids = [shift(mid, j) for j in range(1, recs)]
    from_here = [(j + 1) * quarter + side * (end + middle) for j in range(recs - 1)]
    from_next = [(j + 1) * quarter + (1 - side) * (end + middle) for j in range(recs - 1)]
    centre = [jnp.asarray((j + 1) * quarter + end, I32) for j in range(recs - 1)]
    early = jnp.stack(from_here).astype(I32)
    late = jnp.stack(centre + from_next).astype(I32)
    offsets = jnp.concatenate([early, late])
    base_in = base.reshape(1).astype(I32)
    bases = jnp.stack([base, (1 - core) * quarter]).astype(I32)
    halves = jnp.stack([(dp_index - j) % recs for j in range(recs)]).astype(I32)
    smem = pl.BlockSpec(memory_space=pltpu.SMEM)
    vmem = pl.BlockSpec(memory_space=pltpu.VMEM)
    hbm = pl.BlockSpec(memory_space=HBM)
    anywhere = pl.BlockSpec(memory_space=pl.ANY)

    cot_own = in_hbm(cotangent[0])
    cot_other = swap(cot_own, 1)

    mel_in, spots_in, _, _ = lax.optimization_barrier((mel_frames[0], positions, head, mid))
    mel_in, spots_in = in_hbm(mel_in), in_hbm(spots_in)
    packed = call(
        functools.partial(pack_kernel, owners, capacity, rows),
        HBM((slots, 4 * mel + LANES), BF16),
        "pack_patches",
        in_specs=[hbm, hbm],
        scratch_shapes=[
            pltpu.VMEM((frames, mel), BF16),
            pltpu.VMEM((1, toks), I32),
            pltpu.SemaphoreType.DMA((2,)),
        ],
    )(mel_in, spots_in)
    arrived = lax.all_to_all(
        packed.reshape(owners, capacity, -1), "seq", split_axis=0, concat_axis=0, tiled=True
    ).reshape(slots, -1)
    def mine(x):
        starts = [(halves[j] * 2 + core) * quarter for j in range(recs)]
        return jnp.concatenate(
            [lax.dynamic_slice_in_dim(x, at, quarter, 1) for at in starts], axis=1
        )

    conv_in, bias_in, _ = lax.optimization_barrier((conv_weight, conv_bias, heads))
    kernel = mine(jnp.transpose(conv_in, (1, 0, 2)).reshape(depth, -1))
    bias = mine(bias_in[None, :])
    share = mel // owners
    arrived, kernel, bias = lax.optimization_barrier((arrived, kernel, bias))
    arrived_other = swap(arrived, 1)
    late_weights = mids + tails

    cots, whole, left, slopes, pooled, valid = call(
        functools.partial(prepare_kernel, share),
        [
            pltpu.VMEM((2 * rows, feats), BF16),
            pltpu.VMEM((width, feats), BF16),
            pltpu.VMEM((depth, 2 * rows), BF16),
            pltpu.VMEM((2, rows, width), F32),
            pltpu.VMEM((rows, width), BF16),
            pltpu.VMEM((rows, LANES), F32),
        ],
        "prepare",
        in_specs=[smem, smem] + [vmem] * 3 + [anywhere] * 3 + [vmem] * len(heads),
        out_specs=[vmem] * 6,
        scratch_shapes=[pltpu.SemaphoreType.DMA((3,))],
    )(base_in, early, arrived, kernel, bias, cot_own, cot_other, in_hbm(proj_weight), *heads)

    sums, pooled_other, _ = call(
        functools.partial(backward_kernel, share),
        [
            HBM((recs, depth, quarter), BF16),
            HBM((rows, width), BF16),
            pltpu.VMEM((width, feats), BF16),
        ],
        "backward",
        in_specs=[smem, smem] + [vmem] * (7 + len(late_weights)),
        out_specs=[hbm, hbm, vmem],
        input_output_aliases={3: 2},
        scratch_shapes=[
            pltpu.VMEM((recs, depth, quarter), BF16),
            pltpu.VMEM((rows, width), BF16),
            pltpu.SemaphoreType.DMA((1 + recs,)),
        ],
    )(late, halves, cots, whole, left, slopes, kernel, bias, arrived_other, *late_weights)
    pieces = lax.all_to_all(
        sums.reshape(recs * owners, taps * share, quarter),
        ("dp", "seq"),
        split_axis=0,
        concat_axis=0,
        tiled=True,
    )
    foreign = heads + late_weights
    merged = call(
        merge_kernel,
        HBM((rows, feats), BF16),
        "merge",
        in_specs=[smem, smem] + [vmem] * 4 + [anywhere] * (1 + 2 * len(foreign)),
        scratch_shapes=[
            pltpu.VMEM((2, width, feats), BF16),
            pltpu.SemaphoreType.DMA((2 + 2 * len(foreign),)),
        ],
    )(
        bases,
        offsets,
        pooled,
        swap(pooled_other, 1),
        valid,
        proj_bias[None, :],
        in_hbm(proj_weight),
        *foreign,
        *[swap(w, 1) for w in foreign],
    )
    pieces, merged = lax.optimization_barrier((pieces, merged))
    grad_weight = call(
        sum_kernel,
        jax.ShapeDtypeStruct((taps * share, chans), F32),
        "sum_pieces",
    )(pieces)
    grad_weight = jnp.transpose(grad_weight.reshape(taps, share, chans), (1, 0, 2))
    return merged[None], grad_weight


def solution(mesh):
    in_specs = (
        P("dp", "seq", None),
        P("dp", "seq"),
        P(),
        P(),
        P("dp", None),
        P(),
        P("dp", "seq", None),
    )
    out_specs = (P("dp", "seq", None), P("seq", None, "dp"))
    return jax.shard_map(body, mesh=mesh, in_specs=in_specs, out_specs=out_specs, check_vma=False)
```

time: 73.7 us -> 57.8 us (0.78)
  waiting for transfers between devices: 22.8 us -> 16.6 us
  other arithmetic: 5.61 us -> 0.46 us
  local copies, waits for them, and re-layouts: 11.2 us -> 6.37 us
    all_to_all x1, waiting for transfers between devices: 14 us -> 6.87 us  [body(): lax.all_to_all(sums.reshape(recs * owners, taps * share, quarter), ('dp',...]
    all_to_all x1, waiting for transfers between devices: 0.01 us -> 6.96 us  [body(): lax.all_to_all(packed.reshape(owners, capacity, -1), 'seq', split_axis=0,...]
    ppermute x2, waiting for transfers between devices: 4.32 us -> 0.01 us  [shift(): return lax.ppermute(x, 'dp', [(i, (i + by) % recs) for i in range(recs)])]
    broadcast_in_dim x1 -> x0, other arithmetic: 3.15 us -> none  [body(): return (merged[None], jnp.transpose(grad_weight, (1, 0, 2)))]
    another operation x2 -> x1, local copies, waits for them, and re-layouts: 2.98 us -> 0.08 us  [mine(): x = x.reshape(x.shape[0], recs, 2, quarter)]
    ppermute x4 -> x7, waiting for transfers between devices: 4.5 us -> 2.77 us  [swap(): return lax.ppermute(x, 'seq', [(i, i ^ bit) for i in range(owners)])]
    ppermute x2, starting transfers between devices: 2.04 us -> 3.6 us  [shift(): return lax.ppermute(x, 'dp', [(i, (i + by) % recs) for i in range(recs)])]
    all_to_all x1, starting transfers between devices: 5.69 us -> 4.17 us  [body(): lax.all_to_all(sums.reshape(recs * owners, taps * share, quarter), ('dp',...]
  transfers between devices with their start and end apart: 8 -> 11, of which waited for: 4 -> 6; matrix products, arithmetic and copies ran while one was open for 16% -> 7% of each run, Pallas kernels for 20% -> 18%
where the time goes in v3:
time: 57.8 us; the launch traced here: 57.2 us
  starting transfers between devices  16.9 us (29%)
  waiting for transfers between devices  16.6 us (29%)
  Pallas kernels  16.2 us (28%)
  local copies, waits for them, and re-layouts  6.37 us (11%)
  between operations  0.77 us (1%)
    all_to_all x1, waiting for transfers between devices, body(): lax.all_to_all(packed.reshape(owners, capacity, -1), 'seq', split_axis=0,...  6.96 us
    all_to_all x1, waiting for transfers between devices, body(): lax.all_to_all(sums.reshape(recs * owners, taps * share, quarter), ('dp',...  6.87 us
    all_to_all x1, starting transfers between devices, body(): lax.all_to_all(packed.reshape(owners, capacity, -1), 'seq', split_axis=0,...  6.03 us
    pallas_call x1, Pallas kernels, body(): call(merge_kernel, HBM((rows, feats), BF16), 'merge', in_specs=[smem, sme...  5.65 us
    pallas_call x1, Pallas kernels, body(): call(functools.partial(backward_kernel, share), [HBM((recs, depth, quarte...  5.18 us
    all_to_all x1, starting transfers between devices, body(): lax.all_to_all(sums.reshape(recs * owners, taps * share, quarter), ('dp',...  4.17 us
    ppermute x2, starting transfers between devices, shift(): return lax.ppermute(x, 'dp', [(i, (i + by) % recs) for i in range(recs)])  3.6 us
    ppermute x7, starting transfers between devices, swap(): return lax.ppermute(x, 'seq', [(i, i ^ bit) for i in range(owners)])  3.05 us
  transfers between devices with their start and end apart: 11, of which 6 were waited for; matrix products, arithmetic and copies ran while one was open for 7% of the time, Pallas kernels for 18%

profile of v3, /device:TPU:0, one launch (start us, length us, event | category | flops | bytes accessed | tf_op | source)
XLA Modules:
  0.0 57.2 jit_solution(2516114922603482283)
XLA Ops:
  0.7 1.0 %constant_dynamic-slice_fusion.3 = bf16[96,2048]{1,0:T(8,128)(2,1)S(1)} fusion(bf16[640,2048]{1,0:T(8,128)(2,1)} %refs_0_.1, s32[]{:T(128)S(6)} %select_n.42), kind=kLoop, calls=%fused_computation.5 | loop fusion | bytes 786436 | tf_op jit(solution)/shard_map/dynamic_slice | solution.py:230
  1.7 3.0 %collective-permute-start = (bf16[96,2048]{1,0:T(8,128)(2,1)S(1)}, bf16[96,2048]{1,0:T(8,128)(2,1)S(1)}, u32[]{:S(2)}, u32[]{:S(2)}) collective-permute-start(bf16[96,2048]{1,0:T(8,128)(2,1)S(1)} %constant_dynamic-slice_fusion.3), channel_id=1, source_target_pairs={{0,16},{16,0},{1,17},{17,1},{2,18},{18,2},{3,19},{19,3},{4,20},{20... | collective-permute-start | bytes 1179656 | tf_op jit(solution)/shard_map/ppermute | solution.py:222
  4.7 1.9 %constant_dynamic-slice_fusion.2 = bf16[128,2048]{1,0:T(8,128)(2,1)} fusion(bf16[640,2048]{1,0:T(8,128)(2,1)} %refs_0_.1, s32[]{:T(128)S(6)} %select_n.43), kind=kLoop, calls=%fused_computation.4 | loop fusion | bytes 1048580 | tf_op jit(solution)/shard_map/dynamic_slice | solution.py:234
  6.6 2.0 %pack_patches.1 = bf16[256,640]{1,0:T(8,128)(2,1)} custom-call(bf16[256,128]{1,0:T(8,128)(2,1)} %bitcast.28, s32[1,128]{1,0:T(1,128)} %spots_hbm), custom_call_target="tpu_custom_call" | custom-call | flops 1000000000 | tf_op jit(solution)/shard_map/pack_patches/pallas_call | solution.py:255
  8.7 6.0 %all-to-all-start = ((bf16[16,16,640]{2,1,0:T(8,128)(2,1)}), bf16[16,16,640]{2,1,0:T(8,128)(2,1)S(1)}, u32[]{:S(2)}, u32[]{:S(2)}) async-start(bf16[16,16,640]{2,1,0:T(8,128)(2,1)} %bitcast.27), calls=%async_computation | async-start | bytes 655360 | tf_op jit(solution)/shard_map/all_to_all | solution.py:266
  14.7 0.6 collective-permute-start.3
  15.4 1.9 %collective-permute-start.4 = (bf16[96,2048]{1,0:T(8,128)(2,1)S(1)}, bf16[96,2048]{1,0:T(8,128)(2,1)S(1)}, u32[]{:S(2)}, u32[]{:S(2)}) collective-permute-start(bf16[96,2048]{1,0:T(8,128)(2,1)S(1)} %collective-permute-done.refs_0_.refs_1_), channel_id=1, source_target_pairs={{0,2},{1,3},{2,0},{3,1},{4,6},{5,7},{6,4},{7,5},{8,10},{9,11},{10,... | collective-permute-start | bytes 1179656 | tf_op jit(solution)/shard_map/ppermute | solution.py:225
  17.3 1.4 %constant_dynamic-slice_fusion.1 = (bf16[384,320]{1,0:T(8,128)(2,1)S(1)}, bf16[384,320]{1,0:T(8,128)(2,1)S(1)}) fusion(bf16[384,1280]{1,0:T(8,128)(2,1)} %bitcast.26, s32[]{:T(128)S(6)} %select_n.44, s32[]{:T(128)S(6)} %select_n.45), kind=kLoop, calls=%fused_computation.3 | loop fusion | bytes 983048 | tf_op jit(solution)/shard_map/dynamic_slice | solution.py:272
  18.9 7.0 %all-to-all-done = bf16[16,16,640]{2,1,0:T(8,128)(2,1)S(1)} async-done(((bf16[16,16,640]{2,1,0:T(8,128)(2,1)}), bf16[16,16,640]{2,1,0:T(8,128)(2,1)S(1)}, u32[]{:S(2)}, u32[]{:S(2)}) %all-to-all-start) | async-done | bytes 327712 | tf_op jit(solution)/shard_map/all_to_all | solution.py:266
  26.0 1.0 %copy-done.3 = bf16[256,2048]{1,0:T(8,128)(2,1)} copy-done((bf16[256,2048]{1,0:T(8,128)(2,1)}, bf16[256,2048]{1,0:T(8,128)(2,1)S(1)}, u32[]{:S(2)}) %copy-start.3) | copy-done | bytes 1048600
  27.0 2.6 %prepare.1 = (bf16[512,2048]{1,0:T(8,128)(2,1)S(1)}, bf16[640,2048]{1,0:T(8,128)(2,1)S(1)}, bf16[384,512]{1,0:T(8,128)(2,1)S(1)}, f32[2,256,640]{2,1,0:T(8,128)S...) custom-call(s32[1]{0:T(128)} %bitcast.3.base, s32[1]{0:T(128)} %bitcast.4.offsets, ...), custom_call_target="tpu_custom_call" | custom-call | flops 1000000000 | tf_op jit(solution)/shard_map/prepare/pallas_call | solution.py:283
  29.8 5.2 %backward.1 = (bf16[2,384,320]{2,1,0:T(8,128)(2,1)}, bf16[256,640]{1,0:T(8,128)(2,1)}, bf16[640,2048]{1,0:T(8,128)(2,1)S(1)}) custom-call(s32[2]{0:T(128)S(1)} %get-tuple-element.42.offsets, s32[2]{0:T(128)S(1)} %get-tuple-element.43.halves, bf16[512,2048]{1,0:T(8,128)(2,1)S(1)} %get-tuple-element.28.cots, ...), custom_call_target="tpu_custom_call", output_to_operand_aliasing={{2}: (3, {})} | custom-call | flops 1000000000 | tf_op jit(solution)/shard_map/backward/pallas_call | solution.py:299
  35.0 4.2 %all-to-all-start.1 = ((bf16[32,24,320]{2,1,0:T(8,128)(2,1)}), bf16[32,24,320]{2,1,0:T(8,128)(2,1)S(1)}, u32[]{:S(2)}, u32[]{:S(2)}) async-start(bf16[32,24,320]{2,1,0:T(8,128)(2,1)} %bitcast.25), calls=%async_computation.1 | async-start | bytes 1179648 | tf_op jit(solution)/shard_map/all_to_all | solution.py:316
  39.2 0.3 collective-permute-start.7
  39.5 0.3 collective-permute-start.6
  39.7 0.3 collective-permute-start.8
  40.0 0.3 collective-permute-start.5
  40.4 1.3 %collective-permute-done.6.refs_4_ = bf16[96,2048]{1,0:T(8,128)(2,1)S(1)} collective-permute-done((bf16[96,2048]{1,0:T(8,128)(2,1)S(1)}, bf16[96,2048]{1,0:T(8,128)(2,1)S(1)}, u32[]{:S(2)}, u32[]{:S(2)}) %collective-permute-start.6) | collective-permute-done | bytes 393248 | tf_op jit(solution)/shard_map/ppermute | solution.py:225
  41.7 1.0 %collective-permute-done.8.refs_6_ = bf16[96,2048]{1,0:T(8,128)(2,1)S(1)} collective-permute-done((bf16[96,2048]{1,0:T(8,128)(2,1)S(1)}, bf16[96,2048]{1,0:T(8,128)(2,1)S(1)}, u32[]{:S(2)}, u32[]{:S(2)}) %collective-permute-start.8) | collective-permute-done | bytes 393248 | tf_op jit(solution)/shard_map/ppermute | solution.py:225
  42.7 0.2 collective-permute-done.5.other
  43.0 1.0 %copy-done.1 = bf16[256,640]{1,0:T(8,128)(2,1)S(1)} copy-done((bf16[256,640]{1,0:T(8,128)(2,1)S(1)}, bf16[256,640]{1,0:T(8,128)(2,1)}, u32[]{:S(2)}) %copy-start.1) | copy-done | bytes 327704
  43.9 5.7 %merge.1 = bf16[256,2048]{1,0:T(8,128)(2,1)} custom-call(s32[2]{0:T(128)S(1)} %pad_add_fusion.2.bases, s32[3]{0:T(128)S(1)} %pad_add_fusion.3.offsets, bf16[256,640]{1,0:T(8,128)(2,1)S(1)} %copy-done.1, bf16[256,640]{1,0:T(8,128)(2,1)} %collective-permute-done.5.other, f32[256,128]{1,0:T(8,128)S(1)} %get-tuple-element.35.valid, f32[1,2048]{1,0:T(1,128)S(1)} %bitcast.21, ...), custom_call_target="tpu_custom_call" | custom-call | flops 1000000000 | tf_op jit(solution)/shard_map/merge/pallas_call | solution.py:324
  49.6 6.9 %all-to-all-done.1.pieces = bf16[32,24,320]{2,1,0:T(8,128)(2,1)S(1)} async-done(((bf16[32,24,320]{2,1,0:T(8,128)(2,1)}), bf16[32,24,320]{2,1,0:T(8,128)(2,1)S(1)}, u32[]{:S(2)}, u32[]{:S(2)}) %all-to-all-start.1) | async-done | bytes 491552 | tf_op jit(solution)/shard_map/all_to_all | solution.py:316
  56.5 0.7 %sum_pieces.1 = f32[24,640]{1,0:T(8,128)} custom-call(bf16[32,24,320]{2,1,0:T(8,128)(2,1)S(1)} %all-to-all-done.1.pieces), custom_call_target="tpu_custom_call" | custom-call | flops 1000000000 | tf_op jit(solution)/shard_map/sum_pieces/pallas_call | solution.py:345
  (24 shorter events, 0.8 us)
Async XLA Ops:
  1.7 13.6 %collective-permute-start = (bf16[96,2048]{1,0:T(8,128)(2,1)S(1)}, bf16[96,2048]{1,0:T(8,128)(2,1)S(1)}, u32[]{:S(2)}, u32[]{:S(2)}) collective-permute-start(bf16[96,2048]{1,0:T(8,128)(2,1)S(1)} %constant_dynamic-slice_fusion.3), channel_id=1, source_target_pairs={{0,16},{16,0},{1,17},{17,1},{2,18},{18,2},{3,19},{19,3},{4,20},{20... | collective-permute-start | bytes 1179656 | tf_op jit(solution)/shard_map/ppermute | solution.py:222
  4.7 21.3 %collective-permute-start.1 = (bf16[256,2048]{1,0:T(8,128)(2,1)}, bf16[256,2048]{1,0:T(8,128)(2,1)S(1)}, u32[]{:S(2)}, u32[]{:S(2)}) collective-permute-start(bf16[256,2048]{1,0:T(8,128)(2,1)} %bitcast.22), channel_id=1, source_target_pairs={{0,1},{1,0},{2,3},{3,2},{4,5},{5,4},{6,7},{7,6},{8,9},{9,8},{10,11... | collective-permute-start | bytes 3145736 | tf_op jit(solution)/shard_map/ppermute | solution.py:225
  4.7 10.6 %copy-start.4 = (f32[1280]{0:T(1024)S(1)}, f32[1280]{0:T(1024)}, u32[]{:S(2)}) copy-start(f32[1280]{0:T(1024)} %param.10) | copy-start | bytes 15364
  8.7 17.2 %all-to-all-start = ((bf16[16,16,640]{2,1,0:T(8,128)(2,1)}), bf16[16,16,640]{2,1,0:T(8,128)(2,1)S(1)}, u32[]{:S(2)}, u32[]{:S(2)}) async-start(bf16[16,16,640]{2,1,0:T(8,128)(2,1)} %bitcast.27), calls=%async_computation | async-start | bytes 655360 | tf_op jit(solution)/shard_map/all_to_all | solution.py:266
  14.7 14.9 %collective-permute-start.3 = (bf16[128,2048]{1,0:T(8,128)(2,1)}, bf16[128,2048]{1,0:T(8,128)(2,1)S(1)}, u32[]{:S(2)}, u32[]{:S(2)}) collective-permute-start(bf16[128,2048]{1,0:T(8,128)(2,1)} %constant_dynamic-slice_fusion.2), channel_id=1, source_target_pairs={{0,16},{16,0},{1,17},{17,1},{2,18},{18,2},{3,19},{19,3},{4,20},{20... | collective-permute-start | bytes 1572872 | tf_op jit(solution)/shard_map/ppermute | solution.py:222
  15.4 14.4 %collective-permute-start.4 = (bf16[96,2048]{1,0:T(8,128)(2,1)S(1)}, bf16[96,2048]{1,0:T(8,128)(2,1)S(1)}, u32[]{:S(2)}, u32[]{:S(2)}) collective-permute-start(bf16[96,2048]{1,0:T(8,128)(2,1)S(1)} %collective-permute-done.refs_0_.refs_1_), channel_id=1, source_target_pairs={{0,2},{1,3},{2,0},{3,1},{4,6},{5,7},{6,4},{7,5},{8,10},{9,11},{10,... | collective-permute-start | bytes 1179656 | tf_op jit(solution)/shard_map/ppermute | solution.py:225
  25.8 3.9 %collective-permute-start.2 = (bf16[256,640]{1,0:T(8,128)(2,1)S(1)}, bf16[256,640]{1,0:T(8,128)(2,1)S(1)}, u32[]{:S(2)}, u32[]{:S(2)}) collective-permute-start(bf16[256,640]{1,0:T(8,128)(2,1)S(1)} %bitcast.19), channel_id=1, source_target_pairs={{0,1},{1,0},{2,3},{3,2},{4,5},{5,4},{6,7},{7,6},{8,9},{9,8},{10,11... | collective-permute-start | bytes 983048 | tf_op jit(solution)/shard_map/ppermute | solution.py:225
  26.0 1.0 %copy-start.3 = (bf16[256,2048]{1,0:T(8,128)(2,1)}, bf16[256,2048]{1,0:T(8,128)(2,1)S(1)}, u32[]{:S(2)}) copy-start(bf16[256,2048]{1,0:T(8,128)(2,1)S(1)} %collective-permute-done.1.other_in) | copy-start | bytes 3145732
  29.6 5.4 %copy-start = (bf16[256,640]{1,0:T(8,128)(2,1)}, bf16[256,640]{1,0:T(8,128)(2,1)S(1)}, u32[]{:S(2)}) copy-start(bf16[256,640]{1,0:T(8,128)(2,1)S(1)} %get-tuple-element.33.pooled) | copy-start | bytes 983044
  29.8 13.2 %copy-start.2 = (f32[2048]{0:T(1024)S(1)}, f32[2048]{0:T(1024)}, u32[]{:S(2)}) copy-start(f32[2048]{0:T(1024)} %param.12) | copy-start | bytes 24580
  35.0 21.5 %all-to-all-start.1 = ((bf16[32,24,320]{2,1,0:T(8,128)(2,1)}), bf16[32,24,320]{2,1,0:T(8,128)(2,1)S(1)}, u32[]{:S(2)}, u32[]{:S(2)}) async-start(bf16[32,24,320]{2,1,0:T(8,128)(2,1)} %bitcast.25), calls=%async_computation.1 | async-start | bytes 1179648 | tf_op jit(solution)/shard_map/all_to_all | solution.py:316
  39.2 2.5 %collective-permute-start.7 = (bf16[128,2048]{1,0:T(8,128)(2,1)S(1)}, bf16[128,2048]{1,0:T(8,128)(2,1)S(1)}, u32[]{:S(2)}, u32[]{:S(2)}) collective-permute-start(bf16[128,2048]{1,0:T(8,128)(2,1)S(1)} %collective-permute-done.3.refs_0_.refs_2_), channel_id=1, source_target_pairs={{0,1},{1,0},{2,3},{3,2},{4,5},{5,4},{6,7},{7,6},{8,9},{9,8},{10,11... | collective-permute-start | bytes 1572872 | tf_op jit(solution)/shard_map/ppermute | solution.py:225
  39.5 2.2 %collective-permute-start.6 = (bf16[96,2048]{1,0:T(8,128)(2,1)S(1)}, bf16[96,2048]{1,0:T(8,128)(2,1)S(1)}, u32[]{:S(2)}, u32[]{:S(2)}) collective-permute-start(bf16[96,2048]{1,0:T(8,128)(2,1)S(1)} %collective-permute-done.refs_0_.refs_1_), channel_id=1, source_target_pairs={{0,1},{1,0},{2,3},{3,2},{4,5},{5,4},{6,7},{7,6},{8,9},{9,8},{10,11... | collective-permute-start | bytes 1179656 | tf_op jit(solution)/shard_map/ppermute | solution.py:225
  39.7 3.0 %collective-permute-start.8 = (bf16[96,2048]{1,0:T(8,128)(2,1)S(1)}, bf16[96,2048]{1,0:T(8,128)(2,1)S(1)}, u32[]{:S(2)}, u32[]{:S(2)}) collective-permute-start(bf16[96,2048]{1,0:T(8,128)(2,1)S(1)} %collective-permute-done.4.refs_1_.refs_3_), channel_id=1, source_target_pairs={{0,1},{1,0},{2,3},{3,2},{4,5},{5,4},{6,7},{7,6},{8,9},{9,8},{10,11... | collective-permute-start | bytes 1179656 | tf_op jit(solution)/shard_map/ppermute | solution.py:225
  40.0 3.0 %collective-permute-start.5 = (bf16[256,640]{1,0:T(8,128)(2,1)}, bf16[256,640]{1,0:T(8,128)(2,1)}, u32[]{:S(2)}, u32[]{:S(2)}) collective-permute-start(bf16[256,640]{1,0:T(8,128)(2,1)} %get-tuple-element.34), channel_id=1, source_target_pairs={{0,1},{1,0},{2,3},{3,2},{4,5},{5,4},{6,7},{7,6},{8,9},{9,8},{10,11... | collective-permute-start | bytes 983048 | tf_op jit(solution)/shard_map/ppermute | solution.py:225
  43.0 1.0 %copy-start.1 = (bf16[256,640]{1,0:T(8,128)(2,1)S(1)}, bf16[256,640]{1,0:T(8,128)(2,1)}, u32[]{:S(2)}) copy-start(bf16[256,640]{1,0:T(8,128)(2,1)} %copy-done) | copy-start | bytes 983044

commit v4 on v3

v4 whole, which is shorter than its diff:
```python
import functools

import jax
import jax.numpy as jnp
from jax import lax
from jax.experimental import pallas as pl
from jax.experimental.pallas import tpu as pltpu
from jax.sharding import PartitionSpec as P

SQRT_HALF = 0.7071067811865476
INV_SQRT_TWO_PI = 0.3989422804014327
LANES = 128
VMEM_LIMIT = 16 * 1024 * 1024
HBM = pltpu.MemorySpace.HBM
F32, BF16, I32 = jnp.float32, jnp.bfloat16, jnp.int32


def iota(shape, dim):
    return lax.broadcasted_iota(I32, shape, dim)


def mm(a, b):
    return jnp.dot(a, b, preferred_element_type=F32)


def call(kernel, out_shape, name, micros=1, **kwargs):
    cost = pl.CostEstimate(flops=micros * 10**9, bytes_accessed=0, transcendentals=0)
    return pl.pallas_call(
        kernel,
        out_shape=out_shape,
        compiler_params=pltpu.CompilerParams(vmem_limit_bytes=VMEM_LIMIT),
        cost_estimate=cost,
        name=name,
        **kwargs,
    )


def in_hbm(x):
    return pltpu.with_memory_space_constraint(x, HBM)


def fetch(copies):
    for copy in copies:
        copy.start()


def settle(copies):
    for copy in copies:
        copy.wait()


def pack_kernel(owners, capacity, rows_own, cuts, mel_hbm, spots_hbm, weight, out, head, far, mel_ref, spots_ref, sems):
    loads = [
        pltpu.make_async_copy(spots_hbm, spots_ref, sems.at[0]),
        pltpu.make_async_copy(mel_hbm, mel_ref, sems.at[1]),
    ]
    fetch(loads)
    unit = head.shape[0]
    rows = []
    targets = [head, far.at[pl.ds(0, unit)]]
    if far.shape[0] > unit:
        targets.append(far.at[pl.ds(unit, far.shape[0] - unit)])
    for n, ref in enumerate(targets):
        start = pl.multiple_of(cuts[n], 16)
        rows.append(
            pltpu.make_async_copy(weight.at[pl.ds(start, ref.shape[0])], ref, sems.at[2 + n])
        )
    fetch(rows)
    high = min(capacity, 8)
    slots = owners * high
    frames, mel = mel_ref.shape
    toks = frames // 2
    before = (iota((toks, toks), 0) < iota((toks, toks), 1)).astype(F32).astype(BF16)
    lane = iota((slots, LANES), 1)
    picks = [
        (iota((toks, frames), 1) == 2 * iota((toks, frames), 0) - 1 + k).astype(F32).astype(BF16)
        for k in range(4)
    ]
    settle(loads)
    spots = spots_ref[...]
    owner = spots // rows_own
    row = (spots - owner * rows_own - rows_own).astype(F32)
    mine = (iota((owners, toks), 0) == owner).astype(F32)
    ahead = mm(mine.astype(BF16), before)
    rank = jnp.sum(mine * ahead, axis=0, keepdims=True).astype(I32)
    window = mel_ref[...]
    patch = jnp.concatenate([mm(pick, window).astype(BF16) for pick in picks], axis=1)
    places = jnp.zeros((slots, LANES), F32)
    width = 4 * mel
    for g in range(capacity // high):
        within = rank - g * high
        target = jnp.where((within >= 0) & (within < high), owner * high + within, -1)
        onehot = (iota((slots, toks), 0) == target).astype(F32)
        spot = jnp.sum(onehot * row, axis=1, keepdims=True) + rows_own
        places = jnp.where(lane == g, spot, places)
        out[:, g * width : (g + 1) * width] = mm(onehot.astype(BF16), patch).astype(BF16)
    out[:, capacity // high * width :] = places.astype(BF16)
    settle(rows)


def rows_from_slots(arrived, rows, mel):
    width = 4 * mel
    groups = arrived.shape[1] // width
    places = jnp.transpose(arrived[:, groups * width :].astype(F32)).astype(I32)
    patch, valid = None, None
    for g in range(groups):
        onehot = (iota((rows, places.shape[1]), 0) == places[g : g + 1, :]).astype(F32)
        part = mm(onehot.astype(BF16), arrived[:, g * width : (g + 1) * width])
        patch = part if patch is None else patch + part
        valid = onehot if valid is None else valid + onehot
    return patch.astype(BF16), valid


LAST = (((1,), (1,)), ((), ()))


def ordered(frames, taps, share):
    depth = frames.shape[1]
    mel = depth // taps
    row = iota((depth, 1), 0).astype(F32)
    block = jnp.floor((row + 0.5) / (taps * share))
    within = row - block * (taps * share)
    tap = jnp.floor((within + 0.5) / share)
    source = (tap * mel + block * share + within - tap * share).astype(I32)
    order = (iota((depth, depth), 1) == source).astype(F32).astype(BF16)
    return lax.dot_general(order, frames, LAST, preferred_element_type=F32).astype(BF16)


def activations(frames, kernel, bias, rows):
    acts = mm(frames, kernel) + bias
    pool, slopes = None, []
    for p in range(2):
        x = acts[p * rows : (p + 1) * rows]
        cdf = 0.5 * (1.0 + lax.erf(x * SQRT_HALF))
        act = x * cdf
        pool = act if pool is None else pool + act
        slopes.append(0.5 * (cdf + x * INV_SQRT_TWO_PI * jnp.exp(-0.5 * x * x)))
    return (0.5 * pool).astype(BF16), slopes


def both_frames(patch, depth):
    mel = patch.shape[1] // 4
    return jnp.concatenate([patch[:, p * mel : p * mel + depth] for p in range(2)], axis=0)


def activate(share, arrived, kernel, bias, left, slopes):
    rows = slopes.shape[1]
    depth = kernel.shape[0]
    patch, found = rows_from_slots(arrived[...], rows, LANES)
    frames = both_frames(patch, depth)
    left[...] = ordered(frames, depth // LANES, share)
    pooled, halves = activations(frames, kernel[...], bias[...], rows)
    for p in range(2):
        slopes[p] = halves[p]
    return pooled, found


def prepare_kernel(share, base, offsets, arrived, kernel, bias, own_in, other_in, weight_in, *refs):
    count = offsets.shape[0]
    heads, refs = refs[:count], refs[count:]
    cots, whole, left, slopes, pooled, valid, *ahead, sems = refs
    rows = pooled.shape[0]
    quarter = whole.shape[0] // (len(heads) + 1)
    start = pl.multiple_of(base[0], 16)
    loads = [
        pltpu.make_async_copy(own_in, cots.at[pl.ds(0, rows)], sems.at[0]),
        pltpu.make_async_copy(
            weight_in.at[pl.ds(start, quarter)], whole.at[pl.ds(0, quarter)], sems.at[1]
        ),
    ]
    fetch(loads)
    place(offsets, heads, whole, len(heads))
    cots[rows:, :] = other_in[...]
    pooled[...], found = activate(share, arrived, kernel, bias, left, slopes)
    valid[...] = jnp.broadcast_to(jnp.sum(found, axis=1, keepdims=True), valid.shape)
    settle(loads)
    if not ahead:
        return
    own_early, other_early = ahead
    early = own_early.shape[1]
    grads = lax.dot_general(cots[...], whole[0:early, :], LAST, preferred_element_type=F32)
    grads = grads.astype(BF16)
    other_early[...] = grads[rows:]
    own_early[...] = mm(left[...], sloped(grads[:rows].astype(F32), slopes[:, :, 0:early]))


def segments(offsets, weights, whole, groups):
    quarter = whole.shape[0] // (groups + 1)
    unit = min(ref.shape[0] for ref in weights)
    out = []
    for n, ref in enumerate(weights):
        start = pl.multiple_of(offsets[n], 16)
        out.append((ref.at[pl.ds(0, unit)], whole.at[pl.ds(start, unit)]))
        if (more := ref.shape[0] - unit) > 0:
            end = (n % groups + 2) * quarter
            out.append((ref.at[pl.ds(unit, more)], whole.at[pl.ds(end - more, more)]))
    return out


def sloped(grads, slopes):
    return jnp.concatenate([(grads * slopes[p]).astype(BF16) for p in range(2)], axis=0)


def place(offsets, weights, whole, groups):
    for source, target in segments(offsets, weights, whole, groups):
        target[...] = source[...]


def backward_kernel(share, early, offsets, halves, cots, whole_in, left, slopes, kernel, bias, arrived, *refs):
    ahead, refs = (refs[:2], refs[2:]) if early else ((), refs)
    weights, refs = refs[:-8], refs[-8:]
    sums_out, pooled_out, whole, sums, pooled, other_left, other_slopes, sems = refs
    rows = cots.shape[0] // 2
    place(offsets, weights, whole, len(weights) // 3)
    pooled[...], _ = activate(share, arrived, kernel, bias, other_left, other_slopes)
    stores = [pltpu.make_async_copy(pooled, pooled_out, sems.at[0])]
    stores[0].start()
    weight = whole[early:, :]
    grads = lax.dot_general(cots[:rows, :], weight, LAST, preferred_element_type=F32)
    grads = grads.astype(BF16).astype(F32)
    own = mm(left[...], sloped(grads, slopes[:, :, early:]))
    grads = lax.dot_general(cots[rows:, :], weight, LAST, preferred_element_type=F32).astype(BF16)
    if ahead:
        own = jnp.concatenate([ahead[0][...], own], axis=1)
        grads = jnp.concatenate([ahead[1][...], grads], axis=1)
    total = own + mm(other_left[...], sloped(grads.astype(F32), other_slopes[...]))
    quarter = total.shape[1] // sums.shape[0]
    for j in range(sums.shape[0]):
        group = total[:, j * quarter : (j + 1) * quarter]
        if sums.shape[-1] > quarter:
            group = group.reshape(sums.shape[1], -1, share, quarter)
            group = jnp.concatenate([group[:, k] for k in range(group.shape[1])], axis=2)
        sums[j] = group.astype(BF16)
        stores.append(pltpu.make_async_copy(sums.at[j], sums_out.at[halves[j]], sems.at[1 + j]))
        stores[-1].start()
    settle(stores)


def merge_kernel(quarter, bases, offsets, pooled, other, valid, bias, *refs):
    weights, out, whole, sems = refs[:-3], refs[-3], refs[-2], refs[-1]
    count = (len(weights) - 1) // 2
    loads = []
    for n in range(2):
        start = pl.multiple_of(bases[n], 16)
        loads.append((weights[0].at[pl.ds(start, quarter)], whole.at[n, pl.ds(0, quarter)]))
        foreign = weights[1 + n * count : 1 + (n + 1) * count]
        loads += segments(offsets, foreign, whole.at[n], count // 4)
    loads = [
        pltpu.make_async_copy(source, target, sems.at[i]) for i, (source, target) in enumerate(loads)
    ]
    fetch(loads)
    settle(loads)
    total = mm(pooled[...], whole[0]) + mm(other[...], whole[1]) + bias[...]
    out[...] = jnp.where(valid[:, 0:1] > 0.0, total, 0.0).astype(BF16)


def sum_kernel(quarter, pieces, out):
    for core in range(2):
        total = pieces[core].astype(F32)
        for n in range(core + 2, pieces.shape[0], 2):
            total = total + pieces[n].astype(F32)
        height = total.shape[0]
        for k in range(total.shape[1] // quarter):
            out[k * height : (k + 1) * height, core * quarter : (core + 1) * quarter] = total[
                :, k * quarter : (k + 1) * quarter
            ]


def body(mel_frames, positions, conv_weight, conv_bias, proj_weight, proj_bias, cotangent):
    recs, owners = lax.axis_size("dp"), lax.axis_size("seq")
    dp_index, seq_index = lax.axis_index("dp"), lax.axis_index("seq")
    core, side = seq_index % 2, (seq_index // 2) % 2
    frames, mel = mel_frames.shape[1:]
    toks = positions.shape[1]
    rows, feats = cotangent.shape[1:]
    capacity = rows // owners
    taps = conv_weight.shape[1]
    depth = taps * mel
    chans = proj_weight.shape[0]
    quarter = chans // 2
    width = recs * quarter
    assert taps == 3 and toks == LANES == mel and frames == 2 * toks and rows <= 256

    def shift(x, by):
        return lax.ppermute(x, "dp", [(i, (i + by) % recs) for i in range(recs)])

    def swap(x, bit):
        return lax.ppermute(x, "seq", [(i, i ^ bit) for i in range(owners)])

    bit = (seq_index // 4) % 2
    unit = quarter // 64 * 16
    base = core * quarter
    part = (bit * 2 + side) * unit
    part_x = (bit * 2 + 1 - side) * unit
    part_z = ((1 - bit) * 2 + side) * unit
    part_far = ((1 - bit) * 2 + 1 - side) * unit
    cuts = jnp.stack([base + part, base + part_far, base + 4 * unit]).astype(I32)
    early = jnp.stack([(j + 1) * quarter + part for j in range(recs - 1)]).astype(I32)
    late = [(j + 1) * quarter + p for p in (part_x, part_z, part_far) for j in range(recs - 1)]
    late = jnp.stack(late).astype(I32)
    offsets = jnp.concatenate([early, late])
    base_in = base.reshape(1).astype(I32)
    bases = jnp.stack([base, (1 - core) * quarter]).astype(I32)
    halves = jnp.stack([(dp_index - j) % recs for j in range(recs)]).astype(I32)
    smem = pl.BlockSpec(memory_space=pltpu.SMEM)
    vmem = pl.BlockSpec(memory_space=pltpu.VMEM)
    hbm = pl.BlockSpec(memory_space=HBM)
    anywhere = pl.BlockSpec(memory_space=pl.ANY)

    high = min(capacity, 8)
    slots = owners * high
    wide_slots = capacity // high * 4 * mel + LANES
    packed, head, far = call(
        functools.partial(pack_kernel, owners, capacity, rows),
        [
            HBM((slots, wide_slots), BF16),
            pltpu.VMEM((unit, feats), BF16),
            pltpu.VMEM((quarter - 3 * unit, feats), BF16),
        ],
        "pack_patches",
        in_specs=[smem, hbm, hbm, hbm],
        out_specs=[vmem] * 3,
        scratch_shapes=[
            pltpu.VMEM((frames, mel), BF16),
            pltpu.VMEM((1, toks), I32),
            pltpu.SemaphoreType.DMA((5,)),
        ],
    )(cuts, in_hbm(mel_frames[0]), in_hbm(positions), in_hbm(proj_weight))
    heads = [shift(head, j) for j in range(1, recs)]
    by_x = [swap(h, 2) for h in heads]
    by_z = [swap(h, 4) for h in heads]
    cot_in, _ = lax.optimization_barrier((cotangent[0], packed))
    late_weights = by_x + by_z + [shift(far, j) for j in range(1, recs)]
    cot_own = in_hbm(cot_in)
    cot_other = swap(cot_in, 1)

    arrived = lax.all_to_all(
        packed.reshape(owners, high, -1), "seq", split_axis=0, concat_axis=0, tiled=True
    ).reshape(slots, -1)
    def mine(x):
        starts = [(halves[j] * 2 + core) * quarter for j in range(recs)]
        return jnp.concatenate(
            [lax.dynamic_slice_in_dim(x, at, quarter, 1) for at in starts], axis=1
        )

    conv_in, bias_in, _ = lax.optimization_barrier((conv_weight, conv_bias, heads))
    kernel = mine(jnp.transpose(conv_in, (1, 0, 2)).reshape(depth, -1))
    bias = mine(bias_in[None, :])
    share = mel // owners
    wide = share % 8 == 0
    packet = (recs, owners, share, taps * quarter) if wide else (recs, depth, quarter)
    arrived, kernel, bias = lax.optimization_barrier((arrived, kernel, bias))
    arrived_other = swap(arrived, 1)

    early_lanes = quarter // LANES * LANES
    cots, whole, left, slopes, pooled, valid, *ahead = call(
        functools.partial(prepare_kernel, share),
        [
            pltpu.VMEM((2 * rows, feats), BF16),
            pltpu.VMEM((width, feats), BF16),
            pltpu.VMEM((depth, 2 * rows), BF16),
            pltpu.VMEM((2, rows, width), F32),
            pltpu.VMEM((rows, width), BF16),
            pltpu.VMEM((rows, LANES), F32),
        ]
        + (
            [pltpu.VMEM((depth, early_lanes), F32), pltpu.VMEM((rows, early_lanes), BF16)]
            if early_lanes
            else []
        ),
        "prepare",
        in_specs=[smem, smem] + [vmem] * 3 + [anywhere, vmem, anywhere] + [vmem] * len(heads),
        out_specs=[vmem] * (8 if early_lanes else 6),
        scratch_shapes=[pltpu.SemaphoreType.DMA((2,))],
    )(base_in, early, arrived, kernel, bias, cot_own, cot_other, in_hbm(proj_weight), *heads)

    sums, pooled_other, _ = call(
        functools.partial(backward_kernel, share, early_lanes),
        [HBM(packet, BF16), HBM((rows, width), BF16), pltpu.VMEM((width, feats), BF16)],
        "backward",
        in_specs=[smem, smem] + [vmem] * (7 + len(ahead) + len(late_weights)),
        out_specs=[hbm, hbm, vmem],
        input_output_aliases={3: 2},
        scratch_shapes=[
            pltpu.VMEM(packet, BF16),
            pltpu.VMEM((rows, width), BF16),
            pltpu.VMEM((depth, 2 * rows), BF16),
            pltpu.VMEM((2, rows, width), F32),
            pltpu.SemaphoreType.DMA((1 + recs,)),
        ],
    )(late, halves, cots, whole, left, slopes, kernel, bias, arrived_other, *ahead, *late_weights)
    pieces = lax.all_to_all(
        sums.reshape((recs * owners, -1, packet[-1])),
        ("dp", "seq"),
        split_axis=0,
        concat_axis=0,
        tiled=True,
    )
    foreign = heads + late_weights
    merged = call(
        functools.partial(merge_kernel, quarter),
        HBM((rows, feats), BF16),
        "merge",
        in_specs=[smem, smem] + [vmem] * 4 + [anywhere] * (1 + 2 * len(foreign)),
        scratch_shapes=[
            pltpu.VMEM((2, width, feats), BF16),
            pltpu.SemaphoreType.DMA((2 + 4 * len(foreign),)),
        ],
    )(
        bases,
        offsets,
        pooled,
        swap(pooled_other, 1),
        valid,
        proj_bias[None, :],
        in_hbm(proj_weight),
        *foreign,
        *[swap(w, 1) for w in foreign],
    )
    pieces, merged = lax.optimization_barrier((pieces, merged))
    grad_weight = call(
        functools.partial(sum_kernel, quarter),
        jax.ShapeDtypeStruct((taps * share, chans), F32),
        "sum_pieces",
    )(pieces)
    grad_weight = jnp.transpose(grad_weight.reshape(taps, share, chans), (1, 0, 2))
    return merged[None], grad_weight


def solution(mesh):
    in_specs = (
        P("dp", "seq", None),
        P("dp", "seq"),
        P(),
        P(),
        P("dp", None),
        P(),
        P("dp", "seq", None),
    )
    out_specs = (P("dp", "seq", None), P("seq", None, "dp"))
    return jax.shard_map(body, mesh=mesh, in_specs=in_specs, out_specs=out_specs, check_vma=False)
```

time: 57.8 us -> 53.2 us (0.920)
  local copies, waits for them, and re-layouts: 6.37 us -> 2.39 us
  waiting for transfers between devices: 16.6 us -> 13.1 us
  Pallas kernels: 16.2 us -> 17.6 us
  starting transfers between devices: 16.9 us -> 18.2 us
    all_to_all x2, waiting for transfers between devices: 13.8 us -> 8.91 us  [the longest x1 5.27 us: body(): lax.all_to_all(sums.reshape((recs * owners, -1, packet[-1])), ('dp', 'seq...]
    dynamic_slice x2 -> x0, local copies, waits for them, and re-layouts: 2.93 us -> none  [the longest x1 1.91 us: body(): mid = lax.dynamic_slice_in_dim(weight_in, base + end, middle, 0)]
    ppermute x7 -> x9, starting transfers between devices: 3.05 us -> 5.18 us  [swap(): return lax.ppermute(x, 'seq', [(i, i ^ bit) for i in range(owners)])]
    ppermute x2, waiting for transfers between devices: 0.01 us -> 1.81 us  [shift(): return lax.ppermute(x, 'dp', [(i, (i + by) % recs) for i in range(recs)])]
    pallas_call x1, Pallas kernels: 2.58 us -> 3.86 us  [body(): call(functools.partial(prepare_kernel, share), [pltpu.VMEM((2 * rows, fea...]
    unnamed x10 -> x8, local copies, waits for them, and re-layouts: 1.96 us -> 0.92 us
    ppermute x7 -> x9, waiting for transfers between devices: 2.77 us -> 2.43 us  [swap(): return lax.ppermute(x, 'seq', [(i, i ^ bit) for i in range(owners)])]
  transfers between devices with their start and end apart: 11 -> 13, of which waited for: 6 -> 8; matrix products, arithmetic and copies ran while one was open for 7% -> 4% of each run, Pallas kernels for 18% -> 18%
where the time goes in v4:
time: 53.2 us; the launch traced here: 52.8 us
  starting transfers between devices  18.2 us (34%)
  Pallas kernels  17.6 us (33%)
  waiting for transfers between devices  13.1 us (25%)
  local copies, waits for them, and re-layouts  2.39 us (4%)
  between operations  0.83 us (2%)
  other arithmetic  0.61 us (1%)
    all_to_all x1, starting transfers between devices, body(): lax.all_to_all(packed.reshape(owners, high, -1), 'seq', split_axis=0, con...  5.91 us
    pallas_call x1, Pallas kernels, body(): call(functools.partial(merge_kernel, quarter), HBM((rows, feats), BF16),...  5.81 us
    all_to_all x1, waiting for transfers between devices, body(): lax.all_to_all(sums.reshape((recs * owners, -1, packet[-1])), ('dp', 'seq...  5.27 us
    ppermute x9, starting transfers between devices, swap(): return lax.ppermute(x, 'seq', [(i, i ^ bit) for i in range(owners)])  5.18 us
    pallas_call x1, Pallas kernels, body(): call(functools.partial(backward_kernel, share, early_lanes), [HBM(packet,...  4.46 us
    all_to_all x1, starting transfers between devices, body(): lax.all_to_all(sums.reshape((recs * owners, -1, packet[-1])), ('dp', 'seq...  3.99 us
    pallas_call x1, Pallas kernels, body(): call(functools.partial(prepare_kernel, share), [pltpu.VMEM((2 * rows, fea...  3.86 us
    all_to_all x1, waiting for transfers between devices, body(): lax.all_to_all(packed.reshape(owners, high, -1), 'seq', split_axis=0, con...  3.63 us
  transfers between devices with their start and end apart: 13, of which 8 were waited for; matrix products, arithmetic and copies ran while one was open for 4% of the time, Pallas kernels for 18%

profile of v4, /device:TPU:0, one launch (start us, length us, event | category | flops | bytes accessed | tf_op | source)
XLA Modules:
  0.0 52.8 jit_solution(9662988801219039756)
XLA Ops:
  0.8 2.7 %pack_patches.1 = (bf16[128,1152]{1,0:T(8,128)(2,1)}, bf16[80,2048]{1,0:T(8,128)(2,1)S(1)}, bf16[80,2048]{1,0:T(8,128)(2,1)}) custom-call(s32[3]{0:T(128)S(1)} %pad_add_fusion.2.cuts, bf16[256,128]{1,0:T(8,128)(2,1)} %bitcast.31, s32[1,128]{1,0:T(1,128)} %spots_hbm.1, bf16[640,2048]{1,0:T(8,128)(2,1)} %refs_0_.1), custom_call_target="tpu_custom_call" | custom-call | flops 1000000000 | tf_op jit(solution)/shard_map/pack_patches/pallas_call | solution.py:313
  3.5 0.5 collective-permute-start.1
  4.0 2.6 %collective-permute-start = (bf16[80,2048]{1,0:T(8,128)(2,1)S(1)}, bf16[80,2048]{1,0:T(8,128)(2,1)S(1)}, u32[]{:S(2)}, u32[]{:S(2)}) collective-permute-start(bf16[80,2048]{1,0:T(8,128)(2,1)S(1)} %get-tuple-element.24), channel_id=1, source_target_pairs={{0,16},{16,0},{1,17},{17,1},{2,18},{18,2},{3,19},{19,3},{4,20},{20... | collective-permute-start | bytes 983048 | tf_op jit(solution)/shard_map/ppermute | solution.py:285
  6.6 5.9 %all-to-all-start = ((bf16[16,8,1152]{2,1,0:T(8,128)(2,1)}), bf16[16,8,1152]{2,1,0:T(8,128)(2,1)S(1)}, u32[]{:S(2)}, u32[]{:S(2)}) async-start(bf16[16,8,1152]{2,1,0:T(8,128)(2,1)} %bitcast.30), calls=%async_computation | async-start | bytes 589824 | tf_op jit(solution)/shard_map/all_to_all | solution.py:337
  12.5 0.6 %collective-permute-start.5 = (bf16[80,2048]{1,0:T(8,128)(2,1)}, bf16[80,2048]{1,0:T(8,128)(2,1)S(1)}, u32[]{:S(2)}, u32[]{:S(2)}) collective-permute-start(bf16[80,2048]{1,0:T(8,128)(2,1)} %get-tuple-element.37), channel_id=1, source_target_pairs={{0,16},{16,0},{1,17},{17,1},{2,18},{18,2},{3,19},{19,3},{4,20},{20... | collective-permute-start | bytes 983048 | tf_op jit(solution)/shard_map/ppermute | solution.py:285
  13.1 1.8 %collective-permute-done.refs_0_.refs_1_ = bf16[80,2048]{1,0:T(8,128)(2,1)S(1)} collective-permute-done((bf16[80,2048]{1,0:T(8,128)(2,1)S(1)}, bf16[80,2048]{1,0:T(8,128)(2,1)S(1)}, u32[]{:S(2)}, u32[]{:S(2)}) %collective-permute-start) | collective-permute-done | bytes 327712 | tf_op jit(solution)/shard_map/ppermute | solution.py:285
  15.0 1.7 %collective-permute-start.3 = (bf16[80,2048]{1,0:T(8,128)(2,1)S(1)}, bf16[80,2048]{1,0:T(8,128)(2,1)S(1)}, u32[]{:S(2)}, u32[]{:S(2)}) collective-permute-start(bf16[80,2048]{1,0:T(8,128)(2,1)S(1)} %collective-permute-done.refs_0_.refs_1_), channel_id=1, source_target_pairs={{0,2},{1,3},{2,0},{3,1},{4,6},{5,7},{6,4},{7,5},{8,10},{9,11},{10,... | collective-permute-start | bytes 983048 | tf_op jit(solution)/shard_map/ppermute | solution.py:288
  16.7 1.6 %collective-permute-start.4 = (bf16[80,2048]{1,0:T(8,128)(2,1)S(1)}, bf16[80,2048]{1,0:T(8,128)(2,1)S(1)}, u32[]{:S(2)}, u32[]{:S(2)}) collective-permute-start(bf16[80,2048]{1,0:T(8,128)(2,1)S(1)} %collective-permute-done.refs_0_.refs_1_), channel_id=1, source_target_pairs={{0,4},{1,5},{2,6},{3,7},{4,0},{5,1},{6,2},{7,3},{8,12},{9,13},{10,... | collective-permute-start | bytes 983048 | tf_op jit(solution)/shard_map/ppermute | solution.py:288
  18.3 1.4 %constant_dynamic-slice_fusion.1 = (bf16[384,320]{1,0:T(8,128)(2,1)S(1)}, bf16[384,320]{1,0:T(8,128)(2,1)S(1)}) fusion(bf16[384,1280]{1,0:T(8,128)(2,1)} %bitcast.29, s32[]{:T(128)S(6)} %select_n.45, s32[]{:T(128)S(6)} %select_n.46), kind=kLoop, calls=%fused_computation.8 | loop fusion | bytes 983048 | tf_op jit(solution)/shard_map/dynamic_slice | solution.py:343
  19.9 3.6 %all-to-all-done = bf16[16,8,1152]{2,1,0:T(8,128)(2,1)S(1)} async-done(((bf16[16,8,1152]{2,1,0:T(8,128)(2,1)}), bf16[16,8,1152]{2,1,0:T(8,128)(2,1)S(1)}, u32[]{:S(2)}, u32[]{:S(2)}) %all-to-all-start) | async-done | bytes 294944 | tf_op jit(solution)/shard_map/all_to_all | solution.py:337
  23.7 3.9 %prepare.1 = (bf16[512,2048]{1,0:T(8,128)(2,1)S(1)}, bf16[640,2048]{1,0:T(8,128)(2,1)S(1)}, bf16[384,512]{1,0:T(8,128)(2,1)S(1)}, f32[2,256,640]{2,1,0:T(8,128)S...) custom-call(s32[1]{0:T(128)} %bitcast.5.base, ...), custom_call_target="tpu_custom_call" | custom-call | flops 1000000000 | tf_op jit(solution)/shard_map/prepare/pallas_call | solution.py:356
  27.7 4.5 %backward.1 = (bf16[2,16,8,960]{3,2,1,0:T(8,128)(2,1)}, bf16[256,640]{1,0:T(8,128)(2,1)}, bf16[640,2048]{1,0:T(8,128)(2,1)S(1)}) custom-call(s32[3]{0:T(128)S(1)} %pad_add_fusion.offsets, s32[2]{0:T(128)S(1)} %pad_add_fusion.1.halves, bf16[512,2048]{1,0:T(8,128)(2,1)S(1)} %get-tuple-element.31.cots, ...), custom_call_target="tpu_custom_call", output_to_operand_aliasing={{2}: (3, {})} | custom-call | flops 1000000000 | tf_op jit(solution)/shard_map/backward/pallas_call | solution.py:377
  32.1 4.0 %all-to-all-start.1 = ((bf16[32,8,960]{2,1,0:T(8,128)(2,1)}), bf16[32,8,960]{2,1,0:T(8,128)(2,1)S(1)}, u32[]{:S(2)}, u32[]{:S(2)}) async-start(bf16[32,8,960]{2,1,0:T(8,128)(2,1)} %bitcast.28), calls=%async_computation.1 | async-start | bytes 1048576 | tf_op jit(solution)/shard_map/all_to_all | solution.py:392
  36.1 0.3 collective-permute-start.10
  36.4 0.3 collective-permute-start.7
  36.7 0.3 collective-permute-start.8
  37.0 0.3 collective-permute-start.9
  37.8 0.5 collective-permute-done.7.refs_5_
  38.3 0.9 %collective-permute-done.8.refs_6_ = bf16[80,2048]{1,0:T(8,128)(2,1)S(1)} collective-permute-done((bf16[80,2048]{1,0:T(8,128)(2,1)S(1)}, bf16[80,2048]{1,0:T(8,128)(2,1)S(1)}, u32[]{:S(2)}, u32[]{:S(2)}) %collective-permute-start.8) | collective-permute-done | bytes 327712 | tf_op jit(solution)/shard_map/ppermute | solution.py:288
  39.4 0.7 %collective-permute-done.6.other = bf16[256,640]{1,0:T(8,128)(2,1)} collective-permute-done((bf16[256,640]{1,0:T(8,128)(2,1)}, bf16[256,640]{1,0:T(8,128)(2,1)}, u32[]{:S(2)}, u32[]{:S(2)}) %collective-permute-start.6) | collective-permute-done | bytes 327712 | tf_op jit(solution)/shard_map/ppermute | solution.py:288
  40.0 0.9 %copy-done.1 = f32[256,128]{1,0:T(8,128)S(1)} copy-done((f32[256,128]{1,0:T(8,128)S(1)}, f32[256,128]{1,0:T(8,128)}, u32[]{:S(2)}) %copy-start.1) | copy-done | bytes 131096
  40.9 5.8 %merge.1 = bf16[256,2048]{1,0:T(8,128)(2,1)} custom-call(s32[2]{0:T(128)S(1)} %pad_add_fusion.3.bases, s32[4]{0:T(128)S(1)} %pad_add_fusion.4.offsets, bf16[256,640]{1,0:T(8,128)(2,1)S(1)} %get-tuple-element.39.pooled, bf16[256,640]{1,0:T(8,128)(2,1)} %collective-permute-done.6.other, f32[256,128]{1,0:T(8,128)S(1)} %copy-done.1, f32[1,2048]{1,0:T(1,128)S(1)} %bitcast.26, ...), custom_call_target="tpu_custom_call" | custom-call | flops 1000000000 | tf_op jit(solution)/shard_map/merge/pallas_call | solution.py:400
  46.8 5.3 %all-to-all-done.1.pieces = bf16[32,8,960]{2,1,0:T(8,128)(2,1)S(1)} async-done(((bf16[32,8,960]{2,1,0:T(8,128)(2,1)}), bf16[32,8,960]{2,1,0:T(8,128)(2,1)S(1)}, u32[]{:S(2)}, u32[]{:S(2)}) %all-to-all-start.1) | async-done | bytes 491552 | tf_op jit(solution)/shard_map/all_to_all | solution.py:392
  52.0 0.8 %sum_pieces.1 = f32[24,640]{1,0:T(8,128)} custom-call(bf16[32,8,960]{2,1,0:T(8,128)(2,1)S(1)} %all-to-all-done.1.pieces), custom_call_target="tpu_custom_call" | custom-call | flops 1000000000 | tf_op jit(solution)/shard_map/sum_pieces/pallas_call | solution.py:421
  (26 shorter events, 1.3 us)
Async XLA Ops:
  0.6 14.3 %copy-start.3 = (f32[1280]{0:T(1024)S(1)}, f32[1280]{0:T(1024)}, u32[]{:S(2)}) copy-start(f32[1280]{0:T(1024)} %param.10) | copy-start | bytes 15364
  3.5 20.2 %collective-permute-start.1 = (bf16[256,2048]{1,0:T(8,128)(2,1)}, bf16[256,2048]{1,0:T(8,128)(2,1)S(1)}, u32[]{:S(2)}, u32[]{:S(2)}) collective-permute-start(bf16[256,2048]{1,0:T(8,128)(2,1)} %bitcast.16.own_in), channel_id=1, source_target_pairs={{0,1},{1,0},{2,3},{3,2},{4,5},{5,4},{6,7},{7,6},{8,9},{9,8},{10,11... | collective-permute-start | bytes 3145736 | tf_op jit(solution)/shard_map/ppermute | solution.py:288
  4.0 10.9 %collective-permute-start = (bf16[80,2048]{1,0:T(8,128)(2,1)S(1)}, bf16[80,2048]{1,0:T(8,128)(2,1)S(1)}, u32[]{:S(2)}, u32[]{:S(2)}) collective-permute-start(bf16[80,2048]{1,0:T(8,128)(2,1)S(1)} %get-tuple-element.24), channel_id=1, source_target_pairs={{0,16},{16,0},{1,17},{17,1},{2,18},{18,2},{3,19},{19,3},{4,20},{20... | collective-permute-start | bytes 983048 | tf_op jit(solution)/shard_map/ppermute | solution.py:285
  6.6 17.0 %all-to-all-start = ((bf16[16,8,1152]{2,1,0:T(8,128)(2,1)}), bf16[16,8,1152]{2,1,0:T(8,128)(2,1)S(1)}, u32[]{:S(2)}, u32[]{:S(2)}) async-start(bf16[16,8,1152]{2,1,0:T(8,128)(2,1)} %bitcast.30), calls=%async_computation | async-start | bytes 589824 | tf_op jit(solution)/shard_map/all_to_all | solution.py:337
  12.5 15.1 %collective-permute-start.5 = (bf16[80,2048]{1,0:T(8,128)(2,1)}, bf16[80,2048]{1,0:T(8,128)(2,1)S(1)}, u32[]{:S(2)}, u32[]{:S(2)}) collective-permute-start(bf16[80,2048]{1,0:T(8,128)(2,1)} %get-tuple-element.37), channel_id=1, source_target_pairs={{0,16},{16,0},{1,17},{17,1},{2,18},{18,2},{3,19},{19,3},{4,20},{20... | collective-permute-start | bytes 983048 | tf_op jit(solution)/shard_map/ppermute | solution.py:285
  15.0 12.6 %collective-permute-start.3 = (bf16[80,2048]{1,0:T(8,128)(2,1)S(1)}, bf16[80,2048]{1,0:T(8,128)(2,1)S(1)}, u32[]{:S(2)}, u32[]{:S(2)}) collective-permute-start(bf16[80,2048]{1,0:T(8,128)(2,1)S(1)} %collective-permute-done.refs_0_.refs_1_), channel_id=1, source_target_pairs={{0,2},{1,3},{2,0},{3,1},{4,6},{5,7},{6,4},{7,5},{8,10},{9,11},{10,... | collective-permute-start | bytes 983048 | tf_op jit(solution)/shard_map/ppermute | solution.py:288
  16.7 10.9 %collective-permute-start.4 = (bf16[80,2048]{1,0:T(8,128)(2,1)S(1)}, bf16[80,2048]{1,0:T(8,128)(2,1)S(1)}, u32[]{:S(2)}, u32[]{:S(2)}) collective-permute-start(bf16[80,2048]{1,0:T(8,128)(2,1)S(1)} %collective-permute-done.refs_0_.refs_1_), channel_id=1, source_target_pairs={{0,4},{1,5},{2,6},{3,7},{4,0},{5,1},{6,2},{7,3},{8,12},{9,13},{10,... | collective-permute-start | bytes 983048 | tf_op jit(solution)/shard_map/ppermute | solution.py:288
  23.6 4.1 %collective-permute-start.2 = (bf16[128,1152]{1,0:T(8,128)(2,1)S(1)}, bf16[128,1152]{1,0:T(8,128)(2,1)S(1)}, u32[]{:S(2)}, u32[]{:S(2)}) collective-permute-start(bf16[128,1152]{1,0:T(8,128)(2,1)S(1)} %bitcast.24), channel_id=1, source_target_pairs={{0,1},{1,0},{2,3},{3,2},{4,5},{5,4},{6,7},{7,6},{8,9},{9,8},{10,11... | collective-permute-start | bytes 884744 | tf_op jit(solution)/shard_map/ppermute | solution.py:288
  27.6 4.5 %copy-start = (f32[256,128]{1,0:T(8,128)}, f32[256,128]{1,0:T(8,128)S(1)}, u32[]{:S(2)}) copy-start(f32[256,128]{1,0:T(8,128)S(1)} %get-tuple-element.41.valid) | copy-start | bytes 393220
  27.6 12.4 %copy-start.2 = (f32[2048]{0:T(1024)S(1)}, f32[2048]{0:T(1024)}, u32[]{:S(2)}) copy-start(f32[2048]{0:T(1024)} %param.12) | copy-start | bytes 24580
  32.1 19.9 %all-to-all-start.1 = ((bf16[32,8,960]{2,1,0:T(8,128)(2,1)}), bf16[32,8,960]{2,1,0:T(8,128)(2,1)S(1)}, u32[]{:S(2)}, u32[]{:S(2)}) async-start(bf16[32,8,960]{2,1,0:T(8,128)(2,1)} %bitcast.28), calls=%async_computation.1 | async-start | bytes 1048576 | tf_op jit(solution)/shard_map/all_to_all | solution.py:392
  36.1 1.7 %collective-permute-start.10 = (bf16[80,2048]{1,0:T(8,128)(2,1)S(1)}, bf16[80,2048]{1,0:T(8,128)(2,1)S(1)}, u32[]{:S(2)}, u32[]{:S(2)}) collective-permute-start(bf16[80,2048]{1,0:T(8,128)(2,1)S(1)} %collective-permute-done.5.refs_4_), channel_id=1, source_target_pairs={{0,1},{1,0},{2,3},{3,2},{4,5},{5,4},{6,7},{7,6},{8,9},{9,8},{10,11... | collective-permute-start | bytes 983048 | tf_op jit(solution)/shard_map/ppermute | solution.py:288
  36.4 1.8 %collective-permute-start.7 = (bf16[80,2048]{1,0:T(8,128)(2,1)S(1)}, bf16[80,2048]{1,0:T(8,128)(2,1)S(1)}, u32[]{:S(2)}, u32[]{:S(2)}) collective-permute-start(bf16[80,2048]{1,0:T(8,128)(2,1)S(1)} %collective-permute-done.refs_0_.refs_1_), channel_id=1, source_target_pairs={{0,1},{1,0},{2,3},{3,2},{4,5},{5,4},{6,7},{7,6},{8,9},{9,8},{10,11... | collective-permute-start | bytes 983048 | tf_op jit(solution)/shard_map/ppermute | solution.py:288
  36.7 2.5 %collective-permute-start.8 = (bf16[80,2048]{1,0:T(8,128)(2,1)S(1)}, bf16[80,2048]{1,0:T(8,128)(2,1)S(1)}, u32[]{:S(2)}, u32[]{:S(2)}) collective-permute-start(bf16[80,2048]{1,0:T(8,128)(2,1)S(1)} %collective-permute-done.3.refs_2_), channel_id=1, source_target_pairs={{0,1},{1,0},{2,3},{3,2},{4,5},{5,4},{6,7},{7,6},{8,9},{9,8},{10,11... | collective-permute-start | bytes 983048 | tf_op jit(solution)/shard_map/ppermute | solution.py:288
  37.0 2.4 %collective-permute-start.9 = (bf16[80,2048]{1,0:T(8,128)(2,1)S(1)}, bf16[80,2048]{1,0:T(8,128)(2,1)}, u32[]{:S(2)}, u32[]{:S(2)}) collective-permute-start(bf16[80,2048]{1,0:T(8,128)(2,1)S(1)} %collective-permute-done.4.refs_3_), channel_id=1, source_target_pairs={{0,1},{1,0},{2,3},{3,2},{4,5},{5,4},{6,7},{7,6},{8,9},{9,8},{10,11... | collective-permute-start | bytes 983048 | tf_op jit(solution)/shard_map/ppermute | solution.py:288
  37.2 2.8 %collective-permute-start.6 = (bf16[256,640]{1,0:T(8,128)(2,1)}, bf16[256,640]{1,0:T(8,128)(2,1)}, u32[]{:S(2)}, u32[]{:S(2)}) collective-permute-start(bf16[256,640]{1,0:T(8,128)(2,1)} %get-tuple-element.40), channel_id=1, source_target_pairs={{0,1},{1,0},{2,3},{3,2},{4,5},{5,4},{6,7},{7,6},{8,9},{9,8},{10,11... | collective-permute-start | bytes 983048 | tf_op jit(solution)/shard_map/ppermute | solution.py:288
  40.0 0.9 %copy-start.1 = (f32[256,128]{1,0:T(8,128)S(1)}, f32[256,128]{1,0:T(8,128)}, u32[]{:S(2)}) copy-start(f32[256,128]{1,0:T(8,128)} %copy-done) | copy-start | bytes 393220

commit v5 on v4

--- a/solution.py
+++ b/solution.py
@@ -49,23 +49,15 @@
         copy.wait()
 
 
-def pack_kernel(owners, capacity, rows_own, cuts, mel_hbm, spots_hbm, weight, out, head, far, mel_ref, spots_ref, sems):
+def pack_kernel(owners, capacity, rows_own, cuts, mel_hbm, spots_hbm, weight, out, head, mel_ref, spots_ref, sems):
     loads = [
         pltpu.make_async_copy(spots_hbm, spots_ref, sems.at[0]),
         pltpu.make_async_copy(mel_hbm, mel_ref, sems.at[1]),
     ]
     fetch(loads)
-    unit = head.shape[0]
-    rows = []
-    targets = [head, far.at[pl.ds(0, unit)]]
-    if far.shape[0] > unit:
-        targets.append(far.at[pl.ds(unit, far.shape[0] - unit)])
-    for n, ref in enumerate(targets):
-        start = pl.multiple_of(cuts[n], 16)
-        rows.append(
-            pltpu.make_async_copy(weight.at[pl.ds(start, ref.shape[0])], ref, sems.at[2 + n])
-        )
-    fetch(rows)
+    start = pl.multiple_of(cuts[0], 16)
+    rows = pltpu.make_async_copy(weight.at[pl.ds(start, head.shape[0])], head, sems.at[2])
+    rows.start()
     high = min(capacity, 8)
     slots = owners * high
     frames, mel = mel_ref.shape
@@ -95,7 +87,7 @@
         places = jnp.where(lane == g, spot, places)
         out[:, g * width : (g + 1) * width] = mm(onehot.astype(BF16), patch).astype(BF16)
     out[:, capacity // high * width :] = places.astype(BF16)
-    settle(rows)
+    rows.wait()
 
 
 def rows_from_slots(arrived, rows, mel):
@@ -294,7 +286,7 @@
     part_x = (bit * 2 + 1 - side) * unit
     part_z = ((1 - bit) * 2 + side) * unit
     part_far = ((1 - bit) * 2 + 1 - side) * unit
-    cuts = jnp.stack([base + part, base + part_far, base + 4 * unit]).astype(I32)
+    cuts = (base + part).reshape(1).astype(I32)
     early = jnp.stack([(j + 1) * quarter + part for j in range(recs - 1)]).astype(I32)
     late = [(j + 1) * quarter + p for p in (part_x, part_z, part_far) for j in range(recs - 1)]
     late = jnp.stack(late).astype(I32)
@@ -310,25 +302,29 @@
     high = min(capacity, 8)
     slots = owners * high
     wide_slots = capacity // high * 4 * mel + LANES
-    packed, head, far = call(
+    packed, head = call(
         functools.partial(pack_kernel, owners, capacity, rows),
         [
             HBM((slots, wide_slots), BF16),
             pltpu.VMEM((unit, feats), BF16),
-            pltpu.VMEM((quarter - 3 * unit, feats), BF16),
         ],
         "pack_patches",
         in_specs=[smem, hbm, hbm, hbm],
-        out_specs=[vmem] * 3,
+        out_specs=[vmem] * 2,
         scratch_shapes=[
             pltpu.VMEM((frames, mel), BF16),
             pltpu.VMEM((1, toks), I32),
-            pltpu.SemaphoreType.DMA((5,)),
+            pltpu.SemaphoreType.DMA((3,)),
         ],
     )(cuts, in_hbm(mel_frames[0]), in_hbm(positions), in_hbm(proj_weight))
     heads = [shift(head, j) for j in range(1, recs)]
     by_x = [swap(h, 2) for h in heads]
     by_z = [swap(h, 4) for h in heads]
+    weight_in, _ = lax.optimization_barrier((proj_weight, packed))
+    far = lax.dynamic_slice_in_dim(weight_in, base + part_far, unit, 0)
+    if extra := quarter - 4 * unit:
+        last = lax.dynamic_slice_in_dim(weight_in, base + 4 * unit, extra, 0)
+        far = jnp.concatenate([far, last], axis=0)
     cot_in, _ = lax.optimization_barrier((cotangent[0], packed))
     late_weights = by_x + by_z + [shift(far, j) for j in range(1, recs)]
     cot_own = in_hbm(cot_in)

time: 53.2 us -> 52.5 us (0.987)
  local copies, waits for them, and re-layouts: 2.39 us -> 4.12 us
  waiting for transfers between devices: 13.1 us -> 11.5 us
  Pallas kernels: 17.6 us -> 17 us
    dynamic_slice x0 -> x1, local copies, waits for them, and re-layouts: none -> 1.72 us  [body(): far = lax.dynamic_slice_in_dim(weight_in, base + part_far, unit, 0)]
    ppermute x2, waiting for transfers between devices: 1.81 us -> 0.11 us  [shift(): return lax.ppermute(x, 'dp', [(i, (i + by) % recs) for i in range(recs)])]
    pallas_call x1, Pallas kernels: 2.68 us -> 2.02 us  [body(): call(functools.partial(pack_kernel, owners, capacity, rows), [HBM((slots,...]
  transfers between devices with their start and end apart: 13 -> 13, of which waited for: 8 -> 8; matrix products, arithmetic and copies ran while one was open for 4% -> 7% of each run, Pallas kernels for 18% -> 19%
where the time goes in v5:
time: 52.5 us; the launch traced here: 52.1 us
  starting transfers between devices  18.2 us (35%)
  Pallas kernels  17 us (32%)
  waiting for transfers between devices  11.5 us (22%)
  local copies, waits for them, and re-layouts  4.12 us (8%)
  between operations  0.85 us (2%)
  other arithmetic  0.53 us (1%)
    all_to_all x1, starting transfers between devices, body(): lax.all_to_all(packed.reshape(owners, high, -1), 'seq', split_axis=0, con...  5.91 us
    pallas_call x1, Pallas kernels, body(): call(functools.partial(merge_kernel, quarter), HBM((rows, feats), BF16),...  5.8 us
    all_to_all x1, waiting for transfers between devices, body(): lax.all_to_all(sums.reshape((recs * owners, -1, packet[-1])), ('dp', 'seq...  5.28 us
    ppermute x9, starting transfers between devices, swap(): return lax.ppermute(x, 'seq', [(i, i ^ bit) for i in range(owners)])  5.18 us
    pallas_call x1, Pallas kernels, body(): call(functools.partial(backward_kernel, share, early_lanes), [HBM(packet,...  4.51 us
    all_to_all x1, starting transfers between devices, body(): lax.all_to_all(sums.reshape((recs * owners, -1, packet[-1])), ('dp', 'seq...  3.96 us
    pallas_call x1, Pallas kernels, body(): call(functools.partial(prepare_kernel, share), [pltpu.VMEM((2 * rows, fea...  3.87 us
    all_to_all x1, waiting for transfers between devices, body(): lax.all_to_all(packed.reshape(owners, high, -1), 'seq', split_axis=0, con...  3.63 us
  transfers between devices with their start and end apart: 13, of which 8 were waited for; matrix products, arithmetic and copies ran while one was open for 7% of the time, Pallas kernels for 19%

profile of v5, /device:TPU:0, one launch (start us, length us, event | category | flops | bytes accessed | tf_op | source)
XLA Modules:
  0.0 52.1 jit_solution(9612815093711804986)
XLA Ops:
  0.7 2.0 %pack_patches.1 = (bf16[128,1152]{1,0:T(8,128)(2,1)}, bf16[80,2048]{1,0:T(8,128)(2,1)S(1)}) custom-call(s32[1]{0:T(128)} %bitcast.7.cuts, bf16[256,128]{1,0:T(8,128)(2,1)} %bitcast.29, s32[1,128]{1,0:T(1,128)} %spots_hbm.1, bf16[640,2048]{1,0:T(8,128)(2,1)} %refs_0_.1), custom_call_target="tpu_custom_call" | custom-call | flops 1000000000 | tf_op jit(solution)/shard_map/pack_patches/pallas_call | solution.py:305
  2.7 0.5 collective-permute-start.1
  3.2 2.6 %collective-permute-start = (bf16[80,2048]{1,0:T(8,128)(2,1)S(1)}, bf16[80,2048]{1,0:T(8,128)(2,1)S(1)}, u32[]{:S(2)}, u32[]{:S(2)}) collective-permute-start(bf16[80,2048]{1,0:T(8,128)(2,1)S(1)} %get-tuple-element.24), channel_id=1, source_target_pairs={{0,16},{16,0},{1,17},{17,1},{2,18},{18,2},{3,19},{19,3},{4,20},{20... | collective-permute-start | bytes 983048 | tf_op jit(solution)/shard_map/ppermute | solution.py:277
  5.8 5.9 %all-to-all-start = ((bf16[16,8,1152]{2,1,0:T(8,128)(2,1)}), bf16[16,8,1152]{2,1,0:T(8,128)(2,1)S(1)}, u32[]{:S(2)}, u32[]{:S(2)}) async-start(bf16[16,8,1152]{2,1,0:T(8,128)(2,1)} %bitcast.28), calls=%async_computation | async-start | bytes 589824 | tf_op jit(solution)/shard_map/all_to_all | solution.py:333
  11.8 1.7 %constant_dynamic-slice_fusion = bf16[80,2048]{1,0:T(8,128)(2,1)} fusion(bf16[640,2048]{1,0:T(8,128)(2,1)} %refs_0_.1, s32[]{:T(128)S(6)} %select_n.50), kind=kLoop, calls=%fused_computation.2 | loop fusion | bytes 655364 | tf_op jit(solution)/shard_map/dynamic_slice | solution.py:324
  13.5 0.5 %collective-permute-start.5 = (bf16[80,2048]{1,0:T(8,128)(2,1)}, bf16[80,2048]{1,0:T(8,128)(2,1)S(1)}, u32[]{:S(2)}, u32[]{:S(2)}) collective-permute-start(bf16[80,2048]{1,0:T(8,128)(2,1)} %constant_dynamic-slice_fusion), channel_id=1, source_target_pairs={{0,16},{16,0},{1,17},{17,1},{2,18},{18,2},{3,19},{19,3},{4,20},{20... | collective-permute-start | bytes 983048 | tf_op jit(solution)/shard_map/ppermute | solution.py:277
  14.2 1.8 %collective-permute-start.3 = (bf16[80,2048]{1,0:T(8,128)(2,1)S(1)}, bf16[80,2048]{1,0:T(8,128)(2,1)S(1)}, u32[]{:S(2)}, u32[]{:S(2)}) collective-permute-start(bf16[80,2048]{1,0:T(8,128)(2,1)S(1)} %collective-permute-done.refs_0_.refs_1_), channel_id=1, source_target_pairs={{0,2},{1,3},{2,0},{3,1},{4,6},{5,7},{6,4},{7,5},{8,10},{9,11},{10,... | collective-permute-start | bytes 983048 | tf_op jit(solution)/shard_map/ppermute | solution.py:280
  16.0 1.5 %collective-permute-start.4 = (bf16[80,2048]{1,0:T(8,128)(2,1)S(1)}, bf16[80,2048]{1,0:T(8,128)(2,1)S(1)}, u32[]{:S(2)}, u32[]{:S(2)}) collective-permute-start(bf16[80,2048]{1,0:T(8,128)(2,1)S(1)} %collective-permute-done.refs_0_.refs_1_), channel_id=1, source_target_pairs={{0,4},{1,5},{2,6},{3,7},{4,0},{5,1},{6,2},{7,3},{8,12},{9,13},{10,... | collective-permute-start | bytes 983048 | tf_op jit(solution)/shard_map/ppermute | solution.py:280
  17.6 1.4 %constant_dynamic-slice_fusion.2 = (bf16[384,320]{1,0:T(8,128)(2,1)S(1)}, bf16[384,320]{1,0:T(8,128)(2,1)S(1)}) fusion(bf16[384,1280]{1,0:T(8,128)(2,1)} %bitcast.27, s32[]{:T(128)S(6)} %select_n.48, s32[]{:T(128)S(6)} %select_n.49), kind=kLoop, calls=%fused_computation.4 | loop fusion | bytes 983048 | tf_op jit(solution)/shard_map/dynamic_slice | solution.py:339
  19.2 3.6 %all-to-all-done = bf16[16,8,1152]{2,1,0:T(8,128)(2,1)S(1)} async-done(((bf16[16,8,1152]{2,1,0:T(8,128)(2,1)}), bf16[16,8,1152]{2,1,0:T(8,128)(2,1)S(1)}, u32[]{:S(2)}, u32[]{:S(2)}) %all-to-all-start) | async-done | bytes 294944 | tf_op jit(solution)/shard_map/all_to_all | solution.py:333
  23.0 3.9 %prepare.1 = (bf16[512,2048]{1,0:T(8,128)(2,1)S(1)}, bf16[640,2048]{1,0:T(8,128)(2,1)S(1)}, bf16[384,512]{1,0:T(8,128)(2,1)S(1)}, f32[2,256,640]{2,1,0:T(8,128)S...) custom-call(s32[1]{0:T(128)} %bitcast.5.base, ...), custom_call_target="tpu_custom_call" | custom-call | flops 1000000000 | tf_op jit(solution)/shard_map/prepare/pallas_call | solution.py:352
  26.9 4.5 %backward.1 = (bf16[2,16,8,960]{3,2,1,0:T(8,128)(2,1)}, bf16[256,640]{1,0:T(8,128)(2,1)}, bf16[640,2048]{1,0:T(8,128)(2,1)S(1)}) custom-call(s32[3]{0:T(128)S(1)} %pad_add_fusion.offsets, s32[2]{0:T(128)S(1)} %pad_add_fusion.1.halves, bf16[512,2048]{1,0:T(8,128)(2,1)S(1)} %get-tuple-element.31.cots, ...), custom_call_target="tpu_custom_call", output_to_operand_aliasing={{2}: (3, {})} | custom-call | flops 1000000000 | tf_op jit(solution)/shard_map/backward/pallas_call | solution.py:373
  31.4 4.0 %all-to-all-start.1 = ((bf16[32,8,960]{2,1,0:T(8,128)(2,1)}), bf16[32,8,960]{2,1,0:T(8,128)(2,1)S(1)}, u32[]{:S(2)}, u32[]{:S(2)}) async-start(bf16[32,8,960]{2,1,0:T(8,128)(2,1)} %bitcast.26), calls=%async_computation.1 | async-start | bytes 1048576 | tf_op jit(solution)/shard_map/all_to_all | solution.py:388
  35.4 0.3 collective-permute-start.10
  35.7 0.3 collective-permute-start.7
  36.0 0.3 collective-permute-start.8
  36.2 0.3 collective-permute-start.9
  37.1 0.5 collective-permute-done.7.refs_5_
  37.6 0.9 %collective-permute-done.8.refs_6_ = bf16[80,2048]{1,0:T(8,128)(2,1)S(1)} collective-permute-done((bf16[80,2048]{1,0:T(8,128)(2,1)S(1)}, bf16[80,2048]{1,0:T(8,128)(2,1)S(1)}, u32[]{:S(2)}, u32[]{:S(2)}) %collective-permute-start.8) | collective-permute-done | bytes 327712 | tf_op jit(solution)/shard_map/ppermute | solution.py:280
  38.6 0.7 %collective-permute-done.6.other = bf16[256,640]{1,0:T(8,128)(2,1)} collective-permute-done((bf16[256,640]{1,0:T(8,128)(2,1)}, bf16[256,640]{1,0:T(8,128)(2,1)}, u32[]{:S(2)}, u32[]{:S(2)}) %collective-permute-start.6) | collective-permute-done | bytes 327712 | tf_op jit(solution)/shard_map/ppermute | solution.py:280
  39.3 0.9 %copy-done.1 = f32[256,128]{1,0:T(8,128)S(1)} copy-done((f32[256,128]{1,0:T(8,128)S(1)}, f32[256,128]{1,0:T(8,128)}, u32[]{:S(2)}) %copy-start.1) | copy-done | bytes 131096
  40.2 5.8 %merge.1 = bf16[256,2048]{1,0:T(8,128)(2,1)} custom-call(s32[2]{0:T(128)S(1)} %pad_add_fusion.2.bases, s32[4]{0:T(128)S(1)} %pad_add_fusion.3.offsets, bf16[256,640]{1,0:T(8,128)(2,1)S(1)} %get-tuple-element.39.pooled, bf16[256,640]{1,0:T(8,128)(2,1)} %collective-permute-done.6.other, f32[256,128]{1,0:T(8,128)S(1)} %copy-done.1, f32[1,2048]{1,0:T(1,128)S(1)} %bitcast.24, ...), custom_call_target="tpu_custom_call" | custom-call | flops 1000000000 | tf_op jit(solution)/shard_map/merge/pallas_call | solution.py:396
  46.0 5.3 %all-to-all-done.1.pieces = bf16[32,8,960]{2,1,0:T(8,128)(2,1)S(1)} async-done(((bf16[32,8,960]{2,1,0:T(8,128)(2,1)}), bf16[32,8,960]{2,1,0:T(8,128)(2,1)S(1)}, u32[]{:S(2)}, u32[]{:S(2)}) %all-to-all-start.1) | async-done | bytes 491552 | tf_op jit(solution)/shard_map/all_to_all | solution.py:388
  51.3 0.8 %sum_pieces.1 = f32[24,640]{1,0:T(8,128)} custom-call(bf16[32,8,960]{2,1,0:T(8,128)(2,1)S(1)} %all-to-all-done.1.pieces), custom_call_target="tpu_custom_call" | custom-call | flops 1000000000 | tf_op jit(solution)/shard_map/sum_pieces/pallas_call | solution.py:417
  (26 shorter events, 1.3 us)
Async XLA Ops:
  0.6 13.5 %copy-start.3 = (f32[1280]{0:T(1024)S(1)}, f32[1280]{0:T(1024)}, u32[]{:S(2)}) copy-start(f32[1280]{0:T(1024)} %param.10) | copy-start | bytes 15364
  2.7 20.2 %collective-permute-start.1 = (bf16[256,2048]{1,0:T(8,128)(2,1)}, bf16[256,2048]{1,0:T(8,128)(2,1)S(1)}, u32[]{:S(2)}, u32[]{:S(2)}) collective-permute-start(bf16[256,2048]{1,0:T(8,128)(2,1)} %bitcast.14.own_in), channel_id=1, source_target_pairs={{0,1},{1,0},{2,3},{3,2},{4,5},{5,4},{6,7},{7,6},{8,9},{9,8},{10,11... | collective-permute-start | bytes 3145736 | tf_op jit(solution)/shard_map/ppermute | solution.py:280
  3.2 10.9 %collective-permute-start = (bf16[80,2048]{1,0:T(8,128)(2,1)S(1)}, bf16[80,2048]{1,0:T(8,128)(2,1)S(1)}, u32[]{:S(2)}, u32[]{:S(2)}) collective-permute-start(bf16[80,2048]{1,0:T(8,128)(2,1)S(1)} %get-tuple-element.24), channel_id=1, source_target_pairs={{0,16},{16,0},{1,17},{17,1},{2,18},{18,2},{3,19},{19,3},{4,20},{20... | collective-permute-start | bytes 983048 | tf_op jit(solution)/shard_map/ppermute | solution.py:277
  5.8 17.0 %all-to-all-start = ((bf16[16,8,1152]{2,1,0:T(8,128)(2,1)}), bf16[16,8,1152]{2,1,0:T(8,128)(2,1)S(1)}, u32[]{:S(2)}, u32[]{:S(2)}) async-start(bf16[16,8,1152]{2,1,0:T(8,128)(2,1)} %bitcast.28), calls=%async_computation | async-start | bytes 589824 | tf_op jit(solution)/shard_map/all_to_all | solution.py:333
  13.5 13.4 %collective-permute-start.5 = (bf16[80,2048]{1,0:T(8,128)(2,1)}, bf16[80,2048]{1,0:T(8,128)(2,1)S(1)}, u32[]{:S(2)}, u32[]{:S(2)}) collective-permute-start(bf16[80,2048]{1,0:T(8,128)(2,1)} %constant_dynamic-slice_fusion), channel_id=1, source_target_pairs={{0,16},{16,0},{1,17},{17,1},{2,18},{18,2},{3,19},{19,3},{4,20},{20... | collective-permute-start | bytes 983048 | tf_op jit(solution)/shard_map/ppermute | solution.py:277
  14.2 12.6 %collective-permute-start.3 = (bf16[80,2048]{1,0:T(8,128)(2,1)S(1)}, bf16[80,2048]{1,0:T(8,128)(2,1)S(1)}, u32[]{:S(2)}, u32[]{:S(2)}) collective-permute-start(bf16[80,2048]{1,0:T(8,128)(2,1)S(1)} %collective-permute-done.refs_0_.refs_1_), channel_id=1, source_target_pairs={{0,2},{1,3},{2,0},{3,1},{4,6},{5,7},{6,4},{7,5},{8,10},{9,11},{10,... | collective-permute-start | bytes 983048 | tf_op jit(solution)/shard_map/ppermute | solution.py:280
  16.0 10.9 %collective-permute-start.4 = (bf16[80,2048]{1,0:T(8,128)(2,1)S(1)}, bf16[80,2048]{1,0:T(8,128)(2,1)S(1)}, u32[]{:S(2)}, u32[]{:S(2)}) collective-permute-start(bf16[80,2048]{1,0:T(8,128)(2,1)S(1)} %collective-permute-done.refs_0_.refs_1_), channel_id=1, source_target_pairs={{0,4},{1,5},{2,6},{3,7},{4,0},{5,1},{6,2},{7,3},{8,12},{9,13},{10,... | collective-permute-start | bytes 983048 | tf_op jit(solution)/shard_map/ppermute | solution.py:280
  22.8 4.1 %collective-permute-start.2 = (bf16[128,1152]{1,0:T(8,128)(2,1)S(1)}, bf16[128,1152]{1,0:T(8,128)(2,1)S(1)}, u32[]{:S(2)}, u32[]{:S(2)}) collective-permute-start(bf16[128,1152]{1,0:T(8,128)(2,1)S(1)} %bitcast.22), channel_id=1, source_target_pairs={{0,1},{1,0},{2,3},{3,2},{4,5},{5,4},{6,7},{7,6},{8,9},{9,8},{10,11... | collective-permute-start | bytes 884744 | tf_op jit(solution)/shard_map/ppermute | solution.py:280
  26.8 4.6 %copy-start = (f32[256,128]{1,0:T(8,128)}, f32[256,128]{1,0:T(8,128)S(1)}, u32[]{:S(2)}) copy-start(f32[256,128]{1,0:T(8,128)S(1)} %get-tuple-element.41.valid) | copy-start | bytes 393220
  26.9 12.4 %copy-start.2 = (f32[2048]{0:T(1024)S(1)}, f32[2048]{0:T(1024)}, u32[]{:S(2)}) copy-start(f32[2048]{0:T(1024)} %param.12) | copy-start | bytes 24580
  31.4 19.9 %all-to-all-start.1 = ((bf16[32,8,960]{2,1,0:T(8,128)(2,1)}), bf16[32,8,960]{2,1,0:T(8,128)(2,1)S(1)}, u32[]{:S(2)}, u32[]{:S(2)}) async-start(bf16[32,8,960]{2,1,0:T(8,128)(2,1)} %bitcast.26), calls=%async_computation.1 | async-start | bytes 1048576 | tf_op jit(solution)/shard_map/all_to_all | solution.py:388
  35.4 1.7 %collective-permute-start.10 = (bf16[80,2048]{1,0:T(8,128)(2,1)S(1)}, bf16[80,2048]{1,0:T(8,128)(2,1)S(1)}, u32[]{:S(2)}, u32[]{:S(2)}) collective-permute-start(bf16[80,2048]{1,0:T(8,128)(2,1)S(1)} %collective-permute-done.5.refs_4_), channel_id=1, source_target_pairs={{0,1},{1,0},{2,3},{3,2},{4,5},{5,4},{6,7},{7,6},{8,9},{9,8},{10,11... | collective-permute-start | bytes 983048 | tf_op jit(solution)/shard_map/ppermute | solution.py:280
  35.7 1.8 %collective-permute-start.7 = (bf16[80,2048]{1,0:T(8,128)(2,1)S(1)}, bf16[80,2048]{1,0:T(8,128)(2,1)S(1)}, u32[]{:S(2)}, u32[]{:S(2)}) collective-permute-start(bf16[80,2048]{1,0:T(8,128)(2,1)S(1)} %collective-permute-done.refs_0_.refs_1_), channel_id=1, source_target_pairs={{0,1},{1,0},{2,3},{3,2},{4,5},{5,4},{6,7},{7,6},{8,9},{9,8},{10,11... | collective-permute-start | bytes 983048 | tf_op jit(solution)/shard_map/ppermute | solution.py:280
  36.0 2.5 %collective-permute-start.8 = (bf16[80,2048]{1,0:T(8,128)(2,1)S(1)}, bf16[80,2048]{1,0:T(8,128)(2,1)S(1)}, u32[]{:S(2)}, u32[]{:S(2)}) collective-permute-start(bf16[80,2048]{1,0:T(8,128)(2,1)S(1)} %collective-permute-done.3.refs_2_), channel_id=1, source_target_pairs={{0,1},{1,0},{2,3},{3,2},{4,5},{5,4},{6,7},{7,6},{8,9},{9,8},{10,11... | collective-permute-start | bytes 983048 | tf_op jit(solution)/shard_map/ppermute | solution.py:280
  36.2 2.4 %collective-permute-start.9 = (bf16[80,2048]{1,0:T(8,128)(2,1)S(1)}, bf16[80,2048]{1,0:T(8,128)(2,1)}, u32[]{:S(2)}, u32[]{:S(2)}) collective-permute-start(bf16[80,2048]{1,0:T(8,128)(2,1)S(1)} %collective-permute-done.4.refs_3_), channel_id=1, source_target_pairs={{0,1},{1,0},{2,3},{3,2},{4,5},{5,4},{6,7},{7,6},{8,9},{9,8},{10,11... | collective-permute-start | bytes 983048 | tf_op jit(solution)/shard_map/ppermute | solution.py:280
  36.5 2.8 %collective-permute-start.6 = (bf16[256,640]{1,0:T(8,128)(2,1)}, bf16[256,640]{1,0:T(8,128)(2,1)}, u32[]{:S(2)}, u32[]{:S(2)}) collective-permute-start(bf16[256,640]{1,0:T(8,128)(2,1)} %get-tuple-element.40), channel_id=1, source_target_pairs={{0,1},{1,0},{2,3},{3,2},{4,5},{5,4},{6,7},{7,6},{8,9},{9,8},{10,11... | collective-permute-start | bytes 983048 | tf_op jit(solution)/shard_map/ppermute | solution.py:280
  39.3 0.9 %copy-start.1 = (f32[256,128]{1,0:T(8,128)S(1)}, f32[256,128]{1,0:T(8,128)}, u32[]{:S(2)}) copy-start(f32[256,128]{1,0:T(8,128)} %copy-done) | copy-start | bytes 393220

commit v6 on v5

--- a/solution.py
+++ b/solution.py
@@ -161,7 +161,7 @@
         ),
     ]
     fetch(loads)
-    place(offsets, heads, whole, len(heads))
+    place(offsets, heads, whole, len(heads), quarter)
     cots[rows:, :] = other_in[...]
     pooled[...], found = activate(share, arrived, kernel, bias, left, slopes)
     valid[...] = jnp.broadcast_to(jnp.sum(found, axis=1, keepdims=True), valid.shape)
@@ -176,25 +176,24 @@
     own_early[...] = mm(left[...], sloped(grads[:rows].astype(F32), slopes[:, :, 0:early]))
 
 
-def segments(offsets, weights, whole, groups):
-    quarter = whole.shape[0] // (groups + 1)
+def sloped(grads, slopes):
+    return jnp.concatenate([(grads * slopes[p]).astype(BF16) for p in range(2)], axis=0)
+
+
+def segments(offsets, weights, whole, groups, quarter, skip=0):
     unit = min(ref.shape[0] for ref in weights)
     out = []
     for n, ref in enumerate(weights):
-        start = pl.multiple_of(offsets[n], 16)
+        start = pl.multiple_of(offsets[n] - skip, 16)
         out.append((ref.at[pl.ds(0, unit)], whole.at[pl.ds(start, unit)]))
         if (more := ref.shape[0] - unit) > 0:
-            end = (n % groups + 2) * quarter
+            end = (n % groups + 2) * quarter - skip
             out.append((ref.at[pl.ds(unit, more)], whole.at[pl.ds(end - more, more)]))
     return out
 
 
-def sloped(grads, slopes):
-    return jnp.concatenate([(grads * slopes[p]).astype(BF16) for p in range(2)], axis=0)
-
-
-def place(offsets, weights, whole, groups):
-    for source, target in segments(offsets, weights, whole, groups):
+def place(*args):
+    for source, target in segments(*args):
         target[...] = source[...]
 
 
@@ -202,12 +201,14 @@
     ahead, refs = (refs[:2], refs[2:]) if early else ((), refs)
     weights, refs = refs[:-8], refs[-8:]
     sums_out, pooled_out, whole, sums, pooled, other_left, other_slopes, sems = refs
+    groups = len(weights) // 3
     rows = cots.shape[0] // 2
-    place(offsets, weights, whole, len(weights) // 3)
+    whole[...] = whole_in[early:, :]
+    place(offsets, weights, whole, groups, whole_in.shape[0] // (groups + 1), early)
     pooled[...], _ = activate(share, arrived, kernel, bias, other_left, other_slopes)
     stores = [pltpu.make_async_copy(pooled, pooled_out, sems.at[0])]
     stores[0].start()
-    weight = whole[early:, :]
+    weight = whole[...]
     grads = lax.dot_general(cots[:rows, :], weight, LAST, preferred_element_type=F32)
     grads = grads.astype(BF16).astype(F32)
     own = mm(left[...], sloped(grads, slopes[:, :, early:]))
@@ -236,7 +237,7 @@
         start = pl.multiple_of(bases[n], 16)
         loads.append((weights[0].at[pl.ds(start, quarter)], whole.at[n, pl.ds(0, quarter)]))
         foreign = weights[1 + n * count : 1 + (n + 1) * count]
-        loads += segments(offsets, foreign, whole.at[n], count // 4)
+        loads += segments(offsets, foreign, whole.at[n], count // 4, quarter)
     loads = [
         pltpu.make_async_copy(source, target, sems.at[i]) for i, (source, target) in enumerate(loads)
     ]
@@ -370,14 +371,14 @@
         scratch_shapes=[pltpu.SemaphoreType.DMA((2,))],
     )(base_in, early, arrived, kernel, bias, cot_own, cot_other, in_hbm(proj_weight), *heads)
 
-    sums, pooled_other, _ = call(
+    sums, pooled_other = call(
         functools.partial(backward_kernel, share, early_lanes),
-        [HBM(packet, BF16), HBM((rows, width), BF16), pltpu.VMEM((width, feats), BF16)],
+        [HBM(packet, BF16), HBM((rows, width), BF16)],
         "backward",
         in_specs=[smem, smem] + [vmem] * (7 + len(ahead) + len(late_weights)),
-        out_specs=[hbm, hbm, vmem],
-        input_output_aliases={3: 2},
+        out_specs=[hbm, hbm],
         scratch_shapes=[
+            pltpu.VMEM((width - early_lanes, feats), BF16),
             pltpu.VMEM(packet, BF16),
             pltpu.VMEM((rows, width), BF16),
             pltpu.VMEM((depth, 2 * rows), BF16),

time: 52.5 us -> 52.7 us (level)
  no operation moved by 1% of the time
where the time goes in v6:
time: 52.7 us; the launch traced here: 52.2 us
  starting transfers between devices  18.2 us (35%)
  Pallas kernels  17.1 us (32%)
  waiting for transfers between devices  11.5 us (22%)
  local copies, waits for them, and re-layouts  4.12 us (8%)
  between operations  0.85 us (2%)
  other arithmetic  0.53 us (1%)
    all_to_all x1, starting transfers between devices, body(): lax.all_to_all(packed.reshape(owners, high, -1), 'seq', split_axis=0, con...  5.91 us
    pallas_call x1, Pallas kernels, body(): call(functools.partial(merge_kernel, quarter), HBM((rows, feats), BF16),...  5.8 us
    all_to_all x1, waiting for transfers between devices, body(): lax.all_to_all(sums.reshape((recs * owners, -1, packet[-1])), ('dp', 'seq...  5.28 us
    ppermute x9, starting transfers between devices, swap(): return lax.ppermute(x, 'seq', [(i, i ^ bit) for i in range(owners)])  5.18 us
    pallas_call x1, Pallas kernels, body(): call(functools.partial(backward_kernel, share, early_lanes), [HBM(packet,...  4.63 us
    all_to_all x1, starting transfers between devices, body(): lax.all_to_all(sums.reshape((recs * owners, -1, packet[-1])), ('dp', 'seq...  3.96 us
    pallas_call x1, Pallas kernels, body(): call(functools.partial(prepare_kernel, share), [pltpu.VMEM((2 * rows, fea...  3.87 us
    all_to_all x1, waiting for transfers between devices, body(): lax.all_to_all(packed.reshape(owners, high, -1), 'seq', split_axis=0, con...  3.63 us
  transfers between devices with their start and end apart: 13, of which 8 were waited for; matrix products, arithmetic and copies ran while one was open for 7% of the time, Pallas kernels for 19%

profile of v6, /device:TPU:0, one launch (start us, length us, event | category | flops | bytes accessed | tf_op | source)
XLA Modules:
  0.0 52.2 jit_solution(18200683984462463757)
XLA Ops:
  0.7 2.0 %pack_patches.1 = (bf16[128,1152]{1,0:T(8,128)(2,1)}, bf16[80,2048]{1,0:T(8,128)(2,1)S(1)}) custom-call(s32[1]{0:T(128)} %bitcast.7.cuts, bf16[256,128]{1,0:T(8,128)(2,1)} %bitcast.29, s32[1,128]{1,0:T(1,128)} %spots_hbm.1, bf16[640,2048]{1,0:T(8,128)(2,1)} %refs_0_.1), custom_call_target="tpu_custom_call" | custom-call | flops 1000000000 | tf_op jit(solution)/shard_map/pack_patches/pallas_call | solution.py:306
  2.7 0.5 collective-permute-start.1
  3.2 2.6 %collective-permute-start = (bf16[80,2048]{1,0:T(8,128)(2,1)S(1)}, bf16[80,2048]{1,0:T(8,128)(2,1)S(1)}, u32[]{:S(2)}, u32[]{:S(2)}) collective-permute-start(bf16[80,2048]{1,0:T(8,128)(2,1)S(1)} %get-tuple-element.24), channel_id=1, source_target_pairs={{0,16},{16,0},{1,17},{17,1},{2,18},{18,2},{3,19},{19,3},{4,20},{20... | collective-permute-start | bytes 983048 | tf_op jit(solution)/shard_map/ppermute | solution.py:278
  5.8 5.9 %all-to-all-start = ((bf16[16,8,1152]{2,1,0:T(8,128)(2,1)}), bf16[16,8,1152]{2,1,0:T(8,128)(2,1)S(1)}, u32[]{:S(2)}, u32[]{:S(2)}) async-start(bf16[16,8,1152]{2,1,0:T(8,128)(2,1)} %bitcast.28), calls=%async_computation | async-start | bytes 589824 | tf_op jit(solution)/shard_map/all_to_all | solution.py:334
  11.8 1.7 %constant_dynamic-slice_fusion = bf16[80,2048]{1,0:T(8,128)(2,1)} fusion(bf16[640,2048]{1,0:T(8,128)(2,1)} %refs_0_.1, s32[]{:T(128)S(6)} %select_n.50), kind=kLoop, calls=%fused_computation.2 | loop fusion | bytes 655364 | tf_op jit(solution)/shard_map/dynamic_slice | solution.py:325
  13.5 0.5 %collective-permute-start.5 = (bf16[80,2048]{1,0:T(8,128)(2,1)}, bf16[80,2048]{1,0:T(8,128)(2,1)S(1)}, u32[]{:S(2)}, u32[]{:S(2)}) collective-permute-start(bf16[80,2048]{1,0:T(8,128)(2,1)} %constant_dynamic-slice_fusion), channel_id=1, source_target_pairs={{0,16},{16,0},{1,17},{17,1},{2,18},{18,2},{3,19},{19,3},{4,20},{20... | collective-permute-start | bytes 983048 | tf_op jit(solution)/shard_map/ppermute | solution.py:278
  14.2 1.8 %collective-permute-start.3 = (bf16[80,2048]{1,0:T(8,128)(2,1)S(1)}, bf16[80,2048]{1,0:T(8,128)(2,1)S(1)}, u32[]{:S(2)}, u32[]{:S(2)}) collective-permute-start(bf16[80,2048]{1,0:T(8,128)(2,1)S(1)} %collective-permute-done.refs_0_.refs_1_), channel_id=1, source_target_pairs={{0,2},{1,3},{2,0},{3,1},{4,6},{5,7},{6,4},{7,5},{8,10},{9,11},{10,... | collective-permute-start | bytes 983048 | tf_op jit(solution)/shard_map/ppermute | solution.py:281
  16.0 1.5 %collective-permute-start.4 = (bf16[80,2048]{1,0:T(8,128)(2,1)S(1)}, bf16[80,2048]{1,0:T(8,128)(2,1)S(1)}, u32[]{:S(2)}, u32[]{:S(2)}) collective-permute-start(bf16[80,2048]{1,0:T(8,128)(2,1)S(1)} %collective-permute-done.refs_0_.refs_1_), channel_id=1, source_target_pairs={{0,4},{1,5},{2,6},{3,7},{4,0},{5,1},{6,2},{7,3},{8,12},{9,13},{10,... | collective-permute-start | bytes 983048 | tf_op jit(solution)/shard_map/ppermute | solution.py:281
  17.6 1.4 %constant_dynamic-slice_fusion.2 = (bf16[384,320]{1,0:T(8,128)(2,1)S(1)}, bf16[384,320]{1,0:T(8,128)(2,1)S(1)}) fusion(bf16[384,1280]{1,0:T(8,128)(2,1)} %bitcast.27, s32[]{:T(128)S(6)} %select_n.48, s32[]{:T(128)S(6)} %select_n.49), kind=kLoop, calls=%fused_computation.4 | loop fusion | bytes 983048 | tf_op jit(solution)/shard_map/dynamic_slice | solution.py:340
  19.2 3.6 %all-to-all-done = bf16[16,8,1152]{2,1,0:T(8,128)(2,1)S(1)} async-done(((bf16[16,8,1152]{2,1,0:T(8,128)(2,1)}), bf16[16,8,1152]{2,1,0:T(8,128)(2,1)S(1)}, u32[]{:S(2)}, u32[]{:S(2)}) %all-to-all-start) | async-done | bytes 294944 | tf_op jit(solution)/shard_map/all_to_all | solution.py:334
  23.0 3.9 %prepare.1 = (bf16[512,2048]{1,0:T(8,128)(2,1)S(1)}, bf16[640,2048]{1,0:T(8,128)(2,1)S(1)}, bf16[384,512]{1,0:T(8,128)(2,1)S(1)}, f32[2,256,640]{2,1,0:T(8,128)S...) custom-call(s32[1]{0:T(128)} %bitcast.5.base, ...), custom_call_target="tpu_custom_call" | custom-call | flops 1000000000 | tf_op jit(solution)/shard_map/prepare/pallas_call | solution.py:353
  26.9 4.6 %backward.1 = (bf16[2,16,8,960]{3,2,1,0:T(8,128)(2,1)}, bf16[256,640]{1,0:T(8,128)(2,1)}) custom-call(s32[3]{0:T(128)S(1)} %pad_add_fusion.offsets, s32[2]{0:T(128)S(1)} %pad_add_fusion.1.halves, bf16[512,2048]{1,0:T(8,128)(2,1)S(1)} %get-tuple-element.31.cots, bf16[640,2048]{1,0:T(8,128)(2,1)S(1)} %get-tuple-element.32.whole_in, ...), custom_call_target="tpu_custom_call" | custom-call | flops 1000000000 | tf_op jit(solution)/shard_map/backward/pallas_call | solution.py:374
  31.6 4.0 %all-to-all-start.1 = ((bf16[32,8,960]{2,1,0:T(8,128)(2,1)}), bf16[32,8,960]{2,1,0:T(8,128)(2,1)S(1)}, u32[]{:S(2)}, u32[]{:S(2)}) async-start(bf16[32,8,960]{2,1,0:T(8,128)(2,1)} %bitcast.26), calls=%async_computation.1 | async-start | bytes 1048576 | tf_op jit(solution)/shard_map/all_to_all | solution.py:389
  35.5 0.3 collective-permute-start.10
  35.8 0.3 collective-permute-start.7
  36.1 0.3 collective-permute-start.8
  36.3 0.3 collective-permute-start.9
  37.2 0.5 collective-permute-done.7.refs_5_
  37.7 0.9 %collective-permute-done.8.refs_6_ = bf16[80,2048]{1,0:T(8,128)(2,1)S(1)} collective-permute-done((bf16[80,2048]{1,0:T(8,128)(2,1)S(1)}, bf16[80,2048]{1,0:T(8,128)(2,1)S(1)}, u32[]{:S(2)}, u32[]{:S(2)}) %collective-permute-start.8) | collective-permute-done | bytes 327712 | tf_op jit(solution)/shard_map/ppermute | solution.py:281
  38.8 0.7 %collective-permute-done.6.other = bf16[256,640]{1,0:T(8,128)(2,1)} collective-permute-done((bf16[256,640]{1,0:T(8,128)(2,1)}, bf16[256,640]{1,0:T(8,128)(2,1)}, u32[]{:S(2)}, u32[]{:S(2)}) %collective-permute-start.6) | collective-permute-done | bytes 327712 | tf_op jit(solution)/shard_map/ppermute | solution.py:281
  39.4 0.9 %copy-done.1 = f32[256,128]{1,0:T(8,128)S(1)} copy-done((f32[256,128]{1,0:T(8,128)S(1)}, f32[256,128]{1,0:T(8,128)}, u32[]{:S(2)}) %copy-start.1) | copy-done | bytes 131096
  40.3 5.8 %merge.1 = bf16[256,2048]{1,0:T(8,128)(2,1)} custom-call(s32[2]{0:T(128)S(1)} %pad_add_fusion.2.bases, s32[4]{0:T(128)S(1)} %pad_add_fusion.3.offsets, bf16[256,640]{1,0:T(8,128)(2,1)S(1)} %get-tuple-element.39.pooled, bf16[256,640]{1,0:T(8,128)(2,1)} %collective-permute-done.6.other, f32[256,128]{1,0:T(8,128)S(1)} %copy-done.1, f32[1,2048]{1,0:T(1,128)S(1)} %bitcast.24, ...), custom_call_target="tpu_custom_call" | custom-call | flops 1000000000 | tf_op jit(solution)/shard_map/merge/pallas_call | solution.py:397
  46.2 5.3 %all-to-all-done.1.pieces = bf16[32,8,960]{2,1,0:T(8,128)(2,1)S(1)} async-done(((bf16[32,8,960]{2,1,0:T(8,128)(2,1)}), bf16[32,8,960]{2,1,0:T(8,128)(2,1)S(1)}, u32[]{:S(2)}, u32[]{:S(2)}) %all-to-all-start.1) | async-done | bytes 491552 | tf_op jit(solution)/shard_map/all_to_all | solution.py:389
  51.4 0.8 %sum_pieces.1 = f32[24,640]{1,0:T(8,128)} custom-call(bf16[32,8,960]{2,1,0:T(8,128)(2,1)S(1)} %all-to-all-done.1.pieces), custom_call_target="tpu_custom_call" | custom-call | flops 1000000000 | tf_op jit(solution)/shard_map/sum_pieces/pallas_call | solution.py:418
  (26 shorter events, 1.3 us)
Async XLA Ops:
  0.6 13.5 %copy-start.3 = (f32[1280]{0:T(1024)S(1)}, f32[1280]{0:T(1024)}, u32[]{:S(2)}) copy-start(f32[1280]{0:T(1024)} %param.10) | copy-start | bytes 15364
  2.7 20.2 %collective-permute-start.1 = (bf16[256,2048]{1,0:T(8,128)(2,1)}, bf16[256,2048]{1,0:T(8,128)(2,1)S(1)}, u32[]{:S(2)}, u32[]{:S(2)}) collective-permute-start(bf16[256,2048]{1,0:T(8,128)(2,1)} %bitcast.14.own_in), channel_id=1, source_target_pairs={{0,1},{1,0},{2,3},{3,2},{4,5},{5,4},{6,7},{7,6},{8,9},{9,8},{10,11... | collective-permute-start | bytes 3145736 | tf_op jit(solution)/shard_map/ppermute | solution.py:281
  3.2 10.9 %collective-permute-start = (bf16[80,2048]{1,0:T(8,128)(2,1)S(1)}, bf16[80,2048]{1,0:T(8,128)(2,1)S(1)}, u32[]{:S(2)}, u32[]{:S(2)}) collective-permute-start(bf16[80,2048]{1,0:T(8,128)(2,1)S(1)} %get-tuple-element.24), channel_id=1, source_target_pairs={{0,16},{16,0},{1,17},{17,1},{2,18},{18,2},{3,19},{19,3},{4,20},{20... | collective-permute-start | bytes 983048 | tf_op jit(solution)/shard_map/ppermute | solution.py:278
  5.8 17.0 %all-to-all-start = ((bf16[16,8,1152]{2,1,0:T(8,128)(2,1)}), bf16[16,8,1152]{2,1,0:T(8,128)(2,1)S(1)}, u32[]{:S(2)}, u32[]{:S(2)}) async-start(bf16[16,8,1152]{2,1,0:T(8,128)(2,1)} %bitcast.28), calls=%async_computation | async-start | bytes 589824 | tf_op jit(solution)/shard_map/all_to_all | solution.py:334
  13.5 13.4 %collective-permute-start.5 = (bf16[80,2048]{1,0:T(8,128)(2,1)}, bf16[80,2048]{1,0:T(8,128)(2,1)S(1)}, u32[]{:S(2)}, u32[]{:S(2)}) collective-permute-start(bf16[80,2048]{1,0:T(8,128)(2,1)} %constant_dynamic-slice_fusion), channel_id=1, source_target_pairs={{0,16},{16,0},{1,17},{17,1},{2,18},{18,2},{3,19},{19,3},{4,20},{20... | collective-permute-start | bytes 983048 | tf_op jit(solution)/shard_map/ppermute | solution.py:278
  14.2 12.6 %collective-permute-start.3 = (bf16[80,2048]{1,0:T(8,128)(2,1)S(1)}, bf16[80,2048]{1,0:T(8,128)(2,1)S(1)}, u32[]{:S(2)}, u32[]{:S(2)}) collective-permute-start(bf16[80,2048]{1,0:T(8,128)(2,1)S(1)} %collective-permute-done.refs_0_.refs_1_), channel_id=1, source_target_pairs={{0,2},{1,3},{2,0},{3,1},{4,6},{5,7},{6,4},{7,5},{8,10},{9,11},{10,... | collective-permute-start | bytes 983048 | tf_op jit(solution)/shard_map/ppermute | solution.py:281
  16.0 10.9 %collective-permute-start.4 = (bf16[80,2048]{1,0:T(8,128)(2,1)S(1)}, bf16[80,2048]{1,0:T(8,128)(2,1)S(1)}, u32[]{:S(2)}, u32[]{:S(2)}) collective-permute-start(bf16[80,2048]{1,0:T(8,128)(2,1)S(1)} %collective-permute-done.refs_0_.refs_1_), channel_id=1, source_target_pairs={{0,4},{1,5},{2,6},{3,7},{4,0},{5,1},{6,2},{7,3},{8,12},{9,13},{10,... | collective-permute-start | bytes 983048 | tf_op jit(solution)/shard_map/ppermute | solution.py:281
  22.8 4.1 %collective-permute-start.2 = (bf16[128,1152]{1,0:T(8,128)(2,1)S(1)}, bf16[128,1152]{1,0:T(8,128)(2,1)S(1)}, u32[]{:S(2)}, u32[]{:S(2)}) collective-permute-start(bf16[128,1152]{1,0:T(8,128)(2,1)S(1)} %bitcast.22), channel_id=1, source_target_pairs={{0,1},{1,0},{2,3},{3,2},{4,5},{5,4},{6,7},{7,6},{8,9},{9,8},{10,11... | collective-permute-start | bytes 884744 | tf_op jit(solution)/shard_map/ppermute | solution.py:281
  26.8 4.7 %copy-start = (f32[256,128]{1,0:T(8,128)}, f32[256,128]{1,0:T(8,128)S(1)}, u32[]{:S(2)}) copy-start(f32[256,128]{1,0:T(8,128)S(1)} %get-tuple-element.41.valid) | copy-start | bytes 393220
  26.9 12.5 %copy-start.2 = (f32[2048]{0:T(1024)S(1)}, f32[2048]{0:T(1024)}, u32[]{:S(2)}) copy-start(f32[2048]{0:T(1024)} %param.12) | copy-start | bytes 24580
  31.6 19.9 %all-to-all-start.1 = ((bf16[32,8,960]{2,1,0:T(8,128)(2,1)}), bf16[32,8,960]{2,1,0:T(8,128)(2,1)S(1)}, u32[]{:S(2)}, u32[]{:S(2)}) async-start(bf16[32,8,960]{2,1,0:T(8,128)(2,1)} %bitcast.26), calls=%async_computation.1 | async-start | bytes 1048576 | tf_op jit(solution)/shard_map/all_to_all | solution.py:389
  35.5 1.7 %collective-permute-start.10 = (bf16[80,2048]{1,0:T(8,128)(2,1)S(1)}, bf16[80,2048]{1,0:T(8,128)(2,1)S(1)}, u32[]{:S(2)}, u32[]{:S(2)}) collective-permute-start(bf16[80,2048]{1,0:T(8,128)(2,1)S(1)} %collective-permute-done.5.refs_4_), channel_id=1, source_target_pairs={{0,1},{1,0},{2,3},{3,2},{4,5},{5,4},{6,7},{7,6},{8,9},{9,8},{10,11... | collective-permute-start | bytes 983048 | tf_op jit(solution)/shard_map/ppermute | solution.py:281
  35.8 1.8 %collective-permute-start.7 = (bf16[80,2048]{1,0:T(8,128)(2,1)S(1)}, bf16[80,2048]{1,0:T(8,128)(2,1)S(1)}, u32[]{:S(2)}, u32[]{:S(2)}) collective-permute-start(bf16[80,2048]{1,0:T(8,128)(2,1)S(1)} %collective-permute-done.refs_0_.refs_1_), channel_id=1, source_target_pairs={{0,1},{1,0},{2,3},{3,2},{4,5},{5,4},{6,7},{7,6},{8,9},{9,8},{10,11... | collective-permute-start | bytes 983048 | tf_op jit(solution)/shard_map/ppermute | solution.py:281
  36.1 2.5 %collective-permute-start.8 = (bf16[80,2048]{1,0:T(8,128)(2,1)S(1)}, bf16[80,2048]{1,0:T(8,128)(2,1)S(1)}, u32[]{:S(2)}, u32[]{:S(2)}) collective-permute-start(bf16[80,2048]{1,0:T(8,128)(2,1)S(1)} %collective-permute-done.3.refs_2_), channel_id=1, source_target_pairs={{0,1},{1,0},{2,3},{3,2},{4,5},{5,4},{6,7},{7,6},{8,9},{9,8},{10,11... | collective-permute-start | bytes 983048 | tf_op jit(solution)/shard_map/ppermute | solution.py:281
  36.3 2.4 %collective-permute-start.9 = (bf16[80,2048]{1,0:T(8,128)(2,1)S(1)}, bf16[80,2048]{1,0:T(8,128)(2,1)}, u32[]{:S(2)}, u32[]{:S(2)}) collective-permute-start(bf16[80,2048]{1,0:T(8,128)(2,1)S(1)} %collective-permute-done.4.refs_3_), channel_id=1, source_target_pairs={{0,1},{1,0},{2,3},{3,2},{4,5},{5,4},{6,7},{7,6},{8,9},{9,8},{10,11... | collective-permute-start | bytes 983048 | tf_op jit(solution)/shard_map/ppermute | solution.py:281
  36.6 2.8 %collective-permute-start.6 = (bf16[256,640]{1,0:T(8,128)(2,1)}, bf16[256,640]{1,0:T(8,128)(2,1)}, u32[]{:S(2)}, u32[]{:S(2)}) collective-permute-start(bf16[256,640]{1,0:T(8,128)(2,1)} %get-tuple-element.40), channel_id=1, source_target_pairs={{0,1},{1,0},{2,3},{3,2},{4,5},{5,4},{6,7},{7,6},{8,9},{9,8},{10,11... | collective-permute-start | bytes 983048 | tf_op jit(solution)/shard_map/ppermute | solution.py:281
  39.4 0.9 %copy-start.1 = (f32[256,128]{1,0:T(8,128)S(1)}, f32[256,128]{1,0:T(8,128)}, u32[]{:S(2)}) copy-start(f32[256,128]{1,0:T(8,128)} %copy-done) | copy-start | bytes 393220

commit v7 on v6

--- a/solution.py
+++ b/solution.py
@@ -49,7 +49,7 @@
         copy.wait()
 
 
-def pack_kernel(owners, capacity, rows_own, cuts, mel_hbm, spots_hbm, weight, out, head, mel_ref, spots_ref, sems):
+def pack_kernel(owners, capacity, rows_own, cuts, mel_hbm, spots_hbm, weight, out_hbm, head, out, mel_ref, spots_ref, sems):
     loads = [
         pltpu.make_async_copy(spots_hbm, spots_ref, sems.at[0]),
         pltpu.make_async_copy(mel_hbm, mel_ref, sems.at[1]),
@@ -87,7 +87,10 @@
         places = jnp.where(lane == g, spot, places)
         out[:, g * width : (g + 1) * width] = mm(onehot.astype(BF16), patch).astype(BF16)
     out[:, capacity // high * width :] = places.astype(BF16)
+    store = pltpu.make_async_copy(out, out_hbm, sems.at[3])
+    store.start()
     rows.wait()
+    store.wait()
 
 
 def rows_from_slots(arrived, rows, mel):
@@ -170,10 +173,14 @@
         return
     own_early, other_early = ahead
     early = own_early.shape[1]
-    grads = lax.dot_general(cots[...], whole[0:early, :], LAST, preferred_element_type=F32)
-    grads = grads.astype(BF16)
-    other_early[...] = grads[rows:]
-    own_early[...] = mm(left[...], sloped(grads[:rows].astype(F32), slopes[:, :, 0:early]))
+    for n in range(2):
+        cot = cots[n * rows : (n + 1) * rows, :]
+        grads = lax.dot_general(cot, whole[0:early, :], LAST, preferred_element_type=F32)
+        grads = grads.astype(BF16)
+        if n:
+            other_early[...] = grads
+        else:
+            own_early[...] = mm(left[...], sloped(grads.astype(F32), slopes[:, :, 0:early]))
 
 
 def sloped(grads, slopes):
@@ -262,7 +269,7 @@
 def body(mel_frames, positions, conv_weight, conv_bias, proj_weight, proj_bias, cotangent):
     recs, owners = lax.axis_size("dp"), lax.axis_size("seq")
     dp_index, seq_index = lax.axis_index("dp"), lax.axis_index("seq")
-    core, side = seq_index % 2, (seq_index // 2) % 2
+    core, side = seq_index % 2, (seq_index // 4) % 2
     frames, mel = mel_frames.shape[1:]
     toks = positions.shape[1]
     rows, feats = cotangent.shape[1:]
@@ -280,16 +287,16 @@
     def swap(x, bit):
         return lax.ppermute(x, "seq", [(i, i ^ bit) for i in range(owners)])
 
-    bit = (seq_index // 4) % 2
+    bit = (seq_index // 2) % 2
     unit = quarter // 64 * 16
     base = core * quarter
     part = (bit * 2 + side) * unit
-    part_x = (bit * 2 + 1 - side) * unit
-    part_z = ((1 - bit) * 2 + side) * unit
+    part_z = (bit * 2 + 1 - side) * unit
+    part_x = ((1 - bit) * 2 + side) * unit
     part_far = ((1 - bit) * 2 + 1 - side) * unit
     cuts = (base + part).reshape(1).astype(I32)
     early = jnp.stack([(j + 1) * quarter + part for j in range(recs - 1)]).astype(I32)
-    late = [(j + 1) * quarter + p for p in (part_x, part_z, part_far) for j in range(recs - 1)]
+    late = [(j + 1) * quarter + p for p in (part_z, part_x, part_far) for j in range(recs - 1)]
     late = jnp.stack(late).astype(I32)
     offsets = jnp.concatenate([early, late])
     base_in = base.reshape(1).astype(I32)
@@ -311,23 +318,24 @@
         ],
         "pack_patches",
         in_specs=[smem, hbm, hbm, hbm],
-        out_specs=[vmem] * 2,
+        out_specs=[hbm, vmem],
         scratch_shapes=[
+            pltpu.VMEM((slots, wide_slots), BF16),
             pltpu.VMEM((frames, mel), BF16),
             pltpu.VMEM((1, toks), I32),
-            pltpu.SemaphoreType.DMA((3,)),
+            pltpu.SemaphoreType.DMA((4,)),
         ],
     )(cuts, in_hbm(mel_frames[0]), in_hbm(positions), in_hbm(proj_weight))
     heads = [shift(head, j) for j in range(1, recs)]
+    by_z = [swap(h, 4) for h in heads]
     by_x = [swap(h, 2) for h in heads]
-    by_z = [swap(h, 4) for h in heads]
     weight_in, _ = lax.optimization_barrier((proj_weight, packed))
     far = lax.dynamic_slice_in_dim(weight_in, base + part_far, unit, 0)
     if extra := quarter - 4 * unit:
         last = lax.dynamic_slice_in_dim(weight_in, base + 4 * unit, extra, 0)
         far = jnp.concatenate([far, last], axis=0)
     cot_in, _ = lax.optimization_barrier((cotangent[0], packed))
-    late_weights = by_x + by_z + [shift(far, j) for j in range(1, recs)]
+    late_weights = by_z + by_x + [shift(far, j) for j in range(1, recs)]
     cot_own = in_hbm(cot_in)
     cot_other = swap(cot_in, 1)
 

time: 52.7 us -> 52.7 us (level)
  Pallas kernels: 17.1 us -> 16.4 us
    pallas_call x1, Pallas kernels: 3.87 us -> 3.24 us  [body(): call(functools.partial(prepare_kernel, share), [pltpu.VMEM((2 * rows, fea...]
  transfers between devices with their start and end apart: 13 -> 13, of which waited for: 8 -> 9; matrix products, arithmetic and copies ran while one was open for 7% -> 7% of each run, Pallas kernels for 19% -> 17%
where the time goes in v7:
time: 52.7 us; the launch traced here: 52.2 us
  starting transfers between devices  18.4 us (35%)
  Pallas kernels  16.4 us (31%)
  waiting for transfers between devices  11.9 us (23%)
  local copies, waits for them, and re-layouts  4.11 us (8%)
  between operations  0.82 us (2%)
  other arithmetic  0.53 us (1%)
    all_to_all x1, starting transfers between devices, body(): lax.all_to_all(packed.reshape(owners, high, -1), 'seq', split_axis=0, con...  5.91 us
    pallas_call x1, Pallas kernels, body(): call(functools.partial(merge_kernel, quarter), HBM((rows, feats), BF16),...  5.8 us
    all_to_all x1, waiting for transfers between devices, body(): lax.all_to_all(sums.reshape((recs * owners, -1, packet[-1])), ('dp', 'seq...  5.28 us
    ppermute x9, starting transfers between devices, swap(): return lax.ppermute(x, 'seq', [(i, i ^ bit) for i in range(owners)])  5.18 us
    pallas_call x1, Pallas kernels, body(): call(functools.partial(backward_kernel, share, early_lanes), [HBM(packet,...  4.62 us
    all_to_all x1, starting transfers between devices, body(): lax.all_to_all(sums.reshape((recs * owners, -1, packet[-1])), ('dp', 'seq...  4.19 us
    all_to_all x1, waiting for transfers between devices, body(): lax.all_to_all(packed.reshape(owners, high, -1), 'seq', split_axis=0, con...  3.63 us
    pallas_call x1, Pallas kernels, body(): call(functools.partial(prepare_kernel, share), [pltpu.VMEM((2 * rows, fea...  3.24 us
  transfers between devices with their start and end apart: 13, of which 9 were waited for; matrix products, arithmetic and copies ran while one was open for 7% of the time, Pallas kernels for 17%

profile of v7, /device:TPU:0, one launch (start us, length us, event | category | flops | bytes accessed | tf_op | source)
XLA Modules:
  0.0 52.2 jit_solution(1498034275437735537)
XLA Ops:
  0.7 2.0 %pack_patches.1 = (bf16[128,1152]{1,0:T(8,128)(2,1)}, bf16[80,2048]{1,0:T(8,128)(2,1)S(1)}) custom-call(s32[1]{0:T(128)} %bitcast.7.cuts, bf16[256,128]{1,0:T(8,128)(2,1)} %bitcast.29, s32[1,128]{1,0:T(1,128)} %spots_hbm.1, bf16[640,2048]{1,0:T(8,128)(2,1)} %refs_0_.1), custom_call_target="tpu_custom_call" | custom-call | flops 1000000000 | tf_op jit(solution)/shard_map/pack_patches/pallas_call | solution.py:313
  2.7 0.5 collective-permute-start.1
  3.3 2.6 %collective-permute-start = (bf16[80,2048]{1,0:T(8,128)(2,1)S(1)}, bf16[80,2048]{1,0:T(8,128)(2,1)S(1)}, u32[]{:S(2)}, u32[]{:S(2)}) collective-permute-start(bf16[80,2048]{1,0:T(8,128)(2,1)S(1)} %get-tuple-element.24), channel_id=1, source_target_pairs={{0,16},{16,0},{1,17},{17,1},{2,18},{18,2},{3,19},{19,3},{4,20},{20... | collective-permute-start | bytes 983048 | tf_op jit(solution)/shard_map/ppermute | solution.py:285
  5.8 5.9 %all-to-all-start = ((bf16[16,8,1152]{2,1,0:T(8,128)(2,1)}), bf16[16,8,1152]{2,1,0:T(8,128)(2,1)S(1)}, u32[]{:S(2)}, u32[]{:S(2)}) async-start(bf16[16,8,1152]{2,1,0:T(8,128)(2,1)} %bitcast.28), calls=%async_computation | async-start | bytes 589824 | tf_op jit(solution)/shard_map/all_to_all | solution.py:342
  11.8 1.7 %constant_dynamic-slice_fusion = bf16[80,2048]{1,0:T(8,128)(2,1)} fusion(bf16[640,2048]{1,0:T(8,128)(2,1)} %refs_0_.1, s32[]{:T(128)S(6)} %select_n.50), kind=kLoop, calls=%fused_computation.2 | loop fusion | bytes 655364 | tf_op jit(solution)/shard_map/dynamic_slice | solution.py:333
  13.5 0.5 %collective-permute-start.5 = (bf16[80,2048]{1,0:T(8,128)(2,1)}, bf16[80,2048]{1,0:T(8,128)(2,1)S(1)}, u32[]{:S(2)}, u32[]{:S(2)}) collective-permute-start(bf16[80,2048]{1,0:T(8,128)(2,1)} %constant_dynamic-slice_fusion), channel_id=1, source_target_pairs={{0,16},{16,0},{1,17},{17,1},{2,18},{18,2},{3,19},{19,3},{4,20},{20... | collective-permute-start | bytes 983048 | tf_op jit(solution)/shard_map/ppermute | solution.py:285
  14.2 1.8 %collective-permute-start.3 = (bf16[80,2048]{1,0:T(8,128)(2,1)S(1)}, bf16[80,2048]{1,0:T(8,128)(2,1)S(1)}, u32[]{:S(2)}, u32[]{:S(2)}) collective-permute-start(bf16[80,2048]{1,0:T(8,128)(2,1)S(1)} %collective-permute-done.refs_0_.refs_1_), channel_id=1, source_target_pairs={{0,4},{1,5},{2,6},{3,7},{4,0},{5,1},{6,2},{7,3},{8,12},{9,13},{10,... | collective-permute-start | bytes 983048 | tf_op jit(solution)/shard_map/ppermute | solution.py:288
  16.1 1.5 %collective-permute-start.4 = (bf16[80,2048]{1,0:T(8,128)(2,1)S(1)}, bf16[80,2048]{1,0:T(8,128)(2,1)S(1)}, u32[]{:S(2)}, u32[]{:S(2)}) collective-permute-start(bf16[80,2048]{1,0:T(8,128)(2,1)S(1)} %collective-permute-done.refs_0_.refs_1_), channel_id=1, source_target_pairs={{0,2},{1,3},{2,0},{3,1},{4,6},{5,7},{6,4},{7,5},{8,10},{9,11},{10,... | collective-permute-start | bytes 983048 | tf_op jit(solution)/shard_map/ppermute | solution.py:288
  17.6 1.4 %constant_dynamic-slice_fusion.2 = (bf16[384,320]{1,0:T(8,128)(2,1)S(1)}, bf16[384,320]{1,0:T(8,128)(2,1)S(1)}) fusion(bf16[384,1280]{1,0:T(8,128)(2,1)} %bitcast.27, s32[]{:T(128)S(6)} %select_n.48, s32[]{:T(128)S(6)} %select_n.49), kind=kLoop, calls=%fused_computation.4 | loop fusion | bytes 983048 | tf_op jit(solution)/shard_map/dynamic_slice | solution.py:348
  19.2 3.6 %all-to-all-done = bf16[16,8,1152]{2,1,0:T(8,128)(2,1)S(1)} async-done(((bf16[16,8,1152]{2,1,0:T(8,128)(2,1)}), bf16[16,8,1152]{2,1,0:T(8,128)(2,1)S(1)}, u32[]{:S(2)}, u32[]{:S(2)}) %all-to-all-start) | async-done | bytes 294944 | tf_op jit(solution)/shard_map/all_to_all | solution.py:342
  23.0 3.2 %prepare.1 = (bf16[512,2048]{1,0:T(8,128)(2,1)S(1)}, bf16[640,2048]{1,0:T(8,128)(2,1)S(1)}, bf16[384,512]{1,0:T(8,128)(2,1)S(1)}, f32[2,256,640]{2,1,0:T(8,128)S...) custom-call(s32[1]{0:T(128)} %bitcast.5.base, ...), custom_call_target="tpu_custom_call" | custom-call | flops 1000000000 | tf_op jit(solution)/shard_map/prepare/pallas_call | solution.py:361
  26.2 0.4 collective-permute-done.3.refs_2_
  26.7 4.6 %backward.1 = (bf16[2,16,8,960]{3,2,1,0:T(8,128)(2,1)}, bf16[256,640]{1,0:T(8,128)(2,1)}) custom-call(s32[3]{0:T(128)S(1)} %pad_add_fusion.offsets, s32[2]{0:T(128)S(1)} %pad_add_fusion.1.halves, bf16[512,2048]{1,0:T(8,128)(2,1)S(1)} %get-tuple-element.31.cots, bf16[640,2048]{1,0:T(8,128)(2,1)S(1)} %get-tuple-element.32.whole_in, ...), custom_call_target="tpu_custom_call" | custom-call | flops 1000000000 | tf_op jit(solution)/shard_map/backward/pallas_call | solution.py:382
  31.3 4.2 %all-to-all-start.1 = ((bf16[32,8,960]{2,1,0:T(8,128)(2,1)}), bf16[32,8,960]{2,1,0:T(8,128)(2,1)S(1)}, u32[]{:S(2)}, u32[]{:S(2)}) async-start(bf16[32,8,960]{2,1,0:T(8,128)(2,1)} %bitcast.26), calls=%async_computation.1 | async-start | bytes 1048576 | tf_op jit(solution)/shard_map/all_to_all | solution.py:397
  35.5 0.3 collective-permute-start.10
  35.8 0.3 collective-permute-start.7
  36.3 0.3 collective-permute-start.9
  37.2 0.5 collective-permute-done.7.refs_5_
  37.7 0.9 %collective-permute-done.8.refs_6_ = bf16[80,2048]{1,0:T(8,128)(2,1)S(1)} collective-permute-done((bf16[80,2048]{1,0:T(8,128)(2,1)S(1)}, bf16[80,2048]{1,0:T(8,128)(2,1)S(1)}, u32[]{:S(2)}, u32[]{:S(2)}) %collective-permute-start.8) | collective-permute-done | bytes 327712 | tf_op jit(solution)/shard_map/ppermute | solution.py:288
  38.7 0.7 %collective-permute-done.6.other = bf16[256,640]{1,0:T(8,128)(2,1)} collective-permute-done((bf16[256,640]{1,0:T(8,128)(2,1)}, bf16[256,640]{1,0:T(8,128)(2,1)}, u32[]{:S(2)}, u32[]{:S(2)}) %collective-permute-start.6) | collective-permute-done | bytes 327712 | tf_op jit(solution)/shard_map/ppermute | solution.py:288
  39.4 0.9 %copy-done.1 = f32[256,128]{1,0:T(8,128)S(1)} copy-done((f32[256,128]{1,0:T(8,128)S(1)}, f32[256,128]{1,0:T(8,128)}, u32[]{:S(2)}) %copy-start.1) | copy-done | bytes 131096
  40.3 5.8 %merge.1 = bf16[256,2048]{1,0:T(8,128)(2,1)} custom-call(s32[2]{0:T(128)S(1)} %pad_add_fusion.2.bases, s32[4]{0:T(128)S(1)} %pad_add_fusion.3.offsets, bf16[256,640]{1,0:T(8,128)(2,1)S(1)} %get-tuple-element.39.pooled, bf16[256,640]{1,0:T(8,128)(2,1)} %collective-permute-done.6.other, f32[256,128]{1,0:T(8,128)S(1)} %copy-done.1, f32[1,2048]{1,0:T(1,128)S(1)} %bitcast.24, ...), custom_call_target="tpu_custom_call" | custom-call | flops 1000000000 | tf_op jit(solution)/shard_map/merge/pallas_call | solution.py:405
  46.1 5.3 %all-to-all-done.1.pieces = bf16[32,8,960]{2,1,0:T(8,128)(2,1)S(1)} async-done(((bf16[32,8,960]{2,1,0:T(8,128)(2,1)}), bf16[32,8,960]{2,1,0:T(8,128)(2,1)S(1)}, u32[]{:S(2)}, u32[]{:S(2)}) %all-to-all-start.1) | async-done | bytes 491552 | tf_op jit(solution)/shard_map/all_to_all | solution.py:397
  51.4 0.8 %sum_pieces.1 = f32[24,640]{1,0:T(8,128)} custom-call(bf16[32,8,960]{2,1,0:T(8,128)(2,1)S(1)} %all-to-all-done.1.pieces), custom_call_target="tpu_custom_call" | custom-call | flops 1000000000 | tf_op jit(solution)/shard_map/sum_pieces/pallas_call | solution.py:426
  (26 shorter events, 1.6 us)
Async XLA Ops:
  0.6 13.5 %copy-start.3 = (f32[1280]{0:T(1024)S(1)}, f32[1280]{0:T(1024)}, u32[]{:S(2)}) copy-start(f32[1280]{0:T(1024)} %param.10) | copy-start | bytes 15364
  2.7 20.2 %collective-permute-start.1 = (bf16[256,2048]{1,0:T(8,128)(2,1)}, bf16[256,2048]{1,0:T(8,128)(2,1)S(1)}, u32[]{:S(2)}, u32[]{:S(2)}) collective-permute-start(bf16[256,2048]{1,0:T(8,128)(2,1)} %bitcast.14.own_in), channel_id=1, source_target_pairs={{0,1},{1,0},{2,3},{3,2},{4,5},{5,4},{6,7},{7,6},{8,9},{9,8},{10,11... | collective-permute-start | bytes 3145736 | tf_op jit(solution)/shard_map/ppermute | solution.py:288
  3.3 10.9 %collective-permute-start = (bf16[80,2048]{1,0:T(8,128)(2,1)S(1)}, bf16[80,2048]{1,0:T(8,128)(2,1)S(1)}, u32[]{:S(2)}, u32[]{:S(2)}) collective-permute-start(bf16[80,2048]{1,0:T(8,128)(2,1)S(1)} %get-tuple-element.24), channel_id=1, source_target_pairs={{0,16},{16,0},{1,17},{17,1},{2,18},{18,2},{3,19},{19,3},{4,20},{20... | collective-permute-start | bytes 983048 | tf_op jit(solution)/shard_map/ppermute | solution.py:285
  5.8 17.0 %all-to-all-start = ((bf16[16,8,1152]{2,1,0:T(8,128)(2,1)}), bf16[16,8,1152]{2,1,0:T(8,128)(2,1)S(1)}, u32[]{:S(2)}, u32[]{:S(2)}) async-start(bf16[16,8,1152]{2,1,0:T(8,128)(2,1)} %bitcast.28), calls=%async_computation | async-start | bytes 589824 | tf_op jit(solution)/shard_map/all_to_all | solution.py:342
  13.5 12.7 %collective-permute-start.5 = (bf16[80,2048]{1,0:T(8,128)(2,1)}, bf16[80,2048]{1,0:T(8,128)(2,1)S(1)}, u32[]{:S(2)}, u32[]{:S(2)}) collective-permute-start(bf16[80,2048]{1,0:T(8,128)(2,1)} %constant_dynamic-slice_fusion), channel_id=1, source_target_pairs={{0,16},{16,0},{1,17},{17,1},{2,18},{18,2},{3,19},{19,3},{4,20},{20... | collective-permute-start | bytes 983048 | tf_op jit(solution)/shard_map/ppermute | solution.py:285
  14.2 12.4 %collective-permute-start.3 = (bf16[80,2048]{1,0:T(8,128)(2,1)S(1)}, bf16[80,2048]{1,0:T(8,128)(2,1)S(1)}, u32[]{:S(2)}, u32[]{:S(2)}) collective-permute-start(bf16[80,2048]{1,0:T(8,128)(2,1)S(1)} %collective-permute-done.refs_0_.refs_1_), channel_id=1, source_target_pairs={{0,4},{1,5},{2,6},{3,7},{4,0},{5,1},{6,2},{7,3},{8,12},{9,13},{10,... | collective-permute-start | bytes 983048 | tf_op jit(solution)/shard_map/ppermute | solution.py:288
  16.1 10.6 %collective-permute-start.4 = (bf16[80,2048]{1,0:T(8,128)(2,1)S(1)}, bf16[80,2048]{1,0:T(8,128)(2,1)S(1)}, u32[]{:S(2)}, u32[]{:S(2)}) collective-permute-start(bf16[80,2048]{1,0:T(8,128)(2,1)S(1)} %collective-permute-done.refs_0_.refs_1_), channel_id=1, source_target_pairs={{0,2},{1,3},{2,0},{3,1},{4,6},{5,7},{6,4},{7,5},{8,10},{9,11},{10,... | collective-permute-start | bytes 983048 | tf_op jit(solution)/shard_map/ppermute | solution.py:288
  22.8 3.8 %collective-permute-start.2 = (bf16[128,1152]{1,0:T(8,128)(2,1)S(1)}, bf16[128,1152]{1,0:T(8,128)(2,1)S(1)}, u32[]{:S(2)}, u32[]{:S(2)}) collective-permute-start(bf16[128,1152]{1,0:T(8,128)(2,1)S(1)} %bitcast.22), channel_id=1, source_target_pairs={{0,1},{1,0},{2,3},{3,2},{4,5},{5,4},{6,7},{7,6},{8,9},{9,8},{10,11... | collective-permute-start | bytes 884744 | tf_op jit(solution)/shard_map/ppermute | solution.py:288
  26.2 5.1 %copy-start = (f32[256,128]{1,0:T(8,128)}, f32[256,128]{1,0:T(8,128)S(1)}, u32[]{:S(2)}) copy-start(f32[256,128]{1,0:T(8,128)S(1)} %get-tuple-element.41.valid) | copy-start | bytes 393220
  26.7 12.8 %copy-start.2 = (f32[2048]{0:T(1024)S(1)}, f32[2048]{0:T(1024)}, u32[]{:S(2)}) copy-start(f32[2048]{0:T(1024)} %param.12) | copy-start | bytes 24580
  31.3 20.1 %all-to-all-start.1 = ((bf16[32,8,960]{2,1,0:T(8,128)(2,1)}), bf16[32,8,960]{2,1,0:T(8,128)(2,1)S(1)}, u32[]{:S(2)}, u32[]{:S(2)}) async-start(bf16[32,8,960]{2,1,0:T(8,128)(2,1)} %bitcast.26), calls=%async_computation.1 | async-start | bytes 1048576 | tf_op jit(solution)/shard_map/all_to_all | solution.py:397
  35.5 1.7 %collective-permute-start.10 = (bf16[80,2048]{1,0:T(8,128)(2,1)S(1)}, bf16[80,2048]{1,0:T(8,128)(2,1)S(1)}, u32[]{:S(2)}, u32[]{:S(2)}) collective-permute-start(bf16[80,2048]{1,0:T(8,128)(2,1)S(1)} %collective-permute-done.5.refs_4_), channel_id=1, source_target_pairs={{0,1},{1,0},{2,3},{3,2},{4,5},{5,4},{6,7},{7,6},{8,9},{9,8},{10,11... | collective-permute-start | bytes 983048 | tf_op jit(solution)/shard_map/ppermute | solution.py:288
  35.8 1.8 %collective-permute-start.7 = (bf16[80,2048]{1,0:T(8,128)(2,1)S(1)}, bf16[80,2048]{1,0:T(8,128)(2,1)S(1)}, u32[]{:S(2)}, u32[]{:S(2)}) collective-permute-start(bf16[80,2048]{1,0:T(8,128)(2,1)S(1)} %collective-permute-done.refs_0_.refs_1_), channel_id=1, source_target_pairs={{0,1},{1,0},{2,3},{3,2},{4,5},{5,4},{6,7},{7,6},{8,9},{9,8},{10,11... | collective-permute-start | bytes 983048 | tf_op jit(solution)/shard_map/ppermute | solution.py:288
  36.1 2.5 %collective-permute-start.8 = (bf16[80,2048]{1,0:T(8,128)(2,1)S(1)}, bf16[80,2048]{1,0:T(8,128)(2,1)S(1)}, u32[]{:S(2)}, u32[]{:S(2)}) collective-permute-start(bf16[80,2048]{1,0:T(8,128)(2,1)S(1)} %collective-permute-done.3.refs_2_), channel_id=1, source_target_pairs={{0,1},{1,0},{2,3},{3,2},{4,5},{5,4},{6,7},{7,6},{8,9},{9,8},{10,11... | collective-permute-start | bytes 983048 | tf_op jit(solution)/shard_map/ppermute | solution.py:288
  36.3 2.4 %collective-permute-start.9 = (bf16[80,2048]{1,0:T(8,128)(2,1)S(1)}, bf16[80,2048]{1,0:T(8,128)(2,1)}, u32[]{:S(2)}, u32[]{:S(2)}) collective-permute-start(bf16[80,2048]{1,0:T(8,128)(2,1)S(1)} %collective-permute-done.4.refs_3_), channel_id=1, source_target_pairs={{0,1},{1,0},{2,3},{3,2},{4,5},{5,4},{6,7},{7,6},{8,9},{9,8},{10,11... | collective-permute-start | bytes 983048 | tf_op jit(solution)/shard_map/ppermute | solution.py:288
  36.6 2.8 %collective-permute-start.6 = (bf16[256,640]{1,0:T(8,128)(2,1)}, bf16[256,640]{1,0:T(8,128)(2,1)}, u32[]{:S(2)}, u32[]{:S(2)}) collective-permute-start(bf16[256,640]{1,0:T(8,128)(2,1)} %get-tuple-element.40), channel_id=1, source_target_pairs={{0,1},{1,0},{2,3},{3,2},{4,5},{5,4},{6,7},{7,6},{8,9},{9,8},{10,11... | collective-permute-start | bytes 983048 | tf_op jit(solution)/shard_map/ppermute | solution.py:288
  39.4 0.9 %copy-start.1 = (f32[256,128]{1,0:T(8,128)S(1)}, f32[256,128]{1,0:T(8,128)}, u32[]{:S(2)}) copy-start(f32[256,128]{1,0:T(8,128)} %copy-done) | copy-start | bytes 393220
